TPU v7x, 512 devices: a whole 4x4x16 slice. The times are simulated.
512 devices in a mesh: dp: 64 (over x_hi, z, core), mp: 8 (over x_lo, y).
Axes of the slice: x: 4 (x_hi: 2, x_lo: 2; x = x_hi * 2 + x_lo), y: 4, z: 16, core: 2. Of those that a mesh axis runs over, the one named last changes fastest.
Arguments:
- picture_tower_outputs: bfloat16 [8192, 1408], P('dp', 'mp'), may hold values from -200 to 200
- caption_tower_outputs: bfloat16 [8192, 1408], P('dp', 'mp'), may hold values from -200 to 200
- picture_mapping_matrix: bfloat16 [1408, 1536], P('mp'), may hold values from -1 to 1
- caption_mapping_matrix: bfloat16 [1408, 1536], P('mp'), may hold values from -1 to 1
- sharpness_factor: float32 [1], replicated, may hold values from 15 to 25
- offset_vector: float32 [1], replicated, may hold values from -10 to -6
Outputs:
- loss: float32 [1], replicated
- image_grad: float32 [8192, 1536], P('dp', 'mp')
- text_grad: float32 [8192, 1536], P(('dp', 'mp'))
All inputs are finite; a program needn't handle non-finite values.
Results may differ from a plain program's by a relative error of at most 0.0084.
Values may be sent and summed in bfloat16 or wider, within the bound.
No kernel may reach another device: no remote copies, remote signals or barrier semaphores. Data moves between devices by JAX's collectives and lax.ppermute only.
A program may use at most 64 MiB of HBM per device.

v0:
```python
import jax
import jax.numpy as jnp
from jax import lax
from jax.sharding import PartitionSpec as P

EPSILON = 1e-06


def passed_along(value, axis, steps):
    count = lax.axis_size(axis)
    pairs = [(source, (source + steps) % count) for source in range(count)]
    return lax.ppermute(value, axis, pairs)


def normalize(embedded):
    inverse = lax.rsqrt(jnp.sum(embedded * embedded, axis=1, keepdims=True) + EPSILON)
    return (inverse, (embedded * inverse).astype(jnp.bfloat16))


def tangent_back(embedded, inverse, cotangent):
    row_dot = jnp.sum(embedded * cotangent, axis=1, keepdims=True)
    return inverse * cotangent - inverse * inverse * inverse * embedded * row_dot


def couple_patch(
    picture_unit_vectors,
    caption_tile,
    leading_index,
    caption_vectors,
    affinity_multiplier,
    affinity_offset,
):
    similarity_values = lax.dot_general(
        picture_unit_vectors,
        caption_tile,
        (((1,), (1,)), ((), ())),
        preferred_element_type=jnp.float32,
    )
    affinity_matrix = affinity_multiplier * similarity_values + affinity_offset
    image_ids = leading_index + jnp.arange(picture_unit_vectors.shape[0], dtype=jnp.int32)
    labels = jnp.where(image_ids[:, None] == caption_vectors[None, :], 1.0, -1.0).astype(
        jnp.float32
    )
    margin = labels * affinity_matrix
    loss_part = jnp.sum(jax.nn.softplus(-margin))
    coefficient = (-labels * jax.nn.sigmoid(-margin)).astype(jnp.bfloat16)
    caption_summand = affinity_multiplier * lax.dot_general(
        coefficient,
        picture_unit_vectors,
        (((0,), (0,)), ((), ())),
        preferred_element_type=jnp.float32,
    )
    return (loss_part, coefficient, caption_summand)


def on_device(
    picture_tower_outputs,
    caption_tower_outputs,
    picture_mapping_matrix,
    caption_mapping_matrix,
    sharpness_factor,
    offset_vector,
):
    affinity_multiplier = sharpness_factor[0]
    affinity_offset = offset_vector[0]
    members = lax.axis_size("mp")
    member_entry = lax.axis_index("mp")
    stations = lax.axis_size("dp")
    station = lax.axis_index("dp")
    block_rows = picture_tower_outputs.shape[0]
    shard_rows = block_rows // members
    part_img = jnp.dot(
        picture_tower_outputs, picture_mapping_matrix, preferred_element_type=jnp.float32
    )
    part_txt = jnp.dot(
        caption_tower_outputs, caption_mapping_matrix, preferred_element_type=jnp.float32
    )
    u_img, u_all = lax.psum((part_img, part_txt), "mp")
    u_txt = lax.dynamic_slice_in_dim(u_all, member_entry * shard_rows, shard_rows, 0)
    inv_img, picture_unit_vectors = normalize(u_img)
    inv_txt, caption_unit_vectors = normalize(u_txt)
    embedding_width = caption_unit_vectors.shape[1]
    leading_index = station * block_rows
    total_slots = stations * shard_rows

    def visit_tile(source, caption_tile, text_store, weights):
        caption_vectors = (
            source * block_rows
            + member_entry * shard_rows
            + jnp.arange(shard_rows, dtype=jnp.int32)
        )
        loss_part, coefficient, caption_summand = couple_patch(
            picture_unit_vectors,
            caption_tile,
            leading_index,
            caption_vectors,
            affinity_multiplier,
            affinity_offset,
        )
        text_store = lax.dynamic_update_slice_in_dim(
            text_store, caption_tile, source * shard_rows, 0
        )
        weights = lax.dynamic_update_slice_in_dim(weights, coefficient, source * shard_rows, 1)
        return (loss_part, caption_summand, text_store, weights)

    empty_grads = jnp.zeros((shard_rows, embedding_width), jnp.float32)
    empty_store = jnp.zeros((total_slots, embedding_width), jnp.bfloat16)
    empty_weights = jnp.zeros((block_rows, total_slots), jnp.bfloat16)
    zero_loss = jnp.zeros((), jnp.float32)

    def visit_one(turn_idx, state):
        caption_tile, carried, text_store, weights, loss_sum = state
        source = (station - turn_idx) % stations
        loss_part, caption_summand, text_store, weights = visit_tile(
            source, caption_tile, text_store, weights
        )
        carried = carried + caption_summand
        caption_tile = passed_along(caption_tile, "dp", 1)
        carried = passed_along(carried, "dp", 1)
        return (caption_tile, carried, text_store, weights, loss_sum + loss_part)

    start_state = (caption_unit_vectors, empty_grads, empty_store, empty_weights, zero_loss)
    final_state = lax.fori_loop(0, stations, visit_one, start_state)
    grads_home = final_state[1]
    text_store = final_state[2]
    weights = final_state[3]
    loss_sum = final_state[4]
    picture_derivative = affinity_multiplier * jnp.dot(
        weights, text_store, preferred_element_type=jnp.float32
    )
    image_term = tangent_back(u_img, inv_img, picture_derivative)
    image_grad = lax.psum_scatter(image_term, "mp", scatter_dimension=1, tiled=True)
    text_grad = tangent_back(u_txt, inv_txt, grads_home)
    loss_all = lax.psum(loss_sum, ("dp", "mp"))
    loss = (loss_all / (block_rows * stations)).reshape(1)
    return (loss, image_grad, text_grad)


def solution(mesh):
    return jax.shard_map(
        on_device,
        mesh=mesh,
        in_specs=(P("dp", "mp"), P("dp", "mp"), P("mp", None), P("mp", None), P(), P()),
        out_specs=(P(), P("dp", "mp"), P(("dp", "mp"), None)),
        check_vma=False,
    )
```

profile of v0, /device:TPU:1, one launch (start us, length us, event | category | flops | bytes accessed | tf_op | source)
XLA Modules:
  0.0 1126.0 jit_solution(16047429641612243134)
XLA Ops:
  13.2 95.5 %all-reduce.3.cloned.1.call-done = (f32[128,1536]{1,0:T(8,128)}, f32[128,1536]{1,0:T(8,128)}) async-done(((f32[128,1536]{1,0:T(8,128)}, f32[128,1536]{1,0:T(8,128)}), (f32[128,1536]{1,0:T(8,128)}, f32[128,1536]{1,0:T(8,128)})) %all-reduce.3.cloned.1.call-update) | async-done | bytes 1572880 | tf_op jit(solution)/shard_map/psum | solution.py:78
  115.1 889.8 %while.23 = (s32[]{:T(128)}, bf16[16,1536]{1,0:T(8,128)(2,1)S(1)}, f32[16,1536]{1,0:T(8,128)S(1)}, bf16[1024,1536]{1,0:T(8,128)(2,1)}, bf16[128,1024]{0,1:T(8,12...) while((s32[]{:T(128)}, bf16[16,1536]{1,0:T(8,128)(2,1)S(1)}, ...), condition=%wide.region_6.7_spmd, body=%wide.region_4.6_spmd.sunk | while | flops 12683428 | bytes 1849960 | solution.py:123
  115.1 8.4 collective-permute-start
  151.0 4.5 collective-permute-done.1
  164.9 4.5 collective-permute-done.1
  178.8 4.5 collective-permute-done.1
  192.8 4.5 collective-permute-done.1
  206.7 4.5 collective-permute-done.1
  220.6 4.5 collective-permute-done.1
  234.5 4.5 collective-permute-done.1
  248.5 4.5 collective-permute-done.1
  262.4 4.5 collective-permute-done.1
  276.3 4.5 collective-permute-done.1
  290.2 4.5 collective-permute-done.1
  304.2 4.5 collective-permute-done.1
  318.1 4.5 collective-permute-done.1
  332.0 4.5 collective-permute-done.1
  345.9 4.5 collective-permute-done.1
  359.9 4.5 collective-permute-done.1
  373.8 4.5 collective-permute-done.1
  387.7 4.5 collective-permute-done.1
  401.6 4.5 collective-permute-done.1
  415.6 4.5 collective-permute-done.1
  429.5 4.5 collective-permute-done.1
  443.4 4.5 collective-permute-done.1
  457.3 4.5 collective-permute-done.1
  471.3 4.5 collective-permute-done.1
  485.2 4.5 collective-permute-done.1
  499.1 4.5 collective-permute-done.1
  513.1 4.5 collective-permute-done.1
  527.0 4.5 collective-permute-done.1
  540.9 4.5 collective-permute-done.1
  554.8 4.5 collective-permute-done.1
  568.8 4.5 collective-permute-done.1
  582.7 4.5 collective-permute-done.1
  596.6 4.5 collective-permute-done.1
  610.5 4.5 collective-permute-done.1
  624.5 4.5 collective-permute-done.1
  638.4 4.5 collective-permute-done.1
  652.3 4.5 collective-permute-done.1
  666.2 4.5 collective-permute-done.1
  680.2 4.5 collective-permute-done.1
  694.1 4.5 collective-permute-done.1
  708.0 4.5 collective-permute-done.1
  721.9 4.5 collective-permute-done.1
  735.9 4.5 collective-permute-done.1
  749.8 4.5 collective-permute-done.1
  763.7 4.5 collective-permute-done.1
  777.6 4.5 collective-permute-done.1
  791.6 4.5 collective-permute-done.1
  805.5 4.5 collective-permute-done.1
  819.4 4.5 collective-permute-done.1
  833.3 4.5 collective-permute-done.1
  847.3 4.5 collective-permute-done.1
  861.2 4.5 collective-permute-done.1
  875.1 4.5 collective-permute-done.1
  889.0 4.5 collective-permute-done.1
  903.0 4.5 collective-permute-done.1
  916.9 4.5 collective-permute-done.1
  944.8 4.5 collective-permute-done.1
  958.7 4.5 collective-permute-done.1
  972.6 4.5 collective-permute-done.1
  986.5 4.5 collective-permute-done.1
  1008.9 105.9 %psum.23 = f32[]{:T(128)} all-reduce(f32[]{:T(128)} %get-tuple-element.295), channel_id=1, replica_groups=mesh['dp'=64,'mp'=8] {'dp','mp'}, use_global_device_ids=true, to_apply=%region_7.8 | all-reduce | flops 1 | bytes 8 | tf_op jit(solution)/shard_map/psum | solution.py:134
  (668 shorter events, 591.5 us)
Async XLA Ops:
  7.2 101.4 %all-reduce.3.cloned.1.call-start = ((), (), s32[]{:S(2)}) async-start(), calls=%async_computation.2 | async-start | bytes 3145728 | tf_op jit(solution)/shard_map/psum | solution.py:78
  12.5 1105.6 %reduce-scatter.4.cloned.1.call-start = ((), (), s32[]{:S(2)}) async-start(), calls=%async_computation.1 | async-start | bytes 884736
  115.1 14.6 %collective-permute-start = (bf16[16,1536]{1,0:T(8,128)(2,1)S(1)}, bf16[16,1536]{1,0:T(8,128)(2,1)S(1)}, u32[]{:S(2)}, u32[]{:S(2)}) collective-permute-start(bf16[16,1536]{1,0:T(8,128)(2,1)S(1)} %copy.24), channel_id=1, source_target_pairs={{0,8},{8,16},{16,24},{24,32},{32,40},{40,48},{48,56},{56,64},{64,7... | collective-permute-start | bytes 147464 | tf_op jit(solution)/shard_map/while/body/eval_jaxpr/ppermute | solution.py:12
  129.8 10.3 collective-permute-start
  159.8 9.6 collective-permute-start.1
  173.7 9.6 collective-permute-start.1
  187.7 9.6 collective-permute-start.1
  201.6 9.6 collective-permute-start.1
  215.5 9.6 collective-permute-start.1
  229.4 9.6 collective-permute-start.1
  243.4 9.6 collective-permute-start.1
  257.3 9.6 collective-permute-start.1
  271.2 9.6 collective-permute-start.1
  285.1 9.6 collective-permute-start.1
  299.1 9.6 collective-permute-start.1
  313.0 9.6 collective-permute-start.1
  326.9 9.6 collective-permute-start.1
  340.8 9.6 collective-permute-start.1
  354.8 9.6 collective-permute-start.1
  368.7 9.6 collective-permute-start.1
  382.6 9.6 collective-permute-start.1
  396.5 9.6 collective-permute-start.1
  410.5 9.6 collective-permute-start.1
  424.4 9.6 collective-permute-start.1
  438.3 9.6 collective-permute-start.1
  452.2 9.6 collective-permute-start.1
  466.2 9.6 collective-permute-start.1
  480.1 9.6 collective-permute-start.1
  494.0 9.6 collective-permute-start.1
  508.0 9.6 collective-permute-start.1
  521.9 9.6 collective-permute-start.1
  535.8 9.6 collective-permute-start.1
  549.7 9.6 collective-permute-start.1
  563.7 9.6 collective-permute-start.1
  577.6 9.6 collective-permute-start.1
  591.5 9.6 collective-permute-start.1
  605.4 9.6 collective-permute-start.1
  619.4 9.6 collective-permute-start.1
  633.3 9.6 collective-permute-start.1
  647.2 9.6 collective-permute-start.1
  661.1 9.6 collective-permute-start.1
  675.1 9.6 collective-permute-start.1
  689.0 9.6 collective-permute-start.1
  702.9 9.6 collective-permute-start.1
  716.8 9.6 collective-permute-start.1
  730.8 9.6 collective-permute-start.1
  744.7 9.6 collective-permute-start.1
  758.6 9.6 collective-permute-start.1
  772.5 9.6 collective-permute-start.1
  786.5 9.6 collective-permute-start.1
  800.4 9.6 collective-permute-start.1
  814.3 9.6 collective-permute-start.1
  828.2 9.6 collective-permute-start.1
  842.2 9.6 collective-permute-start.1
  856.1 9.6 collective-permute-start.1
  870.0 9.6 collective-permute-start.1
  883.9 9.6 collective-permute-start.1
  897.9 9.6 collective-permute-start.1
  911.8 9.6 collective-permute-start.1
  925.7 9.6 collective-permute-start.1
  939.7 9.6 collective-permute-start.1
  953.6 9.6 collective-permute-start.1
  967.5 9.6 collective-permute-start.1
  981.4 9.6 collective-permute-start.1
  (68 other events, 1505.1 us)
Sparse Core Ops, SparseCore 0:
  12.6 95.9 all-reduce.2
  1009.0 36.8 reduce-scatter.3
where the time goes:
time: 1130 us
  waiting for transfers between devices  457 us (40%)
  starting transfers between devices  255 us (23%)
  matrix products  160 us (14%)
  blocking collectives  106 us (9%)
  other arithmetic  47 us (4%)
  local copies, waits for them, and re-layouts  44.3 us (4%)
  loops' own time  41.1 us (4%)
  between operations  16.5 us (1%)
    ppermute x128, waiting for transfers between devices, passed_along(): return lax.ppermute(value, axis, pairs)  361 us
    ppermute x128, starting transfers between devices, passed_along(): return lax.ppermute(value, axis, pairs)  255 us
    psum x1, blocking collectives, on_device(): loss_all = lax.psum(loss_sum, ('dp', 'mp'))  106 us
    dot_general x64, matrix products, couple_patch(): lax.dot_general(picture_unit_vectors, caption_tile, (((1,), (1,)), ((), (...  97.4 us
    psum x1, waiting for transfers between devices, on_device(): u_img, u_all = lax.psum((part_img, part_txt), 'mp')  95.5 us
    dot_general x64, matrix products, couple_patch(): lax.dot_general(coefficient, picture_unit_vectors, (((0,), (0,)), ((), ()...  55.6 us
    another operation x1, loops' own time, on_device(): final_state = lax.fori_loop(0, stations, visit_one, start_state)  41.1 us
    dynamic_update_slice x64, local copies, waits for them, and re-layouts, visit_tile(): lax.dynamic_update_slice_in_dim(text_store, caption_tile, source * shard_...  39.9 us
  transfers between devices with their start and end apart: 130, of which 126 were waited for; matrix products, arithmetic and copies ran while one was open for 21% of the time, Pallas kernels for 0%

commit v1 on v0

v1 whole, which is shorter than its diff:
```python
import jax
import jax.numpy as jnp
from jax import lax
from jax.sharding import Mesh, PartitionSpec as P

EPSILON = 1e-06
BF = jnp.bfloat16
F32 = jnp.float32

PARTS = (2, 16, 2, 2, 4)
NAMES = ("xh", "z", "core", "xl", "y")
DP = ("xh", "z", "core")
MP = ("xl", "y")
XY = ("xh", "xl", "y")
N_MP = 8
N_XY = 16
N_Z = 16
PAIRS = 8192


def exchange(value, axes):
    return lax.all_to_all(value, axes, 0, 0, tiled=True)


def other_core(value):
    return lax.ppermute(value, "core", [(0, 1), (1, 0)])


def split_pair(value):
    high = lax.reduce_precision(value, 8, 7)
    return high.astype(BF), (value - high).astype(BF)


def couple(images, texts, scale, offset, same):
    similarity = lax.dot_general(
        images, texts, (((1,), (1,)), ((), ())), preferred_element_type=F32
    )
    labels = jnp.where(same, 1.0, -1.0).astype(F32)
    margin = labels * (scale * similarity + offset)
    loss = jnp.sum(jax.nn.softplus(-margin))
    weight = (-labels * jax.nn.sigmoid(-margin)).astype(BF)
    return loss, weight


def on_device(x_img, x_txt, w_img, w_txt, sharpness_factor, offset_vector):
    scale = sharpness_factor[0]
    offset = offset_vector[0]
    rows = x_img.shape[0]
    shard = rows // N_MP
    width = w_img.shape[1]
    columns = width // N_MP
    xh, z_at = lax.axis_index("xh"), lax.axis_index("z")
    at_xy = lax.axis_index(XY)

    part_img = jnp.dot(x_img, w_img, preferred_element_type=F32).astype(BF)
    part_txt = jnp.dot(x_txt, w_txt, preferred_element_type=F32).astype(BF)
    parts = jnp.concatenate(
        [part_img.reshape(N_MP, shard, width), part_txt.reshape(N_MP, shard, width)], axis=1
    )
    parts = exchange(parts, MP)
    u = jnp.sum(parts.astype(F32), axis=0)
    inverse = lax.rsqrt(jnp.sum(u * u, axis=1, keepdims=True) + EPSILON)
    unit = (u * inverse).astype(BF)
    u_txt, inv_txt = u[shard:], inverse[shard:]
    unit_txt = unit[shard:]
    high, low = split_pair(inverse[:shard])
    unit_img = jnp.concatenate(
        [unit[:shard], high, low, jnp.zeros((shard, 126), BF)], axis=1
    )

    texts = exchange(jnp.broadcast_to(unit_txt, (N_Z,) + unit_txt.shape), ("z",))
    texts = texts.reshape(N_Z * shard, width)
    mine = exchange(jnp.broadcast_to(unit_img, (N_XY,) + unit_img.shape), XY)
    mine = mine.reshape(N_XY * shard, width + 128)
    inv_mine = mine[:, width].astype(F32) + mine[:, width + 1].astype(F32)
    mine = mine[:, :width]
    theirs = other_core(mine)

    image_ids = jnp.arange(N_XY * shard, dtype=jnp.int32)
    text_ids = jnp.arange(N_Z * shard, dtype=jnp.int32)
    same = (
        (image_ids[:, None] // shard == at_xy)
        & (text_ids[None, :] // shard == z_at)
        & (image_ids[:, None] % shard == text_ids[None, :] % shard)
    )
    loss_a, weight_a = couple(mine, texts, scale, offset, same)
    loss_b, weight_b = couple(theirs, texts, scale, offset, jnp.zeros_like(same))
    loss = lax.psum((loss_a + loss_b).reshape(1, 1), "core")

    back = (((0,), (0,)), ((), ()))
    grad_txt = scale * (
        lax.dot_general(weight_a, mine, back, preferred_element_type=F32)
        + lax.dot_general(weight_b, theirs, back, preferred_element_type=F32)
    )
    grad_txt = grad_txt.astype(BF).reshape(N_Z, shard, width)
    high, low = split_pair(loss)
    tag = jnp.concatenate([high, low, jnp.zeros((1, 126), BF)], axis=1)
    tag = jnp.broadcast_to(tag[None], (N_Z, shard, 128))
    sums = exchange(jnp.concatenate([grad_txt, tag], axis=2), ("z",))
    sums = jnp.sum(sums.astype(F32), axis=0)
    loss = sums[0:1, width : width + 1] + sums[0:1, width + 1 : width + 2]
    grad_txt = sums[:, :width]
    row_dot = jnp.sum(u_txt * grad_txt, axis=1, keepdims=True)
    text_grad = inv_txt * grad_txt - inv_txt * inv_txt * inv_txt * u_txt * row_dot

    def tangent(images, weight):
        grad = jnp.dot(weight, texts, preferred_element_type=F32)
        images = images.astype(F32)
        return grad - images * jnp.sum(images * grad, axis=1, keepdims=True)

    from_other = other_core(tangent(theirs, weight_b).astype(BF))
    term = tangent(mine, weight_a) + from_other.astype(F32)
    term = (scale * inv_mine[:, None]) * term
    term = term.astype(BF).reshape(2, rows, N_MP, columns).transpose(0, 2, 1, 3)
    term = term.reshape(N_XY, rows, columns)
    high, low = split_pair(loss)
    tag = jnp.concatenate([high, low, jnp.zeros((1, 62), BF)], axis=1)
    tag = jnp.broadcast_to(tag[None], (N_XY, rows, 64))
    sums = exchange(jnp.concatenate([term, tag], axis=2), XY)
    sums = jnp.sum(sums.astype(F32), axis=0)
    image_grad = sums[:, :columns]
    loss = (sums[0, columns] + sums[0, columns + 1]) / PAIRS
    return loss.reshape(1), image_grad, text_grad


def solution(mesh):
    parts = Mesh(mesh.devices.reshape(PARTS), NAMES)
    return jax.shard_map(
        on_device,
        mesh=parts,
        in_specs=(P(DP, MP), P(DP, MP), P(MP, None), P(MP, None), P(), P()),
        out_specs=(P(), P(DP, MP), P(DP + MP, None)),
        check_vma=False,
    )
```

time: 1130 us -> 185 us (0.16)
  the two profiles are of different devices: /device:TPU:1 before, /device:TPU:160 now
where the time goes in v1:
time: 185 us; the launch traced here: 184 us
  waiting for transfers between devices  81.8 us (44%)
  blocking collectives  39.6 us (21%)
  starting transfers between devices  30.4 us (16%)
  between operations  12.2 us (7%)
  matrix products  9.49 us (5%)
  local copies, waits for them, and re-layouts  5.92 us (3%)
  other arithmetic  5.01 us (3%)
    all_to_all x3, waiting for transfers between devices, exchange(): return lax.all_to_all(value, axes, 0, 0, tiled=True)  80.3 us
    all_to_all x2, blocking collectives, exchange(): return lax.all_to_all(value, axes, 0, 0, tiled=True)  36 us
    all_to_all x3, starting transfers between devices, exchange(): return lax.all_to_all(value, axes, 0, 0, tiled=True)  26.5 us
    ppermute x2, starting transfers between devices, other_core(): return lax.ppermute(value, 'core', [(0, 1), (1, 0)])  3.96 us
  transfers between devices with their start and end apart: 5, of which 4 were waited for; matrix products, arithmetic and copies ran while one was open for 4% of the time, Pallas kernels for 0%

profile of v1, /device:TPU:160, one launch (start us, length us, event | category | flops | bytes accessed | tf_op | source)
XLA Modules:
  0.0 184.4 jit_solution(284164971855758912)
XLA Ops:
  0.6 0.0 copy-start
  0.6 1.0 copy-done
  1.7 1.1 convolution_convert_fusion.1
  2.8 1.4 convolution_convert_fusion
  4.1 0.1 pad_maximum_fusion.2
  4.2 18.1 %all_to_all.25 = bf16[8,32,1536]{2,1,0:T(8,128)(2,1)S(1)} all-to-all(bf16[8,32,1536]{2,1,0:T(8,128)(2,1)S(1)} %pad_maximum_fusion.2), channel_id=1, replica_groups=mesh['xh'=2,'z'=16,'core'=2,'xl'=2,'y'=4] {'xl','y'}, dimensions={0} | all-to-all | bytes 1572864 | tf_op jit(solution)/shard_map/all_to_all | solution.py:22
  22.3 0.1 convert_reduce_fusion.2
  22.4 0.1 multiply_reduce_fusion
  22.5 0.1 multiply_convert_fusion
  22.6 0.1 fusion.21
  22.7 0.1 copy.11
  22.8 0.1 copy.12
  22.9 0.1 concatenate.19
  23.0 0.1 broadcast_in_dim.52
  23.1 17.9 %all_to_all.26 = bf16[16,16,1664]{2,1,0:T(8,128)(2,1)S(1)} all-to-all(bf16[16,16,1664]{2,1,0:T(8,128)(2,1)S(1)} %broadcast_in_dim.52), channel_id=1, replica_groups=mesh['xh'=2,'z'=16,'core'=2,'xl'=2,'y'=4] {'xh','xl','y'}, dimensions={0} | all-to-all | bytes 1703936 | tf_op jit(solution)/shard_map/all_to_all | solution.py:22
  40.9 1.0 broadcast_in_dim.55
  41.9 13.4 %all-to-all-start.2 = ((bf16[16,16,1536]{2,1,0:T(8,128)(2,1)}), bf16[16,16,1536]{2,1,0:T(8,128)(2,1)S(1)}, u32[]{:S(2)}, u32[]{:S(2)}) async-start(bf16[16,16,1536]{2,1,0:T(8,128)(2,1)} %broadcast_in_dim.55), calls=%async_computation.2 | async-start | bytes 1572864 | tf_op jit(solution)/shard_map/all_to_all | solution.py:22
  55.3 0.9 slice.67
  56.2 1.9 %collective-permute-start = (bf16[256,1536]{1,0:T(8,128)(2,1)}, bf16[256,1536]{1,0:T(8,128)(2,1)S(1)}, u32[]{:S(2)}, u32[]{:S(2)}) collective-permute-start(bf16[256,1536]{1,0:T(8,128)(2,1)} %slice.67), channel_id=1, source_target_pairs={{0,8},{8,0},{1,9},{9,1},{2,10},{10,2},{3,11},{11,3},{4,12},{12,4},... | collective-permute-start | bytes 2359304 | tf_op jit(solution)/shard_map/ppermute | solution.py:26
  59.5 30.7 %all-to-all-done.2 = bf16[16,16,1536]{2,1,0:T(8,128)(2,1)S(1)} async-done(((bf16[16,16,1536]{2,1,0:T(8,128)(2,1)}), bf16[16,16,1536]{2,1,0:T(8,128)(2,1)S(1)}, u32[]{:S(2)}, u32[]{:S(2)}) %all-to-all-start.2) | async-done | bytes 786464 | tf_op jit(solution)/shard_map/all_to_all | solution.py:22
  90.2 0.0 copy-start.1
  90.2 1.9 %fusion.16 = (f32[]{:T(128)}, f32[256,256]{1,0:T(8,128)}) fusion(f32[]{:T(128)} %bitcast.46, bf16[256,1536]{1,0:T(8,128)(2,1)S(1)} %bitcast.56, bf16[256,1664]{1,0:T(8,128)(2,1)S(1)} %bitcast.49, f32[]{:T(128)} %bitcast.43, s32[256]{0:T(256)S(1)} %and_select_fusion, pred[256]{0:T(512)(128)(4,1)S(1)} %get-tuple-element.20, ...), kind=kOutput, calls=%fused_computation.34 | convolution fusion | flops 202309632 | bytes 1838092 | tf_op jit(solution)/shard_map/dot_general | solution.py:35
  92.0 0.0 collective-permute-done
  92.0 1.2 fusion.17
  94.5 3.6 %psum.7 = f32[1,1]{1,0:T(1,128)} all-reduce(f32[1,1]{1,0:T(1,128)} %bitcast.10), channel_id=1, replica_groups=mesh['xh'=2,'z'=16,'core'=2,'xl'=2,'y'=4] {'core'}, use_global_device_ids=true, to_apply=%region_6.7 | all-reduce | flops 1 | bytes 8 | tf_op jit(solution)/shard_map/psum | solution.py:88
  101.3 1.5 fusion.25
  102.7 0.1 fusion.23
  102.8 0.4 fusion.1
  103.2 0.0 copy-done.1
  103.3 1.0 pad_maximum_fusion.1
  104.3 8.9 %all-to-all-start.3 = ((bf16[16,16,1664]{2,1,0:T(8,128)(2,1)}), bf16[16,16,1664]{2,1,0:T(8,128)(2,1)S(1)}, u32[]{:S(2)}, u32[]{:S(2)}) async-start(bf16[16,16,1664]{2,1,0:T(8,128)(2,1)} %pad_maximum_fusion.1), calls=%async_computation.3 | async-start | bytes 1703936 | tf_op jit(solution)/shard_map/all_to_all | solution.py:22
  113.2 1.6 fusion.7
  114.8 0.0 copy-start.2
  114.8 0.0 copy-start.3
  114.9 0.3 fusion.9
  115.1 2.1 %collective-permute-start.1 = (bf16[256,1536]{1,0:T(8,128)(2,1)S(1)}, bf16[256,1536]{1,0:T(8,128)(2,1)S(1)}, u32[]{:S(2)}, u32[]{:S(2)}) collective-permute-start(bf16[256,1536]{1,0:T(8,128)(2,1)S(1)} %fusion.9), channel_id=1, source_target_pairs={{0,8},{8,0},{1,9},{9,1},{2,10},{10,2},{3,11},{11,3},{4,12},{12,4},... | collective-permute-start | bytes 2359304 | tf_op jit(solution)/shard_map/ppermute | solution.py:26
  117.2 0.2 multiply_reduce_fusion.1
  117.4 0.0 copy-done.2
  117.4 0.0 copy-done.3
  117.4 0.5 fusion.2
  117.9 1.5 collective-permute-done.1
  119.4 0.5 fusion.6
  119.9 0.3 copy.13
  120.2 0.2 reshape.173
  120.4 0.1 copy.14
  120.5 33.0 %all-to-all-done.3 = bf16[16,16,1664]{2,1,0:T(8,128)(2,1)S(1)} async-done(((bf16[16,16,1664]{2,1,0:T(8,128)(2,1)}), bf16[16,16,1664]{2,1,0:T(8,128)(2,1)S(1)}, u32[]{:S(2)}, u32[]{:S(2)}) %all-to-all-start.3) | async-done | bytes 852000 | tf_op jit(solution)/shard_map/all_to_all | solution.py:22
  153.5 0.1 convert_reduce_fusion.1
  153.7 0.6 fusion.32
  157.4 0.1 fusion.22
  157.5 0.1 pad.1.clone
  157.5 1.3 pad_maximum_fusion
  158.8 4.2 %all-to-all-start.4 = ((bf16[16,128,256]{1,2,0:T(8,128)(2,1)}), bf16[16,128,256]{1,2,0:T(8,128)(2,1)S(1)}, u32[]{:S(2)}, u32[]{:S(2)}) async-start(bf16[16,128,256]{1,2,0:T(8,128)(2,1)} %pad_maximum_fusion), calls=%async_computation.4 | async-start | bytes 2097152 | tf_op jit(solution)/shard_map/all_to_all | solution.py:22
  163.0 0.1 slice.60
  163.1 0.1 multiply_reduce_fusion.2
  163.2 0.7 multiply_subtract_fusion
  163.9 16.6 %all-to-all-done.4 = bf16[16,128,256]{1,2,0:T(8,128)(2,1)S(1)} async-done(((bf16[16,128,256]{1,2,0:T(8,128)(2,1)}), bf16[16,128,256]{1,2,0:T(8,128)(2,1)S(1)}, u32[]{:S(2)}, u32[]{:S(2)}) %all-to-all-start.4) | async-done | bytes 1048608 | tf_op jit(solution)/shard_map/all_to_all | solution.py:22
  180.6 0.1 convert_reduce_fusion
  180.7 0.6 slice.73
  181.4 0.6 fusion.31
  (8 shorter events, 0.0 us)
Async XLA Ops:
  0.6 1.1 copy-start
  41.9 48.2 %all-to-all-start.2 = ((bf16[16,16,1536]{2,1,0:T(8,128)(2,1)}), bf16[16,16,1536]{2,1,0:T(8,128)(2,1)S(1)}, u32[]{:S(2)}, u32[]{:S(2)}) async-start(bf16[16,16,1536]{2,1,0:T(8,128)(2,1)} %broadcast_in_dim.55), calls=%async_computation.2 | async-start | bytes 1572864 | tf_op jit(solution)/shard_map/all_to_all | solution.py:22
  56.2 35.8 %collective-permute-start = (bf16[256,1536]{1,0:T(8,128)(2,1)}, bf16[256,1536]{1,0:T(8,128)(2,1)S(1)}, u32[]{:S(2)}, u32[]{:S(2)}) collective-permute-start(bf16[256,1536]{1,0:T(8,128)(2,1)} %slice.67), channel_id=1, source_target_pairs={{0,8},{8,0},{1,9},{9,1},{2,10},{10,2},{3,11},{11,3},{4,12},{12,4},... | collective-permute-start | bytes 2359304 | tf_op jit(solution)/shard_map/ppermute | solution.py:26
  90.2 13.1 %copy-start.1 = (bf16[16,16,1536]{2,1,0:T(8,128)(2,1)}, bf16[16,16,1536]{2,1,0:T(8,128)(2,1)S(1)}, u32[]{:S(2)}) copy-start(bf16[16,16,1536]{2,1,0:T(8,128)(2,1)S(1)} %all-to-all-done.2) | copy-start | bytes 2359300
  104.3 49.2 %all-to-all-start.3 = ((bf16[16,16,1664]{2,1,0:T(8,128)(2,1)}), bf16[16,16,1664]{2,1,0:T(8,128)(2,1)S(1)}, u32[]{:S(2)}, u32[]{:S(2)}) async-start(bf16[16,16,1664]{2,1,0:T(8,128)(2,1)} %pad_maximum_fusion.1), calls=%async_computation.3 | async-start | bytes 1703936 | tf_op jit(solution)/shard_map/all_to_all | solution.py:22
  114.8 2.5 %copy-start.2 = (bf16[16,16,1536]{2,1,0:T(8,128)(2,1)S(1)}, bf16[16,16,1536]{2,1,0:T(8,128)(2,1)}, u32[]{:S(2)}) copy-start(bf16[16,16,1536]{2,1,0:T(8,128)(2,1)} %copy-done.1) | copy-start | bytes 2359300
  114.8 2.5 %copy-start.3 = (f32[256,256]{1,0:T(8,128)S(1)}, f32[256,256]{1,0:T(8,128)}, u32[]{:S(2)}) copy-start(f32[256,256]{1,0:T(8,128)} %get-tuple-element.17) | copy-start | bytes 786436
  115.1 4.3 %collective-permute-start.1 = (bf16[256,1536]{1,0:T(8,128)(2,1)S(1)}, bf16[256,1536]{1,0:T(8,128)(2,1)S(1)}, u32[]{:S(2)}, u32[]{:S(2)}) collective-permute-start(bf16[256,1536]{1,0:T(8,128)(2,1)S(1)} %fusion.9), channel_id=1, source_target_pairs={{0,8},{8,0},{1,9},{9,1},{2,10},{10,2},{3,11},{11,3},{4,12},{12,4},... | collective-permute-start | bytes 2359304 | tf_op jit(solution)/shard_map/ppermute | solution.py:26
  158.8 21.7 %all-to-all-start.4 = ((bf16[16,128,256]{1,2,0:T(8,128)(2,1)}), bf16[16,128,256]{1,2,0:T(8,128)(2,1)S(1)}, u32[]{:S(2)}, u32[]{:S(2)}) async-start(bf16[16,128,256]{1,2,0:T(8,128)(2,1)} %pad_maximum_fusion), calls=%async_computation.4 | async-start | bytes 2097152 | tf_op jit(solution)/shard_map/all_to_all | solution.py:22

commit v2 on v1

--- a/solution.py
+++ b/solution.py
@@ -7,14 +7,16 @@
 BF = jnp.bfloat16
 F32 = jnp.float32
 
-PARTS = (2, 16, 2, 2, 4)
-NAMES = ("xh", "z", "core", "xl", "y")
-DP = ("xh", "z", "core")
+PARTS = (2, 8, 2, 2, 2, 4)
+NAMES = ("xh", "zh", "zl", "core", "xl", "y")
+DP = ("xh", "zh", "zl", "core")
+Z = ("zh", "zl")
 MP = ("xl", "y")
 XY = ("xh", "xl", "y")
 N_MP = 8
 N_XY = 16
 N_Z = 16
+N_ZH = 8
 PAIRS = 8192
 
 
@@ -24,6 +26,10 @@
 
 def other_core(value):
     return lax.ppermute(value, "core", [(0, 1), (1, 0)])
+
+
+def along_z(value, step):
+    return lax.ppermute(value, Z, [(i, (i + step) % N_Z) for i in range(N_Z)])
 
 
 def split_pair(value):
@@ -49,7 +55,7 @@
     shard = rows // N_MP
     width = w_img.shape[1]
     columns = width // N_MP
-    xh, z_at = lax.axis_index("xh"), lax.axis_index("z")
+    zh = lax.axis_index("zh")
     at_xy = lax.axis_index(XY)
 
     part_img = jnp.dot(x_img, w_img, preferred_element_type=F32).astype(BF)
@@ -68,40 +74,37 @@
         [unit[:shard], high, low, jnp.zeros((shard, 126), BF)], axis=1
     )
 
-    texts = exchange(jnp.broadcast_to(unit_txt, (N_Z,) + unit_txt.shape), ("z",))
-    texts = texts.reshape(N_Z * shard, width)
-    mine = exchange(jnp.broadcast_to(unit_img, (N_XY,) + unit_img.shape), XY)
-    mine = mine.reshape(N_XY * shard, width + 128)
+    even = exchange(jnp.broadcast_to(unit_txt, (N_ZH,) + unit_txt.shape), ("zh",))
+    mine = lax.all_gather(unit_img, XY, axis=0, tiled=True)
+    even = even.reshape(N_ZH * shard, width)
+    half = N_ZH * shard // 2
+    odd = jnp.concatenate([along_z(even[:half], -1), along_z(even[half:], 1)], axis=0)
     inv_mine = mine[:, width].astype(F32) + mine[:, width + 1].astype(F32)
     mine = mine[:, :width]
     theirs = other_core(mine)
+    texts = jnp.concatenate([even, odd], axis=0)
 
     image_ids = jnp.arange(N_XY * shard, dtype=jnp.int32)
-    text_ids = jnp.arange(N_Z * shard, dtype=jnp.int32)
+    text_ids = jnp.arange(2 * N_ZH * shard, dtype=jnp.int32)
     same = (
         (image_ids[:, None] // shard == at_xy)
-        & (text_ids[None, :] // shard == z_at)
+        & (text_ids[None, :] // shard == zh)
         & (image_ids[:, None] % shard == text_ids[None, :] % shard)
     )
     loss_a, weight_a = couple(mine, texts, scale, offset, same)
     loss_b, weight_b = couple(theirs, texts, scale, offset, jnp.zeros_like(same))
-    loss = lax.psum((loss_a + loss_b).reshape(1, 1), "core")
+    loss = (loss_a + loss_b).reshape(1, 1)
+    loss = loss + other_core(loss)
+    loss = loss + lax.ppermute(loss, "zl", [(0, 1), (1, 0)])
 
     back = (((0,), (0,)), ((), ()))
     grad_txt = scale * (
         lax.dot_general(weight_a, mine, back, preferred_element_type=F32)
         + lax.dot_general(weight_b, theirs, back, preferred_element_type=F32)
     )
-    grad_txt = grad_txt.astype(BF).reshape(N_Z, shard, width)
-    high, low = split_pair(loss)
-    tag = jnp.concatenate([high, low, jnp.zeros((1, 126), BF)], axis=1)
-    tag = jnp.broadcast_to(tag[None], (N_Z, shard, 128))
-    sums = exchange(jnp.concatenate([grad_txt, tag], axis=2), ("z",))
-    sums = jnp.sum(sums.astype(F32), axis=0)
-    loss = sums[0:1, width : width + 1] + sums[0:1, width + 1 : width + 2]
-    grad_txt = sums[:, :width]
-    row_dot = jnp.sum(u_txt * grad_txt, axis=1, keepdims=True)
-    text_grad = inv_txt * grad_txt - inv_txt * inv_txt * inv_txt * u_txt * row_dot
+    grad_odd = grad_txt[2 * half :].astype(BF)
+    from_up = along_z(grad_odd[:half], -1)
+    from_down = along_z(grad_odd[half:], 1)
 
     def tangent(images, weight):
         grad = jnp.dot(weight, texts, preferred_element_type=F32)
@@ -119,7 +122,19 @@
     sums = exchange(jnp.concatenate([term, tag], axis=2), XY)
     sums = jnp.sum(sums.astype(F32), axis=0)
     image_grad = sums[:, :columns]
-    loss = (sums[0, columns] + sums[0, columns + 1]) / PAIRS
+    loss = (sums[0, columns] + sums[0, columns + 1]).reshape(1, 1)
+
+    added = jnp.concatenate([from_up, from_down], axis=0).astype(F32)
+    grad_txt = (grad_txt[: 2 * half] + added).astype(BF).reshape(N_ZH, shard, width)
+    high, low = split_pair(loss)
+    tag = jnp.concatenate([high, low, jnp.zeros((1, 126), BF)], axis=1)
+    tag = jnp.broadcast_to(tag[None], (N_ZH, shard, 128))
+    sums = exchange(jnp.concatenate([grad_txt, tag], axis=2), ("zh",))
+    sums = jnp.sum(sums.astype(F32), axis=0)
+    loss = (sums[0, width] + sums[0, width + 1]) / PAIRS
+    grad_txt = sums[:, :width]
+    row_dot = jnp.sum(u_txt * grad_txt, axis=1, keepdims=True)
+    text_grad = inv_txt * grad_txt - inv_txt * inv_txt * inv_txt * u_txt * row_dot
     return loss.reshape(1), image_grad, text_grad
 
 

time: 185 us -> 177 us (0.957)
  the two profiles are of different devices: /device:TPU:160 before, /device:TPU:8 now
where the time goes in v2:
time: 177 us; the launch traced here: 176 us
  starting transfers between devices  53.6 us (30%)
  waiting for transfers between devices  41.5 us (23%)
  blocking collectives  40.8 us (23%)
  between operations  12.1 us (7%)
  local copies, waits for them, and re-layouts  10.1 us (6%)
  other arithmetic  9.13 us (5%)
  matrix products  8.68 us (5%)
    all_to_all x3, starting transfers between devices, exchange(): return lax.all_to_all(value, axes, 0, 0, tiled=True)  30 us
    all_to_all x3, waiting for transfers between devices, exchange(): return lax.all_to_all(value, axes, 0, 0, tiled=True)  27.1 us
    all_gather x1, blocking collectives, on_device(): mine = lax.all_gather(unit_img, XY, axis=0, tiled=True)  24.1 us
    all_to_all x1, blocking collectives, exchange(): return lax.all_to_all(value, axes, 0, 0, tiled=True)  16.7 us
    ppermute x4, starting transfers between devices, along_z(): return lax.ppermute(value, Z, [(i, (i + step) % N_Z) for i in range(N_Z)])  13.1 us
    ppermute x4, waiting for transfers between devices, along_z(): return lax.ppermute(value, Z, [(i, (i + step) % N_Z) for i in range(N_Z)])  12.2 us
    ppermute x3, starting transfers between devices, other_core(): return lax.ppermute(value, 'core', [(0, 1), (1, 0)])  7.31 us
  transfers between devices with their start and end apart: 11, of which 7 were waited for; matrix products, arithmetic and copies ran while one was open for 6% of the time, Pallas kernels for 0%

profile of v2, /device:TPU:8, one launch (start us, length us, event | category | flops | bytes accessed | tf_op | source)
XLA Modules:
  0.0 176.0 jit_solution(4526679407940626885)
XLA Ops:
  0.6 0.0 copy-start
  0.6 1.0 copy-done
  1.7 1.1 convolution_convert_fusion.1
  2.8 1.4 convolution_convert_fusion
  4.1 0.1 pad_maximum_fusion.1
  4.2 16.7 %all_to_all.20 = bf16[8,32,1536]{2,1,0:T(8,128)(2,1)S(1)} all-to-all(bf16[8,32,1536]{2,1,0:T(8,128)(2,1)S(1)} %pad_maximum_fusion.1), channel_id=1, replica_groups=mesh['xh'=2,'zh'=8,'zl'=2,'core'=2,'xl'=2,'y'=4] {'xl','y'}, dimensions={0} | all-to-all | bytes 1572864 | tf_op jit(solution)/shard_map/all_to_all | solution.py:24
  20.9 0.1 convert_reduce_fusion.1
  21.0 0.1 multiply_reduce_fusion
  21.1 0.1 multiply_convert_fusion
  21.2 0.8 broadcast_in_dim.51
  22.0 15.2 %all-to-all-start.1 = ((bf16[8,16,1536]{2,1,0:T(8,128)(2,1)}), bf16[8,16,1536]{2,1,0:T(8,128)(2,1)S(1)}, u32[]{:S(2)}, u32[]{:S(2)}) async-start(bf16[8,16,1536]{2,1,0:T(8,128)(2,1)} %broadcast_in_dim.51), calls=%async_computation.1 | async-start | bytes 786432 | tf_op jit(solution)/shard_map/all_to_all | solution.py:24
  38.5 0.6 fusion.21
  39.1 0.1 copy.19
  39.2 0.1 copy.20
  39.3 0.1 concatenate.25
  39.4 24.1 %all_gather.3 = bf16[256,1664]{1,0:T(8,128)(2,1)S(1)} all-gather(bf16[16,1664]{1,0:T(8,128)(2,1)S(1)} %concatenate.25), channel_id=1, replica_groups=mesh['xh'=2,'zh'=8,'zl'=2,'core'=2,'xl'=2,'y'=4] {'xh','xl','y'}, dimensions={0}, use_global_device_ids=true | all-gather | bytes 905216 | tf_op jit(solution)/shard_map/all_gather | solution.py:78
  63.5 0.1 slice.97
  63.5 1.9 %collective-permute-start.2 = (bf16[256,1536]{1,0:T(8,128)(2,1)S(1)}, bf16[256,1536]{1,0:T(8,128)(2,1)S(1)}, u32[]{:S(2)}, u32[]{:S(2)}) collective-permute-start(bf16[256,1536]{1,0:T(8,128)(2,1)S(1)} %slice.97), channel_id=1, source_target_pairs={{0,8},{8,0},{1,9},{9,1},{2,10},{10,2},{3,11},{11,3},{4,12},{12,4},... | collective-permute-start | bytes 2359304 | tf_op jit(solution)/shard_map/ppermute | solution.py:28
  65.4 0.6 and_select_fusion
  66.0 5.3 %collective-permute-start = (bf16[64,1536]{1,0:T(8,128)(2,1)S(1)}, bf16[64,1536]{1,0:T(8,128)(2,1)S(1)}, u32[]{:S(2)}, u32[]{:S(2)}) collective-permute-start(bf16[64,1536]{1,0:T(8,128)(2,1)S(1)} %bitcast.57), channel_id=1, source_target_pairs={{0,240},{16,0},{32,16},{48,32},{64,48},{80,64},{96,80},{112,96},{1... | collective-permute-start | bytes 589832 | tf_op jit(solution)/shard_map/ppermute | solution.py:32
  71.3 1.9 %collective-permute-start.1 = (bf16[64,1536]{1,0:T(8,128)(2,1)S(1)}, bf16[64,1536]{1,0:T(8,128)(2,1)S(1)}, u32[]{:S(2)}, u32[]{:S(2)}) collective-permute-start(bf16[64,1536]{1,0:T(8,128)(2,1)S(1)} %bitcast.56), channel_id=1, source_target_pairs={{0,16},{16,32},{32,48},{48,64},{64,80},{80,96},{96,112},{112,128},... | collective-permute-start | bytes 589832 | tf_op jit(solution)/shard_map/ppermute | solution.py:32
  73.3 0.7 multiply_reduce_fusion.1
  74.1 2.1 %collective-permute-done = bf16[64,1536]{1,0:T(8,128)(2,1)S(1)} collective-permute-done((bf16[64,1536]{1,0:T(8,128)(2,1)S(1)}, bf16[64,1536]{1,0:T(8,128)(2,1)S(1)}, u32[]{:S(2)}, u32[]{:S(2)}) %collective-permute-start) | collective-permute-done | bytes 196640 | tf_op jit(solution)/shard_map/ppermute | solution.py:32
  76.2 5.3 %collective-permute-done.1 = bf16[64,1536]{1,0:T(8,128)(2,1)S(1)} collective-permute-done((bf16[64,1536]{1,0:T(8,128)(2,1)S(1)}, bf16[64,1536]{1,0:T(8,128)(2,1)S(1)}, u32[]{:S(2)}, u32[]{:S(2)}) %collective-permute-start.1) | collective-permute-done | bytes 196640 | tf_op jit(solution)/shard_map/ppermute | solution.py:32
  81.5 1.2 fusion.17
  82.7 1.2 fusion.16
  85.2 2.9 %collective-permute-start.6 = (f32[1,1]{1,0:T(1,128)}, f32[1,1]{1,0:T(1,128)}, u32[]{:S(2)}, u32[]{:S(2)}) collective-permute-start(f32[1,1]{1,0:T(1,128)} %bitcast.11), channel_id=1, source_target_pairs={{0,8},{8,0},{1,9},{9,1},{2,10},{10,2},{3,11},{11,3},{4,12},{12,4},... | collective-permute-start | bytes 20 | tf_op jit(solution)/shard_map/ppermute | solution.py:28
  88.1 1.5 fusion.6
  89.6 0.3 fusion.8
  89.9 2.5 %collective-permute-start.5 = (bf16[256,1536]{1,0:T(8,128)(2,1)S(1)}, bf16[256,1536]{1,0:T(8,128)(2,1)S(1)}, u32[]{:S(2)}, u32[]{:S(2)}) collective-permute-start(bf16[256,1536]{1,0:T(8,128)(2,1)S(1)} %fusion.8), channel_id=1, source_target_pairs={{0,8},{8,0},{1,9},{9,1},{2,10},{10,2},{3,11},{11,3},{4,12},{12,4},... | collective-permute-start | bytes 2359304 | tf_op jit(solution)/shard_map/ppermute | solution.py:28
  92.4 0.5 fusion.27
  93.0 0.5 fusion.1
  93.5 0.6 copy-done.2
  94.1 0.1 copy-done.4
  94.1 1.4 fusion.36
  96.1 3.2 %collective-permute-start.7 = (f32[1,1]{1,0:T(1,128)}, f32[1,1]{1,0:T(1,128)}, u32[]{:S(2)}, u32[]{:S(2)}) collective-permute-start(f32[1,1]{1,0:T(1,128)} %add.124), channel_id=1, source_target_pairs={{0,16},{16,0},{1,17},{17,1},{2,18},{18,2},{3,19},{19,3},{4,20},{20... | collective-permute-start | bytes 20 | tf_op jit(solution)/shard_map/ppermute | solution.py:98
  99.3 2.2 %collective-permute-done.7 = f32[1,1]{1,0:T(1,128)} collective-permute-done((f32[1,1]{1,0:T(1,128)}, f32[1,1]{1,0:T(1,128)}, u32[]{:S(2)}, u32[]{:S(2)}) %collective-permute-start.7) | collective-permute-done | bytes 36 | tf_op jit(solution)/shard_map/ppermute | solution.py:98
  103.9 0.1 fusion.23
  104.0 0.6 pad.6.clone
  104.6 1.4 fusion.5
  106.0 1.4 copy.21
  107.4 1.1 reshape.175
  108.5 1.3 copy.22
  109.8 1.3 pad_maximum_fusion
  111.1 6.2 %all-to-all-start.2 = ((bf16[16,128,256]{1,2,0:T(8,128)(2,1)}), bf16[16,128,256]{1,2,0:T(8,128)(2,1)S(1)}, u32[]{:S(2)}, u32[]{:S(2)}) async-start(bf16[16,128,256]{1,2,0:T(8,128)(2,1)} %pad_maximum_fusion), calls=%async_computation.2 | async-start | bytes 2097152 | tf_op jit(solution)/shard_map/all_to_all | solution.py:24
  117.3 1.0 fusion.31
  118.4 1.9 %collective-permute-start.3 = (bf16[64,1536]{1,0:T(8,128)(2,1)S(1)}, bf16[64,1536]{1,0:T(8,128)(2,1)S(1)}, u32[]{:S(2)}, u32[]{:S(2)}) collective-permute-start(bf16[64,1536]{1,0:T(8,128)(2,1)S(1)} %get-tuple-element.3), channel_id=1, source_target_pairs={{0,240},{16,0},{32,16},{48,32},{64,48},{80,64},{96,80},{112,96},{1... | collective-permute-start | bytes 589832 | tf_op jit(solution)/shard_map/ppermute | solution.py:32
  120.3 3.9 %collective-permute-start.4 = (bf16[64,1536]{1,0:T(8,128)(2,1)S(1)}, bf16[64,1536]{1,0:T(8,128)(2,1)S(1)}, u32[]{:S(2)}, u32[]{:S(2)}) collective-permute-start(bf16[64,1536]{1,0:T(8,128)(2,1)S(1)} %get-tuple-element.4), channel_id=1, source_target_pairs={{0,16},{16,32},{32,48},{48,64},{64,80},{80,96},{96,112},{112,128},... | collective-permute-start | bytes 589832 | tf_op jit(solution)/shard_map/ppermute | solution.py:32
  124.2 1.7 collective-permute-done.3
  125.9 3.1 %collective-permute-done.4 = bf16[64,1536]{1,0:T(8,128)(2,1)S(1)} collective-permute-done((bf16[64,1536]{1,0:T(8,128)(2,1)S(1)}, bf16[64,1536]{1,0:T(8,128)(2,1)S(1)}, u32[]{:S(2)}, u32[]{:S(2)}) %collective-permute-start.4) | collective-permute-done | bytes 196640 | tf_op jit(solution)/shard_map/ppermute | solution.py:32
  129.1 0.8 fusion.13
  129.9 2.4 %all-to-all-done.2 = bf16[16,128,256]{1,2,0:T(8,128)(2,1)S(1)} async-done(((bf16[16,128,256]{1,2,0:T(8,128)(2,1)}), bf16[16,128,256]{1,2,0:T(8,128)(2,1)S(1)}, u32[]{:S(2)}, u32[]{:S(2)}) %all-to-all-start.2) | async-done | bytes 1048608 | tf_op jit(solution)/shard_map/all_to_all | solution.py:24
  132.3 0.1 convert_reduce_fusion
  132.5 0.5 fusion.33
  136.1 0.1 fusion.22
  136.2 1.8 %pad_maximum_fusion.3 = bf16[8,16,1664]{2,1,0:T(8,128)(2,1)} fusion(bf16[8,16,1536]{2,1,0:T(8,128)(2,1)} %bitcast.53, bf16[1664]{0:T(1024)(128)(2,1)S(1)} %pad.1.clone), kind=kLoop, calls=%fused_computation.32 | loop fusion | flops 851968 | bytes 822528 | tf_op jit(solution)/shard_map/concatenate | solution.py:132
  138.0 8.6 %all-to-all-start.3 = ((bf16[8,16,1664]{2,1,0:T(8,128)(2,1)}), bf16[8,16,1664]{2,1,0:T(8,128)(2,1)S(1)}, u32[]{:S(2)}, u32[]{:S(2)}) async-start(bf16[8,16,1664]{2,1,0:T(8,128)(2,1)} %pad_maximum_fusion.3), calls=%async_computation.3 | async-start | bytes 851968 | tf_op jit(solution)/shard_map/all_to_all | solution.py:24
  146.6 0.1 slice.92
  146.7 0.6 slice.110
  147.4 24.7 %all-to-all-done.3 = bf16[8,16,1664]{2,1,0:T(8,128)(2,1)S(1)} async-done(((bf16[8,16,1664]{2,1,0:T(8,128)(2,1)}), bf16[8,16,1664]{2,1,0:T(8,128)(2,1)S(1)}, u32[]{:S(2)}, u32[]{:S(2)}) %all-to-all-start.3) | async-done | bytes 426016 | tf_op jit(solution)/shard_map/all_to_all | solution.py:24
  172.0 0.1 convert_reduce_fusion.2
  172.1 0.1 multiply_reduce_fusion.2
  172.2 0.6 fusion.34
  174.1 0.7 multiply_subtract_fusion
  (46 shorter events, 0.2 us)
Async XLA Ops:
  0.6 1.1 copy-start
  21.1 18.0 %copy-start.5 = (f32[32]{0:T(128)}, f32[32]{0:T(128)S(1)}, u32[]{:S(2)}) copy-start(f32[32]{0:T(128)S(1)} %add_rsqrt_fusion) | copy-start | bytes 388
  22.0 44.0 %all-to-all-start.1 = ((bf16[8,16,1536]{2,1,0:T(8,128)(2,1)}), bf16[8,16,1536]{2,1,0:T(8,128)(2,1)S(1)}, u32[]{:S(2)}, u32[]{:S(2)}) async-start(bf16[8,16,1536]{2,1,0:T(8,128)(2,1)} %broadcast_in_dim.51), calls=%async_computation.1 | async-start | bytes 786432 | tf_op jit(solution)/shard_map/all_to_all | solution.py:24
  63.5 10.5 %collective-permute-start.2 = (bf16[256,1536]{1,0:T(8,128)(2,1)S(1)}, bf16[256,1536]{1,0:T(8,128)(2,1)S(1)}, u32[]{:S(2)}, u32[]{:S(2)}) collective-permute-start(bf16[256,1536]{1,0:T(8,128)(2,1)S(1)} %slice.97), channel_id=1, source_target_pairs={{0,8},{8,0},{1,9},{9,1},{2,10},{10,2},{3,11},{11,3},{4,12},{12,4},... | collective-permute-start | bytes 2359304 | tf_op jit(solution)/shard_map/ppermute | solution.py:28
  66.0 10.1 %collective-permute-start = (bf16[64,1536]{1,0:T(8,128)(2,1)S(1)}, bf16[64,1536]{1,0:T(8,128)(2,1)S(1)}, u32[]{:S(2)}, u32[]{:S(2)}) collective-permute-start(bf16[64,1536]{1,0:T(8,128)(2,1)S(1)} %bitcast.57), channel_id=1, source_target_pairs={{0,240},{16,0},{32,16},{48,32},{64,48},{80,64},{96,80},{112,96},{1... | collective-permute-start | bytes 589832 | tf_op jit(solution)/shard_map/ppermute | solution.py:32
  71.3 10.1 %collective-permute-start.1 = (bf16[64,1536]{1,0:T(8,128)(2,1)S(1)}, bf16[64,1536]{1,0:T(8,128)(2,1)S(1)}, u32[]{:S(2)}, u32[]{:S(2)}) collective-permute-start(bf16[64,1536]{1,0:T(8,128)(2,1)S(1)} %bitcast.56), channel_id=1, source_target_pairs={{0,16},{16,32},{32,48},{48,64},{64,80},{80,96},{96,112},{112,128},... | collective-permute-start | bytes 589832 | tf_op jit(solution)/shard_map/ppermute | solution.py:32
  73.3 9.4 %copy-start.9 = (pred[256]{0:T(512)(128)(4,1)}, pred[256]{0:T(512)(128)(4,1)S(1)}, u32[]{:S(2)}) copy-start(pred[256]{0:T(512)(128)(4,1)S(1)} %get-tuple-element.26) | copy-start | bytes 772
  73.3 9.4 %copy-start.11 = (pred[256]{0:T(512)(128)(4,1)}, pred[256]{0:T(512)(128)(4,1)S(1)}, u32[]{:S(2)}) copy-start(pred[256]{0:T(512)(128)(4,1)S(1)} %get-tuple-element.27) | copy-start | bytes 772
  74.1 15.5 %copy-start.1 = (bf16[256,1536]{1,0:T(8,128)(2,1)}, bf16[256,1536]{1,0:T(8,128)(2,1)S(1)}, u32[]{:S(2)}) copy-start(bf16[256,1536]{1,0:T(8,128)(2,1)S(1)} %collective-permute-done.2) | copy-start | bytes 2359300
  76.2 6.5 %copy-start.14 = (bf16[64,1536]{1,0:T(8,128)(2,1)}, bf16[64,1536]{1,0:T(8,128)(2,1)S(1)}, u32[]{:S(2)}) copy-start(bf16[64,1536]{1,0:T(8,128)(2,1)S(1)} %collective-permute-done) | copy-start | bytes 589828
  81.5 1.2 copy-start.16
  81.5 1.2 copy-start.18
  82.7 5.4 %copy-start.3 = (f32[256,256]{1,0:T(8,128)}, f32[256,256]{1,0:T(8,128)S(1)}, u32[]{:S(2)}) copy-start(f32[256,256]{1,0:T(8,128)S(1)} %get-tuple-element.25) | copy-start | bytes 786436
  85.2 10.3 %collective-permute-start.6 = (f32[1,1]{1,0:T(1,128)}, f32[1,1]{1,0:T(1,128)}, u32[]{:S(2)}, u32[]{:S(2)}) collective-permute-start(f32[1,1]{1,0:T(1,128)} %bitcast.11), channel_id=1, source_target_pairs={{0,8},{8,0},{1,9},{9,1},{2,10},{10,2},{3,11},{11,3},{4,12},{12,4},... | collective-permute-start | bytes 20 | tf_op jit(solution)/shard_map/ppermute | solution.py:28
  89.5 2.8 %copy-start.10 = (pred[256]{0:T(512)(128)(4,1)S(1)}, pred[256]{0:T(512)(128)(4,1)}, u32[]{:S(2)}) copy-start(pred[256]{0:T(512)(128)(4,1)} %copy-done.9) | copy-start | bytes 772
  89.6 2.8 %copy-start.12 = (pred[256]{0:T(512)(128)(4,1)S(1)}, pred[256]{0:T(512)(128)(4,1)}, u32[]{:S(2)}) copy-start(pred[256]{0:T(512)(128)(4,1)} %copy-done.11) | copy-start | bytes 772
  89.8 3.1 %copy-start.15 = (bf16[64,1536]{1,0:T(8,128)(2,1)S(1)}, bf16[64,1536]{1,0:T(8,128)(2,1)}, u32[]{:S(2)}) copy-start(bf16[64,1536]{1,0:T(8,128)(2,1)} %copy-done.14) | copy-start | bytes 589828
  89.8 3.1 %copy-start.17 = (bf16[64,1536]{1,0:T(8,128)(2,1)S(1)}, bf16[64,1536]{1,0:T(8,128)(2,1)}, u32[]{:S(2)}) copy-start(bf16[64,1536]{1,0:T(8,128)(2,1)} %copy-done.16) | copy-start | bytes 589828
  89.9 14.7 %collective-permute-start.5 = (bf16[256,1536]{1,0:T(8,128)(2,1)S(1)}, bf16[256,1536]{1,0:T(8,128)(2,1)S(1)}, u32[]{:S(2)}, u32[]{:S(2)}) collective-permute-start(bf16[256,1536]{1,0:T(8,128)(2,1)S(1)} %fusion.8), channel_id=1, source_target_pairs={{0,8},{8,0},{1,9},{9,1},{2,10},{10,2},{3,11},{11,3},{4,12},{12,4},... | collective-permute-start | bytes 2359304 | tf_op jit(solution)/shard_map/ppermute | solution.py:28
  93.0 1.1 copy-start.2
  93.0 1.2 copy-start.4
  94.1 10.4 %copy-start.7 = (f32[256]{0:T(256)S(1)}, f32[256]{0:T(256)}, u32[]{:S(2)}) copy-start(f32[256]{0:T(256)} %multiply_reduce_fusion.1) | copy-start | bytes 3076
  96.1 5.4 %collective-permute-start.7 = (f32[1,1]{1,0:T(1,128)}, f32[1,1]{1,0:T(1,128)}, u32[]{:S(2)}, u32[]{:S(2)}) collective-permute-start(f32[1,1]{1,0:T(1,128)} %add.124), channel_id=1, source_target_pairs={{0,16},{16,0},{1,17},{17,1},{2,18},{18,2},{3,19},{19,3},{4,20},{20... | collective-permute-start | bytes 20 | tf_op jit(solution)/shard_map/ppermute | solution.py:98
  107.4 2.4 %copy-start.13 = (bf16[256]{0:T(256)(128)(2,1)S(1)}, bf16[256]{0:T(256)(128)(2,1)}, u32[]{:S(2)}) copy-start(bf16[256]{0:T(256)(128)(2,1)} %pad.6.clone) | copy-start | bytes 1540
  111.1 21.3 %all-to-all-start.2 = ((bf16[16,128,256]{1,2,0:T(8,128)(2,1)}), bf16[16,128,256]{1,2,0:T(8,128)(2,1)S(1)}, u32[]{:S(2)}, u32[]{:S(2)}) async-start(bf16[16,128,256]{1,2,0:T(8,128)(2,1)} %pad_maximum_fusion), calls=%async_computation.2 | async-start | bytes 2097152 | tf_op jit(solution)/shard_map/all_to_all | solution.py:24
  118.4 7.6 %collective-permute-start.3 = (bf16[64,1536]{1,0:T(8,128)(2,1)S(1)}, bf16[64,1536]{1,0:T(8,128)(2,1)S(1)}, u32[]{:S(2)}, u32[]{:S(2)}) collective-permute-start(bf16[64,1536]{1,0:T(8,128)(2,1)S(1)} %get-tuple-element.3), channel_id=1, source_target_pairs={{0,240},{16,0},{32,16},{48,32},{64,48},{80,64},{96,80},{112,96},{1... | collective-permute-start | bytes 589832 | tf_op jit(solution)/shard_map/ppermute | solution.py:32
  120.3 8.8 %collective-permute-start.4 = (bf16[64,1536]{1,0:T(8,128)(2,1)S(1)}, bf16[64,1536]{1,0:T(8,128)(2,1)S(1)}, u32[]{:S(2)}, u32[]{:S(2)}) collective-permute-start(bf16[64,1536]{1,0:T(8,128)(2,1)S(1)} %get-tuple-element.4), channel_id=1, source_target_pairs={{0,16},{16,32},{32,48},{48,64},{64,80},{80,96},{96,112},{112,128},... | collective-permute-start | bytes 589832 | tf_op jit(solution)/shard_map/ppermute | solution.py:32
  129.9 16.8 %copy-start.6 = (f32[32]{0:T(128)S(1)}, f32[32]{0:T(128)}, u32[]{:S(2)}) copy-start(f32[32]{0:T(128)} %copy-done.5) | copy-start | bytes 388
  132.5 41.6 %copy-start.8 = (f32[16]{0:T(128)S(1)}, f32[16]{0:T(128)}, u32[]{:S(2)}) copy-start(f32[16]{0:T(128)} %get-tuple-element.13) | copy-start | bytes 196
  138.0 34.0 %all-to-all-start.3 = ((bf16[8,16,1664]{2,1,0:T(8,128)(2,1)}), bf16[8,16,1664]{2,1,0:T(8,128)(2,1)S(1)}, u32[]{:S(2)}, u32[]{:S(2)}) async-start(bf16[8,16,1664]{2,1,0:T(8,128)(2,1)} %pad_maximum_fusion.3), calls=%async_computation.3 | async-start | bytes 851968 | tf_op jit(solution)/shard_map/all_to_all | solution.py:24

commit v3 on v2

v3 whole, which is shorter than its diff:
```python
import jax
import jax.numpy as jnp
from jax import lax
from jax.experimental import pallas as pl
from jax.experimental.pallas import tpu as pltpu
from jax.sharding import Mesh, PartitionSpec as P

EPSILON = 1e-06
BF = jnp.bfloat16
F32 = jnp.float32

PARTS = (2, 8, 2, 2, 2, 4)
NAMES = ("xh", "zh", "zl", "core", "xl", "y")
DP = ("xh", "zh", "zl", "core")
MP = ("xl", "y")
Z = ("zh", "zl")
XY = ("xh", "xl", "y")
N_MP = 8
N_XY = 16
N_Z = 16
N_ZH = 8
PAIRS = 8192
SHARD = 16
WIDTH = 1536
COLUMNS = WIDTH // N_MP
HALF = N_ZH * SHARD
IMAGES = N_XY * SHARD
LANES = 128
WIDE = WIDTH + LANES

VMEM = pl.BlockSpec(memory_space=pltpu.VMEM)
SMEM = pl.BlockSpec(memory_space=pltpu.SMEM)


def exchange(value, axes):
    return lax.all_to_all(value, axes, 0, 0, tiled=True)


def other_core(value):
    return lax.ppermute(value, "core", [(0, 1), (1, 0)])


def along_z(value, step):
    return lax.ppermute(value, Z, [(i, (i + step) % N_Z) for i in range(N_Z)])


def split_pair(value):
    high = lax.reduce_precision(value, 8, 7)
    return high.astype(BF), (value - high).astype(BF)


def call(body, outs, operands, specs, name, flops=0, moved=0, scratch=()):
    return pl.pallas_call(
        body,
        out_shape=[jax.ShapeDtypeStruct(shape, dtype) for shape, dtype in outs],
        in_specs=specs,
        out_specs=[VMEM] * len(outs),
        scratch_shapes=list(scratch),
        compiler_params=pltpu.CompilerParams(vmem_limit_bytes=24 * 1024 * 1024),
        cost_estimate=pl.CostEstimate(flops=flops, bytes_accessed=moved, transcendentals=0),
        name=name,
    )(*operands)


def dot(a, b, contract):
    return lax.dot_general(a, b, (contract, ((), ())), preferred_element_type=F32)


def terms(similarity, scale, offset, labels):
    value = -labels * (scale * similarity + offset)
    small = jnp.exp(-jnp.abs(value))
    loss = jnp.maximum(value, 0.0) + jnp.log1p(small)
    share = 1.0 / (1.0 + small)
    sigmoid = jnp.where(value >= 0.0, share, small * share)
    return loss, (-labels * sigmoid).astype(BF)


def tangent(images_ref, weight, texts, scale, row):
    rows = pl.ds(row, 128)
    grad = dot(weight, texts, ((1,), (0,)))
    images = images_ref[rows, :WIDTH].astype(F32)
    radial = jnp.sum(images * grad, axis=1, keepdims=True)
    tags = images_ref[rows, WIDTH:].astype(F32)
    inverse = tags[:, 0:1] + tags[:, 1:2]
    return (grad - images * radial) * (scale * inverse)


def pair_body(
    factors, place, mine_ref, theirs_ref, texts_ref,
    sent_ref, odd_ref, loss_ref, weight_ref,
):
    scale, offset = factors[0], factors[1]
    at_xy, at_z, parity = place[0], place[1], place[2]
    own = texts_ref[parity]
    other = texts_ref[1 - parity]
    texts = jnp.concatenate([own, other], axis=0)
    total = jnp.zeros((1, 2 * HALF), F32)
    for block in range(IMAGES // 128):
        rows = pl.ds(block * 128, 128)
        similarity = dot(theirs_ref[rows, :WIDTH], texts, ((1,), (1,)))
        loss, weight = terms(similarity, scale, offset, -1.0)
        total = total + jnp.sum(loss, axis=0, keepdims=True)
        weight_ref[pl.ds(IMAGES + block * 128, 128), :] = weight
        term = tangent(theirs_ref, weight, texts, scale, block * 128)
        sent_ref[rows, :] = term.astype(BF)
    for block in range(IMAGES // 128):
        rows = pl.ds(block * 128, 128)
        similarity = dot(mine_ref[rows, :WIDTH], texts, ((1,), (1,)))
        image = lax.broadcasted_iota(jnp.int32, similarity.shape, 0) + block * 128
        text = lax.broadcasted_iota(jnp.int32, similarity.shape, 1)
        same = (image // SHARD == at_xy) & (image - SHARD * at_xy == text - SHARD * at_z)
        labels = jnp.where(same, 1.0, -1.0)
        loss, weight = terms(similarity, scale, offset, labels)
        total = total + jnp.sum(loss, axis=0, keepdims=True)
        weight_ref[rows, :] = weight
    loss_ref[...] = jnp.broadcast_to(jnp.sum(total, axis=1, keepdims=True), loss_ref.shape)
    for start in range(0, WIDTH, 512):
        cols = pl.ds(start, 512)
        odd = dot(weight_ref[:IMAGES, HALF:], mine_ref[:, cols], ((0,), (0,)))
        odd += dot(weight_ref[IMAGES:, HALF:], theirs_ref[:, cols], ((0,), (0,)))
        odd_ref[:, cols] = (scale * odd).astype(BF)


def own_body(factors, place, mine_ref, theirs_ref, texts_ref, weight_ref, mine_term_ref, even_ref):
    scale = factors[0]
    parity = place[2]
    own = texts_ref[parity]
    other = texts_ref[1 - parity]
    texts = jnp.concatenate([own, other], axis=0)
    for block in range(IMAGES // 128):
        rows = pl.ds(block * 128, 128)
        mine_term_ref[rows, :] = tangent(
            mine_ref, weight_ref[rows, :], texts, scale, block * 128
        )
    for start in range(0, WIDTH, 512):
        cols = pl.ds(start, 512)
        even = dot(weight_ref[:IMAGES, :HALF], mine_ref[:, cols], ((0,), (0,)))
        even += dot(weight_ref[IMAGES:, :HALF], theirs_ref[:, cols], ((0,), (0,)))
        even_ref[:, cols] = scale * even


def lay_out_body(loss_ref, mine_term_ref, other_ref, out_ref):
    loss = jnp.broadcast_to(loss_ref[0:1, 0:1], (128, 64))
    high = loss.astype(BF)
    low = (loss - high.astype(F32)).astype(BF)
    lane = lax.broadcasted_iota(jnp.int32, (128, 64), 1)
    tag = jnp.where(lane == 0, high.astype(F32), jnp.where(lane == 1, low.astype(F32), 0.0))
    for block in range(IMAGES // 128):
        rows = pl.ds(block * 128, 128)
        for part in range(N_MP):
            cols = slice(part * COLUMNS, (part + 1) * COLUMNS)
            term = mine_term_ref[rows, cols] + other_ref[rows, cols].astype(F32)
            out_ref[block * N_MP + part] = jnp.concatenate([term, tag], axis=1).astype(BF)


def add_odd_body(loss_ref, even_ref, up_ref, down_ref, out_ref):
    loss = jnp.broadcast_to(loss_ref[0:1, 0:1], (SHARD, LANES))
    high = loss.astype(BF)
    low = (loss - high.astype(F32)).astype(BF)
    lane = lax.broadcasted_iota(jnp.int32, (SHARD, LANES), 1)
    tag = jnp.where(lane == 0, high.astype(F32), jnp.where(lane == 1, low.astype(F32), 0.0))
    for block in range(N_ZH):
        rows = pl.ds(block * SHARD, SHARD)
        side = up_ref if block < N_ZH // 2 else down_ref
        from_rows = pl.ds((block % (N_ZH // 2)) * SHARD, SHARD)
        total = even_ref[rows, :] + side[from_rows, :].astype(F32)
        out_ref[block, :, :WIDTH] = total.astype(BF)
        out_ref[block, :, WIDTH:] = tag.astype(BF)


def text_body(sums_ref, u_ref, inverse_ref, grad_ref, loss_ref):
    total = sums_ref[0].astype(F32)
    for block in range(1, N_ZH):
        total = total + sums_ref[block].astype(F32)
    tags = total[0:1, WIDTH:]
    loss_ref[...] = jnp.broadcast_to((tags[:, 0:1] + tags[:, 1:2]) * (1.0 / PAIRS), loss_ref.shape)
    grad = total[:, :WIDTH]
    u = u_ref[...]
    inverse = inverse_ref[...]
    row_dot = jnp.sum(u * grad, axis=1, keepdims=True)
    grad_ref[...] = inverse * grad - inverse * inverse * inverse * u * row_dot


def on_device(x_img, x_txt, w_img, w_txt, sharpness_factor, offset_vector):
    rows = x_img.shape[0]
    zh, zl = lax.axis_index("zh"), lax.axis_index("zl")
    factors = jnp.concatenate([sharpness_factor, offset_vector])
    place = jnp.stack([lax.axis_index(XY), zh, zl]).astype(jnp.int32)

    part_img = jnp.dot(x_img, w_img, preferred_element_type=F32).astype(BF)
    part_txt = jnp.dot(x_txt, w_txt, preferred_element_type=F32).astype(BF)
    parts = jnp.concatenate(
        [part_img.reshape(N_MP, SHARD, WIDTH), part_txt.reshape(N_MP, SHARD, WIDTH)], axis=1
    )
    parts = exchange(parts, MP)
    u = jnp.sum(parts.astype(F32), axis=0)
    inverse = lax.rsqrt(jnp.sum(u * u, axis=1, keepdims=True) + EPSILON)
    unit = (u * inverse).astype(BF)
    u_txt, inv_txt = u[SHARD:], inverse[SHARD:]
    unit_txt = unit[SHARD:]
    high, low = split_pair(inverse[:SHARD])
    unit_img = jnp.concatenate(
        [unit[:SHARD], high, low, jnp.zeros((SHARD, LANES - 2), BF)], axis=1
    )

    texts = exchange(jnp.broadcast_to(unit_txt, (N_Z, SHARD, WIDTH)), ("zl", "zh"))
    texts = texts.reshape(2, HALF, WIDTH)
    mine = lax.all_gather(unit_img, XY, axis=0, tiled=True)
    theirs = other_core(mine)

    sent, odd, loss, weight = call(
        pair_body,
        [((IMAGES, WIDTH), BF), ((HALF, WIDTH), BF), ((8, LANES), F32),
         ((2 * IMAGES, 2 * HALF), BF)],
        (factors, place, mine, theirs, texts), [SMEM, SMEM, VMEM, VMEM, VMEM], "pairs",
        flops=900_000_000, moved=4_000_000,
    )
    from_other = other_core(sent)
    swap = [(0, 1), (1, 0)]
    cross = [(0, 3), (1, 2), (2, 1), (3, 0)]
    loss = (
        loss
        + other_core(loss)
        + (lax.ppermute(loss, "zl", swap) + lax.ppermute(loss, ("zl", "core"), cross))
    )
    from_up = along_z(odd[: HALF // 2], -1)
    from_down = along_z(odd[HALF // 2 :], 1)
    mine_term, even = call(
        own_body,
        [((IMAGES, WIDTH), F32), ((HALF, WIDTH), F32)],
        (factors, place, mine, theirs, texts, weight),
        [SMEM, SMEM, VMEM, VMEM, VMEM, VMEM], "own",
        flops=400_000_000, moved=4_000_000,
    )

    (term,) = call(
        lay_out_body, [((N_XY, rows, 256), BF)], (loss, mine_term, from_other),
        [VMEM] * 3, "lay_out", moved=3_000_000,
    )
    sums = exchange(term, XY)
    sums = jnp.sum(sums.astype(F32), axis=0)
    image_grad = sums[:, :COLUMNS]
    loss = jnp.broadcast_to(sums[0:1, COLUMNS : COLUMNS + 1] + sums[0:1, COLUMNS + 1 : COLUMNS + 2], (8, LANES))

    (term,) = call(
        add_odd_body, [((N_ZH, SHARD, WIDE), BF)], (loss, even, from_up, from_down),
        [VMEM] * 4, "add_odd", moved=2_000_000,
    )
    sums = exchange(term, ("zh",))
    text_grad, loss = call(
        text_body, [((SHARD, WIDTH), F32), ((1, LANES), F32)], (sums, u_txt, inv_txt),
        [VMEM] * 3, "text", moved=1_000_000,
    )
    return loss[0, 0:1], image_grad, text_grad


def solution(mesh):
    parts = Mesh(mesh.devices.reshape(PARTS), NAMES)
    return jax.shard_map(
        on_device,
        mesh=parts,
        in_specs=(P(DP, MP), P(DP, MP), P(MP, None), P(MP, None), P(), P()),
        out_specs=(P(), P(DP, MP), P(DP + MP, None)),
        check_vma=False,
    )
```

time: 177 us -> 154 us (0.87)
  the two profiles are of different devices: /device:TPU:8 before, /device:TPU:64 now
where the time goes in v3:
time: 154 us; the launch traced here: 153 us
  waiting for transfers between devices  49.1 us (32%)
  starting transfers between devices  42.4 us (28%)
  blocking collectives  41.9 us (27%)
  Pallas kernels  7.58 us (5%)
  local copies, waits for them, and re-layouts  6.05 us (4%)
  between operations  3.46 us (2%)
  matrix products  2.42 us (2%)
    all_to_all x3, waiting for transfers between devices, exchange(): return lax.all_to_all(value, axes, 0, 0, tiled=True)  48.2 us
    all_to_all x3, starting transfers between devices, exchange(): return lax.all_to_all(value, axes, 0, 0, tiled=True)  24.7 us
    all_gather x1, blocking collectives, on_device(): mine = lax.all_gather(unit_img, XY, axis=0, tiled=True)  23.7 us
    all_to_all x1, blocking collectives, exchange(): return lax.all_to_all(value, axes, 0, 0, tiled=True)  18.1 us
    pallas_call x5, Pallas kernels, call(): pl.pallas_call(body, out_shape=[jax.ShapeDtypeStruct(shape, dtype) for sh...  7.58 us
    ppermute x2, starting transfers between devices, along_z(): return lax.ppermute(value, Z, [(i, (i + step) % N_Z) for i in range(N_Z)])  5.96 us
    ppermute x3, starting transfers between devices, other_core(): return lax.ppermute(value, 'core', [(0, 1), (1, 0)])  5.75 us
    ppermute x1, starting transfers between devices, on_device(): lax.ppermute(loss, 'zl', swap) + lax.ppermute(loss, ('zl', 'core'), cross)  4.02 us
  transfers between devices with their start and end apart: 10, of which 4 were waited for; matrix products, arithmetic and copies ran while one was open for 2% of the time, Pallas kernels for 1%

profile of v3, /device:TPU:64, one launch (start us, length us, event | category | flops | bytes accessed | tf_op | source)
XLA Modules:
  0.0 153.5 jit_solution(6541153044484942307)
XLA Ops:
  0.6 0.0 copy-start
  0.6 1.0 copy-done
  1.7 1.1 convolution_convert_fusion.1
  2.8 1.4 convolution_convert_fusion
  4.1 0.1 pad_maximum_fusion
  4.2 18.1 %all_to_all.20 = bf16[8,32,1536]{2,1,0:T(8,128)(2,1)S(1)} all-to-all(bf16[8,32,1536]{2,1,0:T(8,128)(2,1)S(1)} %pad_maximum_fusion), channel_id=1, replica_groups=mesh['xh'=2,'zh'=8,'zl'=2,'core'=2,'xl'=2,'y'=4] {'xl','y'}, dimensions={0} | all-to-all | bytes 1572864 | tf_op jit(solution)/shard_map/all_to_all | solution.py:36
  22.3 0.1 convert_reduce_fusion.1
  22.4 0.0 copy-start.3
  22.4 0.1 multiply_reduce_fusion
  22.6 0.6 copy-done.3
  23.1 0.1 multiply_convert_fusion
  23.2 1.0 broadcast_in_dim.15
  24.2 14.8 %all-to-all-start.1 = ((bf16[16,16,1536]{2,1,0:T(8,128)(2,1)}), bf16[16,16,1536]{2,1,0:T(8,128)(2,1)S(1)}, u32[]{:S(2)}, u32[]{:S(2)}) async-start(bf16[16,16,1536]{2,1,0:T(8,128)(2,1)} %broadcast_in_dim.15), calls=%async_computation.1 | async-start | bytes 1572864 | tf_op jit(solution)/shard_map/all_to_all | solution.py:36
  39.0 0.1 copy.16
  39.0 0.1 slice_bitcast_fusion
  39.1 0.1 copy.17
  39.2 0.1 concatenate.11
  39.3 23.7 %all_gather.3.mine_ref = bf16[256,1664]{1,0:T(8,128)(2,1)S(1)} all-gather(bf16[16,1664]{1,0:T(8,128)(2,1)S(1)} %concatenate.11), channel_id=1, replica_groups=mesh['xh'=2,'zh'=8,'zl'=2,'core'=2,'xl'=2,'y'=4] {'xh','xl','y'}, dimensions={0}, use_global_device_ids=true | all-gather | bytes 905216 | tf_op jit(solution)/shard_map/all_gather | solution.py:208
  63.0 1.9 %collective-permute-start = (bf16[256,1664]{1,0:T(8,128)(2,1)S(1)}, bf16[256,1664]{1,0:T(8,128)(2,1)S(1)}, u32[]{:S(2)}, u32[]{:S(2)}) collective-permute-start(bf16[256,1664]{1,0:T(8,128)(2,1)S(1)} %all_gather.3.mine_ref), channel_id=1, source_target_pairs={{0,8},{8,0},{1,9},{9,1},{2,10},{10,2},{3,11},{11,3},{4,12},{12,4},... | collective-permute-start | bytes 2555912 | tf_op jit(solution)/shard_map/ppermute | solution.py:40
  66.3 0.1 pad_maximum_fusion.1.factors
  66.3 0.1 pad_add_fusion.place
  66.4 0.9 collective-permute-done.theirs_ref
  67.3 11.7 %all-to-all-done.1 = bf16[16,16,1536]{2,1,0:T(8,128)(2,1)S(1)} async-done(((bf16[16,16,1536]{2,1,0:T(8,128)(2,1)}), bf16[16,16,1536]{2,1,0:T(8,128)(2,1)S(1)}, u32[]{:S(2)}, u32[]{:S(2)}) %all-to-all-start.1) | async-done | bytes 786464 | tf_op jit(solution)/shard_map/all_to_all | solution.py:36
  79.0 3.4 %pairs.1 = (bf16[256,1536]{1,0:T(8,128)(2,1)S(1)}, bf16[128,1536]{1,0:T(8,128)(2,1)S(1)}, f32[8,128]{1,0:T(8,128)S(1)}, bf16[512,256]{1,0:T(8,128)(2,1)S(1)}) custom-call(f32[2]{0:T(128)S(1)} %pad_maximum_fusion.1.factors, s32[3]{0:T(128)S(1)} %pad_add_fusion.place, bf16[256,1664]{1,0:T(8,128)(2,1)S(1)} %all_gather.3.mine_ref, ...), custom_call_target="tpu_custom_call" | custom-call | flops 900000000 | bytes 4000000 | tf_op jit(solution)/shard_map/pairs/pallas_call | solution.py:53
  82.5 1.9 %collective-permute-start.4 = (bf16[256,1536]{1,0:T(8,128)(2,1)S(1)}, bf16[256,1536]{1,0:T(8,128)(2,1)S(1)}, u32[]{:S(2)}, u32[]{:S(2)}) collective-permute-start(bf16[256,1536]{1,0:T(8,128)(2,1)S(1)} %get-tuple-element.14), channel_id=1, source_target_pairs={{0,8},{8,0},{1,9},{9,1},{2,10},{10,2},{3,11},{11,3},{4,12},{12,4},... | collective-permute-start | bytes 2359304 | tf_op jit(solution)/shard_map/ppermute | solution.py:40
  84.4 1.9 %collective-permute-start.3 = (f32[8,128]{1,0:T(8,128)S(1)}, f32[8,128]{1,0:T(8,128)S(1)}, u32[]{:S(2)}, u32[]{:S(2)}) collective-permute-start(f32[8,128]{1,0:T(8,128)S(1)} %get-tuple-element.11), channel_id=1, source_target_pairs={{0,24},{8,16},{16,8},{24,0},{1,25},{9,17},{17,9},{25,1},{2,26},{10... | collective-permute-start | bytes 12296 | tf_op jit(solution)/shard_map/ppermute | solution.py:224
  86.3 4.0 %collective-permute-start.2 = (f32[8,128]{1,0:T(8,128)S(1)}, f32[8,128]{1,0:T(8,128)S(1)}, u32[]{:S(2)}, u32[]{:S(2)}) collective-permute-start(f32[8,128]{1,0:T(8,128)S(1)} %get-tuple-element.11), channel_id=1, source_target_pairs={{0,16},{16,0},{1,17},{17,1},{2,18},{18,2},{3,19},{19,3},{4,20},{20... | collective-permute-start | bytes 12296 | tf_op jit(solution)/shard_map/ppermute | solution.py:224
  90.3 1.9 %collective-permute-start.1 = (f32[8,128]{1,0:T(8,128)S(1)}, f32[8,128]{1,0:T(8,128)S(1)}, u32[]{:S(2)}, u32[]{:S(2)}) collective-permute-start(f32[8,128]{1,0:T(8,128)S(1)} %get-tuple-element.11), channel_id=1, source_target_pairs={{0,8},{8,0},{1,9},{9,1},{2,10},{10,2},{3,11},{11,3},{4,12},{12,4},... | collective-permute-start | bytes 12296 | tf_op jit(solution)/shard_map/ppermute | solution.py:40
  92.3 1.2 own.1
  93.5 0.0 copy-start.1
  93.5 0.9 copy-done.1
  94.5 0.0 collective-permute-done.3
  94.5 0.0 collective-permute-done.2
  94.5 0.0 collective-permute-done.1
  94.5 0.0 collective-permute-done.4.other_ref
  94.5 1.3 lay_out.1
  95.8 0.0 copy-start.2
  95.8 5.1 %all-to-all-start.2 = ((bf16[16,128,256]{2,1,0:T(8,128)(2,1)}), bf16[16,128,256]{2,1,0:T(8,128)(2,1)S(1)}, u32[]{:S(2)}, u32[]{:S(2)}) async-start(bf16[16,128,256]{2,1,0:T(8,128)(2,1)} %lay_out.1), calls=%async_computation.2 | async-start | bytes 2097152 | tf_op jit(solution)/shard_map/all_to_all | solution.py:36
  100.9 0.8 fusion.1
  101.7 2.0 %collective-permute-start.6 = (bf16[64,1536]{1,0:T(8,128)(2,1)}, bf16[64,1536]{1,0:T(8,128)(2,1)S(1)}, u32[]{:S(2)}, u32[]{:S(2)}) collective-permute-start(bf16[64,1536]{1,0:T(8,128)(2,1)} %get-tuple-element.25), channel_id=1, source_target_pairs={{0,16},{16,32},{32,48},{48,64},{64,80},{80,96},{96,112},{112,128},... | collective-permute-start | bytes 589832 | tf_op jit(solution)/shard_map/ppermute | solution.py:44
  103.8 0.0 copy-start.4
  103.8 3.9 %collective-permute-start.5 = (bf16[64,1536]{1,0:T(8,128)(2,1)}, bf16[64,1536]{1,0:T(8,128)(2,1)S(1)}, u32[]{:S(2)}, u32[]{:S(2)}) collective-permute-start(bf16[64,1536]{1,0:T(8,128)(2,1)} %get-tuple-element.26), channel_id=1, source_target_pairs={{0,240},{16,0},{32,16},{48,32},{64,48},{80,64},{96,80},{112,96},{1... | collective-permute-start | bytes 589832 | tf_op jit(solution)/shard_map/ppermute | solution.py:44
  107.7 11.7 %all-to-all-done.2 = bf16[16,128,256]{2,1,0:T(8,128)(2,1)S(1)} async-done(((bf16[16,128,256]{2,1,0:T(8,128)(2,1)}), bf16[16,128,256]{2,1,0:T(8,128)(2,1)S(1)}, u32[]{:S(2)}, u32[]{:S(2)}) %all-to-all-start.2) | async-done | bytes 1048608 | tf_op jit(solution)/shard_map/all_to_all | solution.py:36
  119.4 0.1 convert_reduce_fusion
  119.5 0.6 fusion.2
  121.4 0.0 collective-permute-done.6.down_ref
  121.4 0.0 collective-permute-done.5.up_ref
  121.5 0.0 copy-done.2
  121.5 0.8 add_odd.1
  122.3 4.8 %all-to-all-start.3 = ((bf16[8,16,1664]{2,1,0:T(8,128)(2,1)}), bf16[8,16,1664]{2,1,0:T(8,128)(2,1)S(1)}, u32[]{:S(2)}, u32[]{:S(2)}) async-start(bf16[8,16,1664]{2,1,0:T(8,128)(2,1)} %add_odd.1), calls=%async_computation.3 | async-start | bytes 851968 | tf_op jit(solution)/shard_map/all_to_all | solution.py:36
  127.1 0.0 copy-done.4
  127.2 0.1 copy.19.inverse_ref
  127.2 0.7 copy.20
  128.0 24.7 %all-to-all-done.3.sums_ref = bf16[8,16,1664]{2,1,0:T(8,128)(2,1)S(1)} async-done(((bf16[8,16,1664]{2,1,0:T(8,128)(2,1)}), bf16[8,16,1664]{2,1,0:T(8,128)(2,1)S(1)}, u32[]{:S(2)}, u32[]{:S(2)}) %all-to-all-start.3) | async-done | bytes 426016 | tf_op jit(solution)/shard_map/all_to_all | solution.py:36
  152.7 0.8 text.1
  (8 shorter events, 0.0 us)
Async XLA Ops:
  0.6 1.1 copy-start
  22.4 0.7 copy-start.3
  24.2 54.8 %all-to-all-start.1 = ((bf16[16,16,1536]{2,1,0:T(8,128)(2,1)}), bf16[16,16,1536]{2,1,0:T(8,128)(2,1)S(1)}, u32[]{:S(2)}, u32[]{:S(2)}) async-start(bf16[16,16,1536]{2,1,0:T(8,128)(2,1)} %broadcast_in_dim.15), calls=%async_computation.1 | async-start | bytes 1572864 | tf_op jit(solution)/shard_map/all_to_all | solution.py:36
  63.0 4.3 %collective-permute-start = (bf16[256,1664]{1,0:T(8,128)(2,1)S(1)}, bf16[256,1664]{1,0:T(8,128)(2,1)S(1)}, u32[]{:S(2)}, u32[]{:S(2)}) collective-permute-start(bf16[256,1664]{1,0:T(8,128)(2,1)S(1)} %all_gather.3.mine_ref), channel_id=1, source_target_pairs={{0,8},{8,0},{1,9},{9,1},{2,10},{10,2},{3,11},{11,3},{4,12},{12,4},... | collective-permute-start | bytes 2555912 | tf_op jit(solution)/shard_map/ppermute | solution.py:40
  82.5 12.0 %collective-permute-start.4 = (bf16[256,1536]{1,0:T(8,128)(2,1)S(1)}, bf16[256,1536]{1,0:T(8,128)(2,1)S(1)}, u32[]{:S(2)}, u32[]{:S(2)}) collective-permute-start(bf16[256,1536]{1,0:T(8,128)(2,1)S(1)} %get-tuple-element.14), channel_id=1, source_target_pairs={{0,8},{8,0},{1,9},{9,1},{2,10},{10,2},{3,11},{11,3},{4,12},{12,4},... | collective-permute-start | bytes 2359304 | tf_op jit(solution)/shard_map/ppermute | solution.py:40
  84.4 10.1 %collective-permute-start.3 = (f32[8,128]{1,0:T(8,128)S(1)}, f32[8,128]{1,0:T(8,128)S(1)}, u32[]{:S(2)}, u32[]{:S(2)}) collective-permute-start(f32[8,128]{1,0:T(8,128)S(1)} %get-tuple-element.11), channel_id=1, source_target_pairs={{0,24},{8,16},{16,8},{24,0},{1,25},{9,17},{17,9},{25,1},{2,26},{10... | collective-permute-start | bytes 12296 | tf_op jit(solution)/shard_map/ppermute | solution.py:224
  86.3 8.2 %collective-permute-start.2 = (f32[8,128]{1,0:T(8,128)S(1)}, f32[8,128]{1,0:T(8,128)S(1)}, u32[]{:S(2)}, u32[]{:S(2)}) collective-permute-start(f32[8,128]{1,0:T(8,128)S(1)} %get-tuple-element.11), channel_id=1, source_target_pairs={{0,16},{16,0},{1,17},{17,1},{2,18},{18,2},{3,19},{19,3},{4,20},{20... | collective-permute-start | bytes 12296 | tf_op jit(solution)/shard_map/ppermute | solution.py:224
  90.3 4.1 %collective-permute-start.1 = (f32[8,128]{1,0:T(8,128)S(1)}, f32[8,128]{1,0:T(8,128)S(1)}, u32[]{:S(2)}, u32[]{:S(2)}) collective-permute-start(f32[8,128]{1,0:T(8,128)S(1)} %get-tuple-element.11), channel_id=1, source_target_pairs={{0,8},{8,0},{1,9},{9,1},{2,10},{10,2},{3,11},{11,3},{4,12},{12,4},... | collective-permute-start | bytes 12296 | tf_op jit(solution)/shard_map/ppermute | solution.py:40
  93.5 0.9 copy-start.1
  95.8 25.7 %copy-start.2 = (f32[128,1536]{1,0:T(8,128)S(1)}, f32[128,1536]{1,0:T(8,128)}, u32[]{:S(2)}) copy-start(f32[128,1536]{1,0:T(8,128)} %copy-done.1) | copy-start | bytes 2359300
  95.8 23.6 %all-to-all-start.2 = ((bf16[16,128,256]{2,1,0:T(8,128)(2,1)}), bf16[16,128,256]{2,1,0:T(8,128)(2,1)S(1)}, u32[]{:S(2)}, u32[]{:S(2)}) async-start(bf16[16,128,256]{2,1,0:T(8,128)(2,1)} %lay_out.1), calls=%async_computation.2 | async-start | bytes 2097152 | tf_op jit(solution)/shard_map/all_to_all | solution.py:36
  101.7 19.7 %collective-permute-start.6 = (bf16[64,1536]{1,0:T(8,128)(2,1)}, bf16[64,1536]{1,0:T(8,128)(2,1)S(1)}, u32[]{:S(2)}, u32[]{:S(2)}) collective-permute-start(bf16[64,1536]{1,0:T(8,128)(2,1)} %get-tuple-element.25), channel_id=1, source_target_pairs={{0,16},{16,32},{32,48},{48,64},{64,80},{80,96},{96,112},{112,128},... | collective-permute-start | bytes 589832 | tf_op jit(solution)/shard_map/ppermute | solution.py:44
  103.8 23.4 %copy-start.4 = (f32[32,1536]{1,0:T(8,128)S(1)}, f32[32,1536]{1,0:T(8,128)}, u32[]{:S(2)}) copy-start(f32[32,1536]{1,0:T(8,128)} %copy-done.3) | copy-start | bytes 589828
  103.8 17.7 %collective-permute-start.5 = (bf16[64,1536]{1,0:T(8,128)(2,1)}, bf16[64,1536]{1,0:T(8,128)(2,1)S(1)}, u32[]{:S(2)}, u32[]{:S(2)}) collective-permute-start(bf16[64,1536]{1,0:T(8,128)(2,1)} %get-tuple-element.26), channel_id=1, source_target_pairs={{0,240},{16,0},{32,16},{48,32},{64,48},{80,64},{96,80},{112,96},{1... | collective-permute-start | bytes 589832 | tf_op jit(solution)/shard_map/ppermute | solution.py:44
  122.3 30.4 %all-to-all-start.3 = ((bf16[8,16,1664]{2,1,0:T(8,128)(2,1)}), bf16[8,16,1664]{2,1,0:T(8,128)(2,1)S(1)}, u32[]{:S(2)}, u32[]{:S(2)}) async-start(bf16[8,16,1664]{2,1,0:T(8,128)(2,1)} %add_odd.1), calls=%async_computation.3 | async-start | bytes 851968 | tf_op jit(solution)/shard_map/all_to_all | solution.py:36

commit v4 on v1

v4 whole, which is shorter than its diff:
```python
import jax
import jax.numpy as jnp
from jax import lax
from jax.experimental import pallas as pl
from jax.experimental.pallas import tpu as pltpu
from jax.sharding import Mesh, PartitionSpec as P

EPSILON = 1e-06
BF = jnp.bfloat16
F32 = jnp.float32

PARTS = (2, 16, 2, 2, 4)
NAMES = ("xh", "z", "core", "xl", "y")
DP = ("xh", "z", "core")
MP = ("xl", "y")
X = ("xh", "xl")
PLANE = ("xh", "core", "xl", "y")
N_MP = 8
N_PLANE = 32
N_Z = 16
PAIRS = 8192
SHARD = 16
WIDTH = 1536
COLUMNS = WIDTH // N_MP
BLOCK = 128
IMAGES = N_PLANE * SHARD
TEXTS = N_Z * SHARD
LANES = 128
WIDE = WIDTH + LANES
HALF = BLOCK // 2
PIECE = BLOCK + HALF

VMEM = pl.BlockSpec(memory_space=pltpu.VMEM)
SMEM = pl.BlockSpec(memory_space=pltpu.SMEM)


def exchange(value, axes):
    return lax.all_to_all(value, axes, 0, 0, tiled=True)


def other_core(value):
    return lax.ppermute(value, "core", [(0, 1), (1, 0)])


def along_x(value, flip):
    return lax.ppermute(value, X, [(i, i ^ flip) for i in range(4)])


def along_y(value, step):
    return lax.ppermute(value, "y", [(i, (i + step) % 4) for i in range(4)])


def split_pair(value):
    high = lax.reduce_precision(value, 8, 7)
    return high.astype(BF), (value - high).astype(BF)


def call(body, outs, operands, specs, name, flops=0, moved=0):
    return pl.pallas_call(
        body,
        out_shape=[jax.ShapeDtypeStruct(shape, dtype) for shape, dtype in outs],
        in_specs=specs,
        out_specs=[VMEM] * len(outs),
        compiler_params=pltpu.CompilerParams(vmem_limit_bytes=24 * 1024 * 1024),
        cost_estimate=pl.CostEstimate(flops=flops, bytes_accessed=moved, transcendentals=0),
        name=name,
    )(*operands)


def dot(a, b, contract):
    return lax.dot_general(a, b, (contract, ((), ())), preferred_element_type=F32)


def terms(similarity, scale, offset, labels):
    value = -labels * (scale * similarity + offset)
    small = jnp.exp(-jnp.abs(value))
    loss = jnp.maximum(value, 0.0) + jnp.log1p(small)
    share = 1.0 / (1.0 + small)
    sigmoid = jnp.where(value >= 0.0, share, small * share)
    return loss, (-labels * sigmoid).astype(BF)


def weights_body(factors, place, images_ref, texts_ref, weight_ref, loss_ref):
    scale, offset = factors[0], factors[1]
    at_plane, at_z = place[0], place[1]
    total = jnp.zeros((1, TEXTS), F32)
    for block in range(IMAGES // BLOCK):
        rows = pl.ds(block * BLOCK, BLOCK)
        similarity = dot(images_ref[rows, :WIDTH], texts_ref[...], ((1,), (1,)))
        image = lax.broadcasted_iota(jnp.int32, similarity.shape, 0) + block * BLOCK
        text = lax.broadcasted_iota(jnp.int32, similarity.shape, 1)
        same = (image // SHARD == at_plane) & (image - SHARD * at_plane == text - SHARD * at_z)
        loss, weight = terms(similarity, scale, offset, jnp.where(same, 1.0, -1.0))
        total = total + jnp.sum(loss, axis=0, keepdims=True)
        weight_ref[rows, :] = weight
    loss_ref[...] = jnp.broadcast_to(jnp.sum(total, axis=1, keepdims=True), loss_ref.shape)


def text_sums_body(factors, loss_ref, images_ref, weight_ref, out_ref):
    scale = factors[0]
    loss = jnp.broadcast_to(loss_ref[0:1, 0:1], (SHARD, LANES))
    high = loss.astype(BF)
    low = (loss - high.astype(F32)).astype(BF)
    lane = lax.broadcasted_iota(jnp.int32, (SHARD, LANES), 1)
    tag = jnp.where(lane == 0, high.astype(F32), jnp.where(lane == 1, low.astype(F32), 0.0))
    for start in range(0, WIDTH, 256):
        cols = pl.ds(start, 256)
        grad = scale * dot(weight_ref[...], images_ref[:, cols], ((0,), (0,)))
        for plane in range(N_Z):
            out_ref[plane, :, cols] = grad[plane * SHARD : (plane + 1) * SHARD].astype(BF)
    for plane in range(N_Z):
        out_ref[plane, :, WIDTH:] = tag.astype(BF)


def image_terms_body(factors, place, images_ref, texts_ref, weight_ref, kept_ref, sent_ref):
    scale = factors[0]
    core = place[2]
    for hi in range(2):
        for out_ref, side in ((sent_ref, 1 - core), (kept_ref, core)):
            rows = pl.ds(pl.multiple_of((hi * 2 + side) * BLOCK, BLOCK), BLOCK)
            grad = dot(weight_ref[rows, :], texts_ref[...], ((1,), (0,)))
            images = images_ref[rows, :WIDTH].astype(F32)
            radial = jnp.sum(images * grad, axis=1, keepdims=True)
            tags = images_ref[rows, WIDTH:].astype(F32)
            inverse = tags[:, 0:1] + tags[:, 1:2]
            term = (grad - images * radial) * (scale * inverse)
            for part in range(N_MP):
                at = part * COLUMNS
                piece = hi * N_MP + part
                out_ref[piece, :BLOCK] = term[:, at : at + BLOCK].astype(out_ref.dtype)
                rest = term[:, at + BLOCK : at + COLUMNS]
                rest = jnp.concatenate([rest[:HALF], rest[HALF:]], axis=1)
                out_ref[piece, BLOCK:] = rest.astype(out_ref.dtype)


def add_core_body(place, kept_ref, other_ref, own_ref, one_ref, two_ref, three_ref):
    at_x = place[3]
    for flip, out_ref in enumerate((own_ref, one_ref, two_ref, three_ref)):
        first = jnp.bitwise_xor(at_x, flip) * 4
        for y in range(4):
            total = kept_ref[first + y] + other_ref[first + y].astype(F32)
            out_ref[y] = total.astype(out_ref.dtype)


def add_x_body(place, own_ref, a_ref, b_ref, c_ref, mine_ref, one_ref, two_ref, three_ref):
    at_y = place[4]
    for step, out_ref in enumerate((mine_ref, one_ref, two_ref, three_ref)):
        y = lax.rem(at_y + step, 4)
        total = own_ref[y] + a_ref[y].astype(F32) + (b_ref[y].astype(F32) + c_ref[y].astype(F32))
        out_ref[...] = total.astype(out_ref.dtype)


def add_y_body(mine_ref, a_ref, b_ref, c_ref, grad_ref):
    total = mine_ref[...] + a_ref[...].astype(F32)
    total = total + (b_ref[...].astype(F32) + c_ref[...].astype(F32))
    grad_ref[:, :LANES] = total[:BLOCK]
    grad_ref[:HALF, LANES:] = total[BLOCK:, :HALF]
    grad_ref[HALF:, LANES:] = total[BLOCK:, HALF:]


def text_body(sums_ref, u_ref, inverse_ref, image_ref, grad_ref, loss_ref):
    total = sums_ref[0].astype(F32)
    for block in range(1, N_Z):
        total = total + sums_ref[block].astype(F32)
    tags = total[0:1, WIDTH:]
    loss_ref[...] = jnp.broadcast_to(tags[:, 0:1] + tags[:, 1:2], loss_ref.shape)
    grad = total[:, :WIDTH]
    u = u_ref[...]
    inverse = inverse_ref[...]
    row_dot = jnp.sum(u * grad, axis=1, keepdims=True)
    grad_ref[...] = inverse * grad - inverse * inverse * inverse * u * row_dot


def on_device(x_img, x_txt, w_img, w_txt, sharpness_factor, offset_vector):
    factors = jnp.concatenate([sharpness_factor, offset_vector])
    place = jnp.stack([lax.axis_index(axes) for axes in (PLANE, "z", "core", X, "y")])
    place = place.astype(jnp.int32)

    part_img = jnp.dot(x_img, w_img, preferred_element_type=F32).astype(BF)
    part_txt = jnp.dot(x_txt, w_txt, preferred_element_type=F32).astype(BF)
    parts = jnp.concatenate(
        [part_img.reshape(N_MP, SHARD, WIDTH), part_txt.reshape(N_MP, SHARD, WIDTH)], axis=1
    )
    parts = exchange(parts, MP)
    u = jnp.sum(parts.astype(F32), axis=0)
    inverse = lax.rsqrt(jnp.sum(u * u, axis=1, keepdims=True) + EPSILON)
    unit = (u * inverse).astype(BF)
    u_txt, inv_txt = u[SHARD:], inverse[SHARD:]
    unit_txt = unit[SHARD:]
    high, low = split_pair(inverse[:SHARD])
    unit_img = jnp.concatenate(
        [unit[:SHARD], high, low, jnp.zeros((SHARD, LANES - 2), BF)], axis=1
    )

    images = exchange(jnp.broadcast_to(unit_img, (N_PLANE, SHARD, WIDE)), PLANE)
    images = images.reshape(IMAGES, WIDE)
    texts = lax.all_gather(unit_txt, ("z",), axis=0, tiled=True)

    weight, loss = call(
        weights_body, [((IMAGES, TEXTS), BF), ((8, LANES), F32)],
        (factors, place, images, texts), [SMEM, SMEM, VMEM, VMEM], "weights",
        flops=403_000_000, moved=2_700_000,
    )

    (term,) = call(
        text_sums_body, [((N_Z, SHARD, WIDE), BF)], (factors, loss, images, weight),
        [SMEM, VMEM, VMEM, VMEM], "text_sums", flops=403_000_000, moved=2_700_000,
    )
    sums = exchange(term, ("z",))

    pieces = N_PLANE // 2
    kept, sent = call(
        image_terms_body, [((pieces, PIECE, LANES), F32), ((pieces, PIECE, LANES), BF)],
        (factors, place, images, texts, weight),
        [SMEM, SMEM, VMEM, VMEM, VMEM], "image_terms",
        flops=403_000_000, moved=4_700_000,
    )
    own, one, two, three = call(
        add_core_body, [((4, PIECE, LANES), F32)] + [((4, PIECE, LANES), BF)] * 3,
        (place, kept, other_core(sent)), [SMEM, VMEM, VMEM], "add_core", moved=3_000_000,
    )
    mine, one, two, three = call(
        add_x_body, [((PIECE, LANES), F32)] + [((PIECE, LANES), BF)] * 3,
        (place, own, along_x(one, 1), along_x(two, 2), along_x(three, 3)),
        [SMEM] + [VMEM] * 4, "add_x", moved=1_200_000,
    )
    (image_grad,) = call(
        add_y_body, [((BLOCK, COLUMNS), F32)],
        (mine, along_y(one, 1), along_y(two, 2), along_y(three, 3)),
        [VMEM] * 4, "add_y", moved=350_000,
    )

    text_grad, loss = call(
        text_body, [((SHARD, WIDTH), F32), ((8, LANES), F32)], (sums, u_txt, inv_txt, image_grad),
        [VMEM] * 3 + [pl.BlockSpec(memory_space=pl.ANY)], "text", moved=1_000_000,
    )
    loss = exchange(jnp.broadcast_to(loss, (N_PLANE, 8, LANES)), PLANE)
    loss = jnp.sum(loss, axis=0)[0, 0:1] * (1.0 / PAIRS)
    return loss, image_grad, text_grad


def solution(mesh):
    parts = Mesh(mesh.devices.reshape(PARTS), NAMES)
    return jax.shard_map(
        on_device,
        mesh=parts,
        in_specs=(P(DP, MP), P(DP, MP), P(MP, None), P(MP, None), P(), P()),
        out_specs=(P(), P(DP, MP), P(DP + MP, None)),
        check_vma=False,
    )
```

time: 185 us -> 142 us (0.77)
  the two profiles are of different devices: /device:TPU:160 before, /device:TPU:1 now
where the time goes in v4:
time: 142 us; the launch traced here: 141 us
  starting transfers between devices  51.2 us (36%)
  blocking collectives  48.4 us (34%)
  waiting for transfers between devices  20.5 us (14%)
  Pallas kernels  8.8 us (6%)
  local copies, waits for them, and re-layouts  5.73 us (4%)
  between operations  3.92 us (3%)
  matrix products  2.42 us (2%)
    all_gather x1, blocking collectives, on_device(): texts = lax.all_gather(unit_txt, ('z',), axis=0, tiled=True)  33.6 us
    all_to_all x3, starting transfers between devices, exchange(): return lax.all_to_all(value, axes, 0, 0, tiled=True)  23.5 us
    all_to_all x1, blocking collectives, exchange(): return lax.all_to_all(value, axes, 0, 0, tiled=True)  14.8 us
    ppermute x3, starting transfers between devices, along_y(): return lax.ppermute(value, 'y', [(i, (i + step) % 4) for i in range(4)])  10.4 us
    ppermute x3, waiting for transfers between devices, along_x(): return lax.ppermute(value, X, [(i, i ^ flip) for i in range(4)])  9.99 us
    ppermute x3, starting transfers between devices, along_x(): return lax.ppermute(value, X, [(i, i ^ flip) for i in range(4)])  9.58 us
    pallas_call x7, Pallas kernels, call(): pl.pallas_call(body, out_shape=[jax.ShapeDtypeStruct(shape, dtype) for sh...  8.8 us
    ppermute x1, starting transfers between devices, other_core(): return lax.ppermute(value, 'core', [(0, 1), (1, 0)])  7.69 us
  transfers between devices with their start and end apart: 10, of which 5 were waited for; matrix products, arithmetic and copies ran while one was open for 1% of the time, Pallas kernels for 2%

profile of v4, /device:TPU:1, one launch (start us, length us, event | category | flops | bytes accessed | tf_op | source)
XLA Modules:
  0.0 141.5 jit_solution(6844871177767503413)
XLA Ops:
  0.6 0.0 copy-start
  0.6 1.0 copy-done
  1.7 1.1 convolution_convert_fusion.1
  2.8 1.4 convolution_convert_fusion
  4.1 0.1 pad_maximum_fusion
  4.2 14.8 %all_to_all.20 = bf16[8,32,1536]{2,1,0:T(8,128)(2,1)S(1)} all-to-all(bf16[8,32,1536]{2,1,0:T(8,128)(2,1)S(1)} %pad_maximum_fusion), channel_id=1, replica_groups=mesh['xh'=2,'z'=16,'core'=2,'xl'=2,'y'=4] {'xl','y'}, dimensions={0} | all-to-all | bytes 1572864 | tf_op jit(solution)/shard_map/all_to_all | solution.py:38
  18.9 0.1 convert_reduce_fusion
  19.0 0.1 multiply_reduce_fusion
  19.2 0.1 slice_bitcast_fusion
  19.3 0.1 multiply_convert_fusion
  19.4 0.1 copy.18
  19.4 0.1 copy.17
  19.6 0.1 concatenate.11
  19.6 1.3 broadcast_in_dim.11
  21.0 9.4 %all-to-all-start.1 = ((bf16[32,16,1664]{2,1,0:T(8,128)(2,1)}), bf16[32,16,1664]{2,1,0:T(8,128)(2,1)S(1)}, u32[]{:S(2)}, u32[]{:S(2)}) async-start(bf16[32,16,1664]{2,1,0:T(8,128)(2,1)} %broadcast_in_dim.11), calls=%async_computation.1 | async-start | bytes 3407872 | tf_op jit(solution)/shard_map/all_to_all | solution.py:38
  31.7 0.1 stack.23.place
  31.8 0.1 pad_maximum_fusion.1.factors
  31.8 33.6 %all_gather.3.texts_ref = bf16[256,1536]{1,0:T(8,128)(2,1)S(1)} all-gather(bf16[16,1536]{1,0:T(8,128)(2,1)S(1)} %get-tuple-element.40), channel_id=1, replica_groups=mesh['xh'=2,'z'=16,'core'=2,'xl'=2,'y'=4] {'z'}, dimensions={0}, use_global_device_ids=true | all-gather | bytes 835584 | tf_op jit(solution)/shard_map/all_gather | solution.py:197
  65.5 0.0 all-to-all-done.1
  65.5 2.1 %weights.1 = (bf16[512,256]{1,0:T(8,128)(2,1)S(1)}, f32[8,128]{1,0:T(8,128)S(1)}) custom-call(f32[2]{0:T(128)S(1)} %pad_maximum_fusion.1.factors, s32[5]{0:T(128)S(1)} %stack.23.place, bf16[512,1664]{1,0:T(8,128)(2,1)S(1)} %bitcast.19, bf16[256,1536]{1,0:T(8,128)(2,1)S(1)} %all_gather.3.texts_ref), custom_call_target="tpu_custom_call" | custom-call | flops 403000000 | bytes 2700000 | tf_op jit(solution)/shard_map/weights/pallas_call | solution.py:59
  67.6 1.2 text_sums.1
  68.8 0.0 copy-start.1
  68.8 0.9 copy-done.1
  69.7 7.5 %all-to-all-start.2 = ((bf16[16,16,1664]{2,1,0:T(8,128)(2,1)}), bf16[16,16,1664]{2,1,0:T(8,128)(2,1)}, u32[]{:S(2)}, u32[]{:S(2)}) async-start(bf16[16,16,1664]{2,1,0:T(8,128)(2,1)} %copy-done.1), calls=%async_computation.2 | async-start | bytes 1703936 | tf_op jit(solution)/shard_map/all_to_all | solution.py:38
  77.2 2.1 %image_terms.1 = (f32[16,192,128]{2,1,0:T(8,128)S(1)}, bf16[16,192,128]{2,1,0:T(8,128)(2,1)S(1)}) custom-call(f32[2]{0:T(128)S(1)} %pad_maximum_fusion.1.factors, s32[5]{0:T(128)S(1)} %stack.23.place, bf16[512,1664]{1,0:T(8,128)(2,1)S(1)} %bitcast.21, bf16[256,1536]{1,0:T(8,128)(2,1)S(1)} %all_gather.3.texts_ref, ...), custom_call_target="tpu_custom_call" | custom-call | flops 403000000 | bytes 4700000 | tf_op jit(solution)/shard_map/image_terms/pallas_call | solution.py:59
  79.4 7.7 %collective-permute-start = (bf16[16,192,128]{2,1,0:T(8,128)(2,1)S(1)}, bf16[16,192,128]{2,1,0:T(8,128)(2,1)S(1)}, u32[]{:S(2)}, u32[]{:S(2)}) collective-permute-start(bf16[16,192,128]{2,1,0:T(8,128)(2,1)S(1)} %get-tuple-element.20), channel_id=1, source_target_pairs={{0,8},{8,0},{1,9},{9,1},{2,10},{10,2},{3,11},{11,3},{4,12},{12,4},... | collective-permute-start | bytes 2359304 | tf_op jit(solution)/shard_map/ppermute | solution.py:42
  87.1 1.9 %collective-permute-done.other_ref = bf16[16,192,128]{2,1,0:T(8,128)(2,1)S(1)} collective-permute-done((bf16[16,192,128]{2,1,0:T(8,128)(2,1)S(1)}, bf16[16,192,128]{2,1,0:T(8,128)(2,1)S(1)}, u32[]{:S(2)}, u32[]{:S(2)}) %collective-permute-start) | collective-permute-done | bytes 786464 | tf_op jit(solution)/shard_map/ppermute | solution.py:42
  89.0 0.7 add_core.1
  89.6 3.3 %collective-permute-start.1 = (bf16[4,192,128]{2,1,0:T(8,128)(2,1)S(1)}, bf16[4,192,128]{2,1,0:T(8,128)(2,1)S(1)}, u32[]{:S(2)}, u32[]{:S(2)}) collective-permute-start(bf16[4,192,128]{2,1,0:T(8,128)(2,1)S(1)} %get-tuple-element.22), channel_id=1, source_target_pairs={{0,4},{4,0},{256,260},{260,256},{1,5},{5,1},{257,261},{261,257},{2... | collective-permute-start | bytes 589832 | tf_op jit(solution)/shard_map/ppermute | solution.py:46
  92.9 4.3 %collective-permute-start.2 = (bf16[4,192,128]{2,1,0:T(8,128)(2,1)S(1)}, bf16[4,192,128]{2,1,0:T(8,128)(2,1)S(1)}, u32[]{:S(2)}, u32[]{:S(2)}) collective-permute-start(bf16[4,192,128]{2,1,0:T(8,128)(2,1)S(1)} %get-tuple-element.23), channel_id=1, source_target_pairs={{0,256},{4,260},{256,0},{260,4},{1,257},{5,261},{257,1},{261,5},{2... | collective-permute-start | bytes 589832 | tf_op jit(solution)/shard_map/ppermute | solution.py:46
  97.3 1.9 %collective-permute-start.3 = (bf16[4,192,128]{2,1,0:T(8,128)(2,1)S(1)}, bf16[4,192,128]{2,1,0:T(8,128)(2,1)S(1)}, u32[]{:S(2)}, u32[]{:S(2)}) collective-permute-start(bf16[4,192,128]{2,1,0:T(8,128)(2,1)S(1)} %get-tuple-element.24), channel_id=1, source_target_pairs={{0,260},{4,256},{256,4},{260,0},{1,261},{5,257},{257,5},{261,1},{2... | collective-permute-start | bytes 589832 | tf_op jit(solution)/shard_map/ppermute | solution.py:46
  99.2 0.0 collective-permute-done.1.a_ref
  99.3 5.1 %collective-permute-done.2.b_ref = bf16[4,192,128]{2,1,0:T(8,128)(2,1)S(1)} collective-permute-done((bf16[4,192,128]{2,1,0:T(8,128)(2,1)S(1)}, bf16[4,192,128]{2,1,0:T(8,128)(2,1)S(1)}, u32[]{:S(2)}, u32[]{:S(2)}) %collective-permute-start.2) | collective-permute-done | bytes 196640 | tf_op jit(solution)/shard_map/ppermute | solution.py:46
  104.3 4.9 %collective-permute-done.3.c_ref = bf16[4,192,128]{2,1,0:T(8,128)(2,1)S(1)} collective-permute-done((bf16[4,192,128]{2,1,0:T(8,128)(2,1)S(1)}, bf16[4,192,128]{2,1,0:T(8,128)(2,1)S(1)}, u32[]{:S(2)}, u32[]{:S(2)}) %collective-permute-start.3) | collective-permute-done | bytes 196640 | tf_op jit(solution)/shard_map/ppermute | solution.py:46
  109.2 0.6 add_x.1
  109.9 3.0 %collective-permute-start.4 = (bf16[192,128]{1,0:T(8,128)(2,1)S(1)}, bf16[192,128]{1,0:T(8,128)(2,1)S(1)}, u32[]{:S(2)}, u32[]{:S(2)}) collective-permute-start(bf16[192,128]{1,0:T(8,128)(2,1)S(1)} %get-tuple-element.26), channel_id=1, source_target_pairs={{0,1},{1,2},{2,3},{3,0},{4,5},{5,6},{6,7},{7,4},{8,9},{9,10},{10,1... | collective-permute-start | bytes 147464 | tf_op jit(solution)/shard_map/ppermute | solution.py:50
  112.9 4.4 %collective-permute-start.5 = (bf16[192,128]{1,0:T(8,128)(2,1)S(1)}, bf16[192,128]{1,0:T(8,128)(2,1)S(1)}, u32[]{:S(2)}, u32[]{:S(2)}) collective-permute-start(bf16[192,128]{1,0:T(8,128)(2,1)S(1)} %get-tuple-element.27), channel_id=1, source_target_pairs={{0,2},{1,3},{2,0},{3,1},{4,6},{5,7},{6,4},{7,5},{8,10},{9,11},{10,... | collective-permute-start | bytes 147464 | tf_op jit(solution)/shard_map/ppermute | solution.py:50
  117.3 3.0 %collective-permute-start.6 = (bf16[192,128]{1,0:T(8,128)(2,1)S(1)}, bf16[192,128]{1,0:T(8,128)(2,1)S(1)}, u32[]{:S(2)}, u32[]{:S(2)}) collective-permute-start(bf16[192,128]{1,0:T(8,128)(2,1)S(1)} %get-tuple-element.28), channel_id=1, source_target_pairs={{0,3},{1,0},{2,1},{3,2},{4,7},{5,4},{6,5},{7,6},{8,11},{9,8},{10,9... | collective-permute-start | bytes 147464 | tf_op jit(solution)/shard_map/ppermute | solution.py:50
  120.3 0.1 copy.20.inverse_ref
  120.4 0.0 collective-permute-done.4.a_ref
  120.4 0.0 collective-permute-done.5.b_ref
  120.4 1.7 %collective-permute-done.6.c_ref = bf16[192,128]{1,0:T(8,128)(2,1)S(1)} collective-permute-done((bf16[192,128]{1,0:T(8,128)(2,1)S(1)}, bf16[192,128]{1,0:T(8,128)(2,1)S(1)}, u32[]{:S(2)}, u32[]{:S(2)}) %collective-permute-start.6) | collective-permute-done | bytes 49184 | tf_op jit(solution)/shard_map/ppermute | solution.py:50
  122.1 0.1 add_y.1.image_ref
  122.2 0.0 all-to-all-done.2.sums_ref
  122.2 2.0 %text.1 = (f32[16,1536]{1,0:T(8,128)}, f32[8,128]{1,0:T(8,128)S(1)}) custom-call(bf16[16,16,1664]{2,1,0:T(8,128)(2,1)} %all-to-all-done.2.sums_ref, f32[16,1536]{1,0:T(8,128)S(1)} %slice.34.u_ref, f32[16,1]{1,0:T(8,128)S(1)} %copy.20.inverse_ref, f32[128,192]{1,0:T(8,128)S(1)} %add_y.1.image_ref), custom_call_target="tpu_custom_call" | custom-call | bytes 1000000 | tf_op jit(solution)/shard_map/text/pallas_call | solution.py:59
  124.2 0.7 broadcast_in_dim.12
  124.9 6.6 %all-to-all-start.3 = ((f32[32,8,128]{2,1,0:T(8,128)}), f32[32,8,128]{2,1,0:T(8,128)S(1)}, u32[]{:S(2)}, u32[]{:S(2)}) async-start(f32[32,8,128]{2,1,0:T(8,128)} %broadcast_in_dim.12), calls=%async_computation.3 | async-start | bytes 262144 | tf_op jit(solution)/shard_map/all_to_all | solution.py:38
  131.5 0.7 copy.21
  132.2 6.9 %all-to-all-done.3 = f32[32,8,128]{2,1,0:T(8,128)S(1)} async-done(((f32[32,8,128]{2,1,0:T(8,128)}), f32[32,8,128]{2,1,0:T(8,128)S(1)}, u32[]{:S(2)}, u32[]{:S(2)}) %all-to-all-start.3) | async-done | bytes 131104 | tf_op jit(solution)/shard_map/all_to_all | solution.py:38
  139.2 0.5 slice.31
  (7 shorter events, 0.1 us)
Async XLA Ops:
  0.6 1.1 copy-start
  21.0 44.5 %all-to-all-start.1 = ((bf16[32,16,1664]{2,1,0:T(8,128)(2,1)}), bf16[32,16,1664]{2,1,0:T(8,128)(2,1)S(1)}, u32[]{:S(2)}, u32[]{:S(2)}) async-start(bf16[32,16,1664]{2,1,0:T(8,128)(2,1)} %broadcast_in_dim.11), calls=%async_computation.1 | async-start | bytes 3407872 | tf_op jit(solution)/shard_map/all_to_all | solution.py:38
  68.8 0.9 copy-start.1
  69.7 52.5 %all-to-all-start.2 = ((bf16[16,16,1664]{2,1,0:T(8,128)(2,1)}), bf16[16,16,1664]{2,1,0:T(8,128)(2,1)}, u32[]{:S(2)}, u32[]{:S(2)}) async-start(bf16[16,16,1664]{2,1,0:T(8,128)(2,1)} %copy-done.1), calls=%async_computation.2 | async-start | bytes 1703936 | tf_op jit(solution)/shard_map/all_to_all | solution.py:38
  79.4 9.6 %collective-permute-start = (bf16[16,192,128]{2,1,0:T(8,128)(2,1)S(1)}, bf16[16,192,128]{2,1,0:T(8,128)(2,1)S(1)}, u32[]{:S(2)}, u32[]{:S(2)}) collective-permute-start(bf16[16,192,128]{2,1,0:T(8,128)(2,1)S(1)} %get-tuple-element.20), channel_id=1, source_target_pairs={{0,8},{8,0},{1,9},{9,1},{2,10},{10,2},{3,11},{11,3},{4,12},{12,4},... | collective-permute-start | bytes 2359304 | tf_op jit(solution)/shard_map/ppermute | solution.py:42
  89.6 9.6 %collective-permute-start.1 = (bf16[4,192,128]{2,1,0:T(8,128)(2,1)S(1)}, bf16[4,192,128]{2,1,0:T(8,128)(2,1)S(1)}, u32[]{:S(2)}, u32[]{:S(2)}) collective-permute-start(bf16[4,192,128]{2,1,0:T(8,128)(2,1)S(1)} %get-tuple-element.22), channel_id=1, source_target_pairs={{0,4},{4,0},{256,260},{260,256},{1,5},{5,1},{257,261},{261,257},{2... | collective-permute-start | bytes 589832 | tf_op jit(solution)/shard_map/ppermute | solution.py:46
  92.9 11.4 %collective-permute-start.2 = (bf16[4,192,128]{2,1,0:T(8,128)(2,1)S(1)}, bf16[4,192,128]{2,1,0:T(8,128)(2,1)S(1)}, u32[]{:S(2)}, u32[]{:S(2)}) collective-permute-start(bf16[4,192,128]{2,1,0:T(8,128)(2,1)S(1)} %get-tuple-element.23), channel_id=1, source_target_pairs={{0,256},{4,260},{256,0},{260,4},{1,257},{5,261},{257,1},{261,5},{2... | collective-permute-start | bytes 589832 | tf_op jit(solution)/shard_map/ppermute | solution.py:46
  97.3 12.0 %collective-permute-start.3 = (bf16[4,192,128]{2,1,0:T(8,128)(2,1)S(1)}, bf16[4,192,128]{2,1,0:T(8,128)(2,1)S(1)}, u32[]{:S(2)}, u32[]{:S(2)}) collective-permute-start(bf16[4,192,128]{2,1,0:T(8,128)(2,1)S(1)} %get-tuple-element.24), channel_id=1, source_target_pairs={{0,260},{4,256},{256,4},{260,0},{1,261},{5,257},{257,5},{261,1},{2... | collective-permute-start | bytes 589832 | tf_op jit(solution)/shard_map/ppermute | solution.py:46
  109.9 10.5 %collective-permute-start.4 = (bf16[192,128]{1,0:T(8,128)(2,1)S(1)}, bf16[192,128]{1,0:T(8,128)(2,1)S(1)}, u32[]{:S(2)}, u32[]{:S(2)}) collective-permute-start(bf16[192,128]{1,0:T(8,128)(2,1)S(1)} %get-tuple-element.26), channel_id=1, source_target_pairs={{0,1},{1,2},{2,3},{3,0},{4,5},{5,6},{6,7},{7,4},{8,9},{9,10},{10,1... | collective-permute-start | bytes 147464 | tf_op jit(solution)/shard_map/ppermute | solution.py:50
  112.9 7.5 %collective-permute-start.5 = (bf16[192,128]{1,0:T(8,128)(2,1)S(1)}, bf16[192,128]{1,0:T(8,128)(2,1)S(1)}, u32[]{:S(2)}, u32[]{:S(2)}) collective-permute-start(bf16[192,128]{1,0:T(8,128)(2,1)S(1)} %get-tuple-element.27), channel_id=1, source_target_pairs={{0,2},{1,3},{2,0},{3,1},{4,6},{5,7},{6,4},{7,5},{8,10},{9,11},{10,... | collective-permute-start | bytes 147464 | tf_op jit(solution)/shard_map/ppermute | solution.py:50
  117.3 4.8 %collective-permute-start.6 = (bf16[192,128]{1,0:T(8,128)(2,1)S(1)}, bf16[192,128]{1,0:T(8,128)(2,1)S(1)}, u32[]{:S(2)}, u32[]{:S(2)}) collective-permute-start(bf16[192,128]{1,0:T(8,128)(2,1)S(1)} %get-tuple-element.28), channel_id=1, source_target_pairs={{0,3},{1,0},{2,1},{3,2},{4,7},{5,4},{6,5},{7,6},{8,11},{9,8},{10,9... | collective-permute-start | bytes 147464 | tf_op jit(solution)/shard_map/ppermute | solution.py:50
  124.9 14.3 %all-to-all-start.3 = ((f32[32,8,128]{2,1,0:T(8,128)}), f32[32,8,128]{2,1,0:T(8,128)S(1)}, u32[]{:S(2)}, u32[]{:S(2)}) async-start(f32[32,8,128]{2,1,0:T(8,128)} %broadcast_in_dim.12), calls=%async_computation.3 | async-start | bytes 262144 | tf_op jit(solution)/shard_map/all_to_all | solution.py:38

commit v5 on v4

v5 whole, which is shorter than its diff:
```python
import jax
import jax.numpy as jnp
from jax import lax
from jax.experimental import pallas as pl
from jax.experimental.pallas import tpu as pltpu
from jax.sharding import Mesh, PartitionSpec as P

EPSILON = 1e-06
BF = jnp.bfloat16
F32 = jnp.float32

PARTS = (2, 16, 2, 2, 4)
NAMES = ("xh", "z", "core", "xl", "y")
DP = ("xh", "z", "core")
MP = ("xl", "y")
X = ("xh", "xl")
PLANE = ("xh", "core", "xl", "y")
N_MP = 8
N_PLANE = 32
N_Z = 16
PAIRS = 8192
SHARD = 16
WIDTH = 1536
COLUMNS = WIDTH // N_MP
BLOCK = 128
IMAGES = N_PLANE * SHARD
TEXTS = N_Z * SHARD
LANES = 128
WIDE = WIDTH + LANES
HALF = BLOCK // 2
PIECE = BLOCK + HALF

CHUNK = 512
COPIED = 4
VMEM = pl.BlockSpec(memory_space=pltpu.VMEM)
HBM = pl.BlockSpec(memory_space=pltpu.HBM)


def exchange(value, axes):
    return lax.all_to_all(value, axes, 0, 0, tiled=True)


def other_core(value):
    return lax.ppermute(value, "core", [(0, 1), (1, 0)])


def along_x(value, flip):
    return lax.ppermute(value, X, [(i, i ^ flip) for i in range(4)])


def along_y(value, step):
    return lax.ppermute(value, "y", [(i, (i + step) % 4) for i in range(4)])


def call(body, outs, operands, specs, name, flops=0, moved=0):
    return pl.pallas_call(
        body,
        out_shape=[jax.ShapeDtypeStruct(shape, dtype) for shape, dtype in outs],
        in_specs=specs,
        out_specs=[VMEM] * len(outs),
        compiler_params=pltpu.CompilerParams(vmem_limit_bytes=24 * 1024 * 1024),
        cost_estimate=pl.CostEstimate(flops=flops, bytes_accessed=moved, transcendentals=0),
        name=name,
    )(*operands)


def dot(a, b, contract):
    return lax.dot_general(a, b, (contract, ((), ())), preferred_element_type=F32)


def terms(similarity, scale, offset, labels):
    value = -labels * (scale * similarity + offset)
    small = jnp.exp(-jnp.abs(value))
    loss = jnp.maximum(value, 0.0) + jnp.log1p(small)
    share = 1.0 / (1.0 + small)
    sigmoid = jnp.where(value >= 0.0, share, small * share)
    return loss, (-labels * sigmoid).astype(BF)


def loss_tag(total, rows):
    loss = jnp.broadcast_to(total, (rows, LANES))
    high = loss.astype(BF)
    low = (loss - high.astype(F32)).astype(BF)
    lane = lax.broadcasted_iota(jnp.int32, (rows, LANES), 1)
    tag = jnp.where(lane == 0, high.astype(F32), jnp.where(lane == 1, low.astype(F32), 0.0))
    return tag.astype(BF)


def normalize_body(parts_ref, images_hbm, text_ref, u_ref, inverse_ref, images_ref, sems):
    copies = []
    for at in (0, SHARD):
        rows = slice(at, at + SHARD)
        u = parts_ref[0, rows].astype(F32)
        for member in range(1, N_MP):
            u = u + parts_ref[member, rows].astype(F32)
        inverse = lax.rsqrt(jnp.sum(u * u, axis=1, keepdims=True) + EPSILON)
        unit = (u * inverse).astype(BF)
        if at:
            text_ref[...] = unit
            u_ref[...] = u
            inverse_ref[...] = jnp.broadcast_to(inverse, inverse_ref.shape)
        else:
            tag = loss_tag(inverse, SHARD)
            for piece in range(COPIED):
                images_ref[piece, :, :WIDTH] = unit
                images_ref[piece, :, WIDTH:] = tag
            for start in range(0, N_PLANE, COPIED):
                target = images_hbm.at[pl.ds(start, COPIED)]
                copies.append(pltpu.make_async_copy(images_ref, target, sems.at[start // COPIED]))
                copies[-1].start()
    for copy in copies:
        copy.wait()


def pairs_body(scale_ref, offset_ref, images_ref, texts_ref, weight_hbm, out_hbm, weight_ref, sums_ref, sems):
    scale, offset = scale_ref[...], offset_ref[...]
    at_plane, at_z = lax.axis_index(PLANE), lax.axis_index("z")
    copies = []

    def send(source, target):
        copies.append(pltpu.make_async_copy(source, target, sems.at[len(copies)]))
        copies[-1].start()

    total = jnp.zeros((1, TEXTS), F32)
    for block in range(IMAGES // BLOCK):
        rows = pl.ds(block * BLOCK, BLOCK)
        similarity = dot(images_ref[rows, :WIDTH], texts_ref[...], ((1,), (1,)))
        image = lax.broadcasted_iota(jnp.int32, similarity.shape, 0) + block * BLOCK
        text = lax.broadcasted_iota(jnp.int32, similarity.shape, 1)
        same = (image // SHARD == at_plane) & (image - SHARD * at_plane == text - SHARD * at_z)
        loss, weight = terms(similarity, scale, offset, jnp.where(same, 1.0, -1.0))
        total = total + jnp.sum(loss, axis=0, keepdims=True)
        weight_ref[rows, :] = weight
    send(weight_ref, weight_hbm)
    tag = loss_tag(jnp.sum(total, axis=1, keepdims=True), SHARD)
    for plane in range(N_Z):
        sums_ref[plane, :, WIDTH:] = tag
    for start in range(0, WIDTH, CHUNK):
        cols = pl.ds(start, CHUNK)
        grad = scale * dot(weight_ref[...], images_ref[:, cols], ((0,), (0,)))
        for plane in range(N_Z):
            sums_ref[plane, :, cols] = grad[plane * SHARD : (plane + 1) * SHARD].astype(BF)
        cols = pl.ds(start, CHUNK + (LANES if start + CHUNK == WIDTH else 0))
        send(sums_ref.at[:, :, cols], out_hbm.at[:, :, cols])
    for copy in copies:
        copy.wait()


def image_terms_body(scale_ref, images_ref, texts_ref, weight_ref, kept_ref, sent_ref):
    scale = scale_ref[...]
    core = lax.axis_index("core")
    for hi in range(2):
        for side_ref, side in ((sent_ref, 1 - core), (kept_ref, core)):
            rows = pl.ds(pl.multiple_of((hi * 2 + side) * BLOCK, BLOCK), BLOCK)
            grad = dot(weight_ref[rows, :], texts_ref[...], ((1,), (0,)))
            images = images_ref[rows, :WIDTH].astype(F32)
            radial = jnp.sum(images * grad, axis=1, keepdims=True)
            tags = images_ref[rows, WIDTH:].astype(F32)
            inverse = tags[:, 0:1] + tags[:, 1:2]
            term = (grad - images * radial) * (scale * inverse)
            for part in range(N_MP):
                at = part * COLUMNS
                piece = hi * N_MP + part
                side_ref[piece, :BLOCK] = term[:, at : at + BLOCK].astype(side_ref.dtype)
                rest = term[:, at + BLOCK : at + COLUMNS]
                rest = jnp.concatenate([rest[:HALF], rest[HALF:]], axis=1)
                side_ref[piece, BLOCK:] = rest.astype(side_ref.dtype)


def add_core_body(kept_ref, other_ref, own_ref, one_ref, two_ref, three_ref):
    at_x = lax.axis_index(X)
    for flip, out_ref in enumerate((own_ref, one_ref, two_ref, three_ref)):
        first = jnp.bitwise_xor(at_x, flip) * 4
        for y in range(4):
            total = kept_ref[first + y] + other_ref[first + y].astype(F32)
            out_ref[y] = total.astype(out_ref.dtype)


def add_x_body(own_ref, a_ref, b_ref, c_ref, mine_ref, one_ref, two_ref, three_ref):
    at_y = lax.axis_index("y")
    for step, out_ref in enumerate((mine_ref, one_ref, two_ref, three_ref)):
        y = lax.rem(at_y + step, 4)
        total = own_ref[y] + a_ref[y].astype(F32) + (b_ref[y].astype(F32) + c_ref[y].astype(F32))
        out_ref[...] = total.astype(out_ref.dtype)


def add_y_body(mine_ref, a_ref, b_ref, c_ref, grad_ref):
    total = mine_ref[...] + a_ref[...].astype(F32)
    total = total + (b_ref[...].astype(F32) + c_ref[...].astype(F32))
    grad_ref[:, :LANES] = total[:BLOCK]
    grad_ref[:HALF, LANES:] = total[BLOCK:, :HALF]
    grad_ref[HALF:, LANES:] = total[BLOCK:, HALF:]


def text_body(sums_ref, u_ref, inverse_ref, image_ref, grad_ref, loss_ref):
    total = sums_ref[0].astype(F32)
    for block in range(1, N_Z):
        total = total + sums_ref[block].astype(F32)
    tags = total[0:1, WIDTH:]
    loss_ref[...] = jnp.broadcast_to((tags[:, 0:1] + tags[:, 1:2])[None], loss_ref.shape)
    grad = total[:, :WIDTH]
    u = u_ref[...]
    inverse = inverse_ref[:, 0:1]
    row_dot = jnp.sum(u * grad, axis=1, keepdims=True)
    grad_ref[...] = inverse * grad - inverse * inverse * inverse * u * row_dot


def on_device(x_img, x_txt, w_img, w_txt, sharpness_factor, offset_vector):
    part_img = jnp.dot(x_img, w_img, preferred_element_type=F32).astype(BF)
    part_txt = jnp.dot(x_txt, w_txt, preferred_element_type=F32).astype(BF)
    parts = jnp.concatenate(
        [part_img.reshape(N_MP, SHARD, WIDTH), part_txt.reshape(N_MP, SHARD, WIDTH)], axis=1
    )
    parts = exchange(parts, MP)
    unit_img, unit_txt, u_txt, inv_txt = pl.pallas_call(
        normalize_body,
        out_shape=[
            pltpu.HBM((N_PLANE, SHARD, WIDE), BF),
            jax.ShapeDtypeStruct((SHARD, WIDTH), BF),
            jax.ShapeDtypeStruct((SHARD, WIDTH), F32),
            jax.ShapeDtypeStruct((SHARD, LANES), F32),
        ],
        in_specs=[VMEM],
        out_specs=[HBM, VMEM, VMEM, VMEM],
        scratch_shapes=[
            pltpu.VMEM((COPIED, SHARD, WIDE), BF),
            pltpu.SemaphoreType.DMA((N_PLANE // COPIED,)),
        ],
        compiler_params=pltpu.CompilerParams(vmem_limit_bytes=24 * 1024 * 1024),
        cost_estimate=pl.CostEstimate(flops=0, bytes_accessed=2_700_000, transcendentals=0),
        name="normalize",
    )(parts)

    images = exchange(unit_img, PLANE)
    images = images.reshape(IMAGES, WIDE)
    texts = lax.all_gather(unit_txt, ("z",), axis=0, tiled=True)

    scale, offset = sharpness_factor.reshape(1, 1), offset_vector.reshape(1, 1)
    weight, term = pl.pallas_call(
        pairs_body,
        out_shape=[pltpu.HBM((IMAGES, TEXTS), BF), pltpu.HBM((N_Z, SHARD, WIDE), BF)],
        in_specs=[VMEM] * 4,
        out_specs=[HBM, HBM],
        scratch_shapes=[
            pltpu.VMEM((IMAGES, TEXTS), BF),
            pltpu.VMEM((N_Z, SHARD, WIDE), BF),
            pltpu.SemaphoreType.DMA((1 + WIDTH // CHUNK,)),
        ],
        compiler_params=pltpu.CompilerParams(vmem_limit_bytes=24 * 1024 * 1024),
        cost_estimate=pl.CostEstimate(flops=806_000_000, bytes_accessed=3_500_000, transcendentals=0),
        name="pairs",
    )(scale, offset, images, texts)
    sums = exchange(term, ("z",))

    pieces = N_PLANE // 2
    kept, sent = call(
        image_terms_body, [((pieces, PIECE, LANES), F32), ((pieces, PIECE, LANES), BF)],
        (scale, images, texts, weight), [VMEM] * 4, "image_terms",
        flops=403_000_000, moved=4_700_000,
    )
    own, one, two, three = call(
        add_core_body, [((4, PIECE, LANES), F32)] + [((4, PIECE, LANES), BF)] * 3,
        (kept, other_core(sent)), [VMEM, VMEM], "add_core", moved=3_000_000,
    )
    mine, one, two, three = call(
        add_x_body, [((PIECE, LANES), F32)] + [((PIECE, LANES), BF)] * 3,
        (own, along_x(two, 2), along_x(three, 3), along_x(one, 1)),
        [VMEM] * 4, "add_x", moved=1_200_000,
    )
    (image_grad,) = call(
        add_y_body, [((BLOCK, COLUMNS), F32)],
        (mine, along_y(two, 2), along_y(one, 1), along_y(three, 3)),
        [VMEM] * 4, "add_y", moved=350_000,
    )

    text_grad, loss = call(
        text_body, [((SHARD, WIDTH), F32), ((N_PLANE, 8, LANES), F32)], (sums, u_txt, inv_txt, image_grad),
        [VMEM] * 3 + [pl.BlockSpec(memory_space=pl.ANY)], "text", moved=1_000_000,
    )
    loss = exchange(loss, PLANE)
    loss = jnp.sum(loss[:, 0, 0]).reshape(1) * (1.0 / PAIRS)
    return loss, image_grad, text_grad


def solution(mesh):
    parts = Mesh(mesh.devices.reshape(PARTS), NAMES)
    return jax.shard_map(
        on_device,
        mesh=parts,
        in_specs=(P(DP, MP), P(DP, MP), P(MP, None), P(MP, None), P(), P()),
        out_specs=(P(), P(DP, MP), P(DP + MP, None)),
        check_vma=False,
    )
```

time: 142 us -> 137 us (0.965)
  waiting for transfers between devices: 20.5 us -> 15.4 us
  starting transfers between devices: 51.2 us -> 55.2 us
  local copies, waits for them, and re-layouts: 5.73 us -> 2.92 us
  Pallas kernels: 8.8 us -> 7 us
    pallas_call x7 -> x5, Pallas kernels: 8.8 us -> 2.77 us  [call(): pl.pallas_call(body, out_shape=[jax.ShapeDtypeStruct(shape, dtype) for sh...]
    ppermute x3, waiting for transfers between devices: 9.99 us -> 5.42 us  [along_x(): return lax.ppermute(value, X, [(i, i ^ flip) for i in range(4)])]
    pallas_call x0 -> x2, Pallas kernels: none -> 4.24 us  [the longest x1 2.8 us: on_device(): pl.pallas_call(pairs_body, out_shape=[pltpu.HBM((IMAGES, TEXTS), BF), plt...]
    all_to_all x3, starting transfers between devices: 23.5 us -> 26.8 us  [exchange(): return lax.all_to_all(value, axes, 0, 0, tiled=True)]
    broadcast_in_dim x3 -> x0, local copies, waits for them, and re-layouts: 1.99 us -> none  [the longest x1 1.32 us: on_device(): images = exchange(jnp.broadcast_to(unit_img, (N_PLANE, SHARD, WIDE)), PLANE)]
    unnamed x5 -> x9, local copies, waits for them, and re-layouts: 2.71 us -> 2.92 us
  transfers between devices with their start and end apart: 10 -> 10, of which waited for: 5 -> 5; matrix products, arithmetic and copies ran while one was open for 1% -> 1% of each run, Pallas kernels for 2% -> 1%
where the time goes in v5:
time: 137 us; the launch traced here: 136 us
  starting transfers between devices  55.2 us (40%)
  blocking collectives  48.4 us (35%)
  waiting for transfers between devices  15.4 us (11%)
  Pallas kernels  7 us (5%)
  between operations  3.9 us (3%)
  local copies, waits for them, and re-layouts  2.92 us (2%)
  matrix products  2.42 us (2%)
    all_gather x1, blocking collectives, on_device(): texts = lax.all_gather(unit_txt, ('z',), axis=0, tiled=True)  33.6 us
    all_to_all x3, starting transfers between devices, exchange(): return lax.all_to_all(value, axes, 0, 0, tiled=True)  26.8 us
    all_to_all x1, blocking collectives, exchange(): return lax.all_to_all(value, axes, 0, 0, tiled=True)  14.8 us
    ppermute x3, starting transfers between devices, along_y(): return lax.ppermute(value, 'y', [(i, (i + step) % 4) for i in range(4)])  11.1 us
    ppermute x3, starting transfers between devices, along_x(): return lax.ppermute(value, X, [(i, i ^ flip) for i in range(4)])  9.52 us
    ppermute x1, starting transfers between devices, other_core(): return lax.ppermute(value, 'core', [(0, 1), (1, 0)])  7.69 us
    all_to_all x3, waiting for transfers between devices, exchange(): return lax.all_to_all(value, axes, 0, 0, tiled=True)  6.9 us
    ppermute x3, waiting for transfers between devices, along_x(): return lax.ppermute(value, X, [(i, i ^ flip) for i in range(4)])  5.42 us
  transfers between devices with their start and end apart: 10, of which 5 were waited for; matrix products, arithmetic and copies ran while one was open for 1% of the time, Pallas kernels for 1%

profile of v5, /device:TPU:1, one launch (start us, length us, event | category | flops | bytes accessed | tf_op | source)
XLA Modules:
  0.0 135.9 jit_solution(2640523358321266257)
XLA Ops:
  0.6 0.0 copy-start
  0.6 1.0 copy-done
  1.7 1.1 convolution_convert_fusion
  2.8 1.4 convolution_convert_fusion.1
  4.1 0.1 pad_maximum_fusion
  4.2 14.8 %all_to_all.20.parts_ref = bf16[8,32,1536]{2,1,0:T(8,128)(2,1)S(1)} all-to-all(bf16[8,32,1536]{2,1,0:T(8,128)(2,1)S(1)} %pad_maximum_fusion), channel_id=1, replica_groups=mesh['xh'=2,'z'=16,'core'=2,'xl'=2,'y'=4] {'xl','y'}, dimensions={0} | all-to-all | bytes 1572864 | tf_op jit(solution)/shard_map/all_to_all | solution.py:40
  18.9 1.4 %normalize.1 = (bf16[32,16,1664]{2,1,0:T(8,128)(2,1)}, bf16[16,1536]{1,0:T(8,128)(2,1)S(1)}, f32[16,1536]{1,0:T(8,128)S(1)}, f32[16,128]{1,0:T(8,128)S(1)}) custom-call(bf16[8,32,1536]{2,1,0:T(8,128)(2,1)S(1)} %all_to_all.20.parts_ref), custom_call_target="tpu_custom_call" | custom-call | bytes 2700000 | tf_op jit(solution)/shard_map/normalize/pallas_call | solution.py:215
  20.4 9.4 %all-to-all-start.1 = ((bf16[32,16,1664]{2,1,0:T(8,128)(2,1)}), bf16[32,16,1664]{2,1,0:T(8,128)(2,1)S(1)}, u32[]{:S(2)}, u32[]{:S(2)}) async-start(bf16[32,16,1664]{2,1,0:T(8,128)(2,1)} %get-tuple-element.21), calls=%async_computation.1 | async-start | bytes 3407872 | tf_op jit(solution)/shard_map/all_to_all | solution.py:40
  31.1 33.6 %all_gather.3.texts_ref = bf16[256,1536]{1,0:T(8,128)(2,1)S(1)} all-gather(bf16[16,1536]{1,0:T(8,128)(2,1)S(1)} %get-tuple-element.22), channel_id=1, replica_groups=mesh['xh'=2,'z'=16,'core'=2,'xl'=2,'y'=4] {'z'}, dimensions={0}, use_global_device_ids=true | all-gather | bytes 835584 | tf_op jit(solution)/shard_map/all_gather | solution.py:236
  64.7 0.0 copy-start.1
  64.7 0.0 all-to-all-done.1
  64.7 2.8 %pairs.1 = (bf16[512,256]{1,0:T(8,128)(2,1)}, bf16[16,16,1664]{2,1,0:T(8,128)(2,1)}) custom-call(f32[1,1]{1,0:T(1,128)} %bitcast.10.scale_ref, f32[1,1]{1,0:T(1,128)} %bitcast.12.offset_ref, bf16[512,1664]{1,0:T(8,128)(2,1)S(1)} %bitcast.13, bf16[256,1536]{1,0:T(8,128)(2,1)S(1)} %all_gather.3.texts_ref), custom_call_target="tpu_custom_call" | custom-call | flops 806000000 | bytes 3500000 | tf_op jit(solution)/shard_map/pairs/pallas_call | solution.py:239
  67.5 0.0 copy-start.3
  67.5 0.0 copy-done.1
  67.6 7.6 %all-to-all-start.2 = ((bf16[16,16,1664]{2,1,0:T(8,128)(2,1)}), bf16[16,16,1664]{2,1,0:T(8,128)(2,1)S(1)}, u32[]{:S(2)}, u32[]{:S(2)}) async-start(bf16[16,16,1664]{2,1,0:T(8,128)(2,1)} %get-tuple-element.23), calls=%async_computation.2 | async-start | bytes 1703936 | tf_op jit(solution)/shard_map/all_to_all | solution.py:40
  75.2 0.0 copy-done.3
  75.2 0.0 copy-start.2
  75.2 1.1 copy-done.2
  76.3 1.6 %image_terms.1 = (f32[16,192,128]{2,1,0:T(8,128)S(1)}, bf16[16,192,128]{2,1,0:T(8,128)(2,1)S(1)}) custom-call(f32[1,1]{1,0:T(1,128)} %bitcast.11.scale_ref, bf16[512,1664]{1,0:T(8,128)(2,1)S(1)} %bitcast.14, bf16[256,1536]{1,0:T(8,128)(2,1)S(1)} %copy-done.2, bf16[512,256]{1,0:T(8,128)(2,1)S(1)} %copy-done.3), custom_call_target="tpu_custom_call" | custom-call | flops 403000000 | bytes 4700000 | tf_op jit(solution)/shard_map/image_terms/pallas_call | solution.py:56
  78.0 7.7 %collective-permute-start = (bf16[16,192,128]{2,1,0:T(8,128)(2,1)S(1)}, bf16[16,192,128]{2,1,0:T(8,128)(2,1)S(1)}, u32[]{:S(2)}, u32[]{:S(2)}) collective-permute-start(bf16[16,192,128]{2,1,0:T(8,128)(2,1)S(1)} %get-tuple-element.28), channel_id=1, source_target_pairs={{0,8},{8,0},{1,9},{9,1},{2,10},{10,2},{3,11},{11,3},{4,12},{12,4},... | collective-permute-start | bytes 2359304 | tf_op jit(solution)/shard_map/ppermute | solution.py:44
  85.7 1.9 %collective-permute-done.other_ref = bf16[16,192,128]{2,1,0:T(8,128)(2,1)S(1)} collective-permute-done((bf16[16,192,128]{2,1,0:T(8,128)(2,1)S(1)}, bf16[16,192,128]{2,1,0:T(8,128)(2,1)S(1)}, u32[]{:S(2)}, u32[]{:S(2)}) %collective-permute-start) | collective-permute-done | bytes 786464 | tf_op jit(solution)/shard_map/ppermute | solution.py:44
  87.6 0.1 add_core.1
  87.7 4.8 %collective-permute-start.1 = (bf16[4,192,128]{2,1,0:T(8,128)(2,1)S(1)}, bf16[4,192,128]{2,1,0:T(8,128)(2,1)S(1)}, u32[]{:S(2)}, u32[]{:S(2)}) collective-permute-start(bf16[4,192,128]{2,1,0:T(8,128)(2,1)S(1)} %get-tuple-element.30), channel_id=1, source_target_pairs={{0,256},{4,260},{256,0},{260,4},{1,257},{5,261},{257,1},{261,5},{2... | collective-permute-start | bytes 589832 | tf_op jit(solution)/shard_map/ppermute | solution.py:48
  92.5 2.8 %collective-permute-start.2 = (bf16[4,192,128]{2,1,0:T(8,128)(2,1)S(1)}, bf16[4,192,128]{2,1,0:T(8,128)(2,1)S(1)}, u32[]{:S(2)}, u32[]{:S(2)}) collective-permute-start(bf16[4,192,128]{2,1,0:T(8,128)(2,1)S(1)} %get-tuple-element.31), channel_id=1, source_target_pairs={{0,260},{4,256},{256,4},{260,0},{1,261},{5,257},{257,5},{261,1},{2... | collective-permute-start | bytes 589832 | tf_op jit(solution)/shard_map/ppermute | solution.py:48
  95.3 1.9 %collective-permute-start.3 = (bf16[4,192,128]{2,1,0:T(8,128)(2,1)S(1)}, bf16[4,192,128]{2,1,0:T(8,128)(2,1)S(1)}, u32[]{:S(2)}, u32[]{:S(2)}) collective-permute-start(bf16[4,192,128]{2,1,0:T(8,128)(2,1)S(1)} %get-tuple-element.32), channel_id=1, source_target_pairs={{0,4},{4,0},{256,260},{260,256},{1,5},{5,1},{257,261},{261,257},{2... | collective-permute-start | bytes 589832 | tf_op jit(solution)/shard_map/ppermute | solution.py:48
  97.2 0.0 collective-permute-done.1.a_ref
  97.2 4.2 %collective-permute-done.2.b_ref = bf16[4,192,128]{2,1,0:T(8,128)(2,1)S(1)} collective-permute-done((bf16[4,192,128]{2,1,0:T(8,128)(2,1)S(1)}, bf16[4,192,128]{2,1,0:T(8,128)(2,1)S(1)}, u32[]{:S(2)}, u32[]{:S(2)}) %collective-permute-start.2) | collective-permute-done | bytes 196640 | tf_op jit(solution)/shard_map/ppermute | solution.py:48
  101.4 1.2 collective-permute-done.3.c_ref
  102.7 0.1 add_x.1
  102.8 4.6 %collective-permute-start.4 = (bf16[192,128]{1,0:T(8,128)(2,1)S(1)}, bf16[192,128]{1,0:T(8,128)(2,1)S(1)}, u32[]{:S(2)}, u32[]{:S(2)}) collective-permute-start(bf16[192,128]{1,0:T(8,128)(2,1)S(1)} %get-tuple-element.34), channel_id=1, source_target_pairs={{0,2},{1,3},{2,0},{3,1},{4,6},{5,7},{6,4},{7,5},{8,10},{9,11},{10,... | collective-permute-start | bytes 147464 | tf_op jit(solution)/shard_map/ppermute | solution.py:52
  107.4 2.2 %collective-permute-start.5 = (bf16[192,128]{1,0:T(8,128)(2,1)S(1)}, bf16[192,128]{1,0:T(8,128)(2,1)S(1)}, u32[]{:S(2)}, u32[]{:S(2)}) collective-permute-start(bf16[192,128]{1,0:T(8,128)(2,1)S(1)} %get-tuple-element.35), channel_id=1, source_target_pairs={{0,1},{1,2},{2,3},{3,0},{4,5},{5,6},{6,7},{7,4},{8,9},{9,10},{10,1... | collective-permute-start | bytes 147464 | tf_op jit(solution)/shard_map/ppermute | solution.py:52
  109.6 4.3 %collective-permute-start.6 = (bf16[192,128]{1,0:T(8,128)(2,1)S(1)}, bf16[192,128]{1,0:T(8,128)(2,1)S(1)}, u32[]{:S(2)}, u32[]{:S(2)}) collective-permute-start(bf16[192,128]{1,0:T(8,128)(2,1)S(1)} %get-tuple-element.36), channel_id=1, source_target_pairs={{0,3},{1,0},{2,1},{3,2},{4,7},{5,4},{6,5},{7,6},{8,11},{9,8},{10,9... | collective-permute-start | bytes 147464 | tf_op jit(solution)/shard_map/ppermute | solution.py:52
  113.9 0.0 collective-permute-done.4.a_ref
  113.9 0.0 collective-permute-done.5.b_ref
  113.9 1.1 collective-permute-done.6.c_ref
  115.1 0.1 add_y.1.image_ref
  115.2 0.0 all-to-all-done.2.sums_ref
  115.2 0.8 text.1
  116.0 9.8 %all-to-all-start.3 = ((f32[32,8,128]{2,1,0:T(8,128)}), f32[32,8,128]{2,1,0:T(8,128)S(1)}, u32[]{:S(2)}, u32[]{:S(2)}) async-start(f32[32,8,128]{2,1,0:T(8,128)} %get-tuple-element.37), calls=%async_computation.3 | async-start | bytes 262144 | tf_op jit(solution)/shard_map/all_to_all | solution.py:40
  125.8 0.7 copy.9
  126.5 6.9 %all-to-all-done.3 = f32[32,8,128]{2,1,0:T(8,128)S(1)} async-done(((f32[32,8,128]{2,1,0:T(8,128)}), f32[32,8,128]{2,1,0:T(8,128)S(1)}, u32[]{:S(2)}, u32[]{:S(2)}) %all-to-all-start.3) | async-done | bytes 131104 | tf_op jit(solution)/shard_map/all_to_all | solution.py:40
  133.4 0.6 slice_reduce_fusion
Async XLA Ops:
  0.6 1.1 copy-start
  20.4 44.3 %all-to-all-start.1 = ((bf16[32,16,1664]{2,1,0:T(8,128)(2,1)}), bf16[32,16,1664]{2,1,0:T(8,128)(2,1)S(1)}, u32[]{:S(2)}, u32[]{:S(2)}) async-start(bf16[32,16,1664]{2,1,0:T(8,128)(2,1)} %get-tuple-element.21), calls=%async_computation.1 | async-start | bytes 3407872 | tf_op jit(solution)/shard_map/all_to_all | solution.py:40
  64.7 2.8 %copy-start.1 = (bf16[256,1536]{1,0:T(8,128)(2,1)}, bf16[256,1536]{1,0:T(8,128)(2,1)S(1)}, u32[]{:S(2)}) copy-start(bf16[256,1536]{1,0:T(8,128)(2,1)S(1)} %all_gather.3.texts_ref) | copy-start | bytes 2359300
  67.5 7.7 %copy-start.3 = (bf16[512,256]{1,0:T(8,128)(2,1)S(1)}, bf16[512,256]{1,0:T(8,128)(2,1)}, u32[]{:S(2)}) copy-start(bf16[512,256]{1,0:T(8,128)(2,1)} %get-tuple-element.26.weight_ref) | copy-start | bytes 786436
  67.6 47.6 %all-to-all-start.2 = ((bf16[16,16,1664]{2,1,0:T(8,128)(2,1)}), bf16[16,16,1664]{2,1,0:T(8,128)(2,1)S(1)}, u32[]{:S(2)}, u32[]{:S(2)}) async-start(bf16[16,16,1664]{2,1,0:T(8,128)(2,1)} %get-tuple-element.23), calls=%async_computation.2 | async-start | bytes 1703936 | tf_op jit(solution)/shard_map/all_to_all | solution.py:40
  75.2 1.1 copy-start.2
  78.0 9.6 %collective-permute-start = (bf16[16,192,128]{2,1,0:T(8,128)(2,1)S(1)}, bf16[16,192,128]{2,1,0:T(8,128)(2,1)S(1)}, u32[]{:S(2)}, u32[]{:S(2)}) collective-permute-start(bf16[16,192,128]{2,1,0:T(8,128)(2,1)S(1)} %get-tuple-element.28), channel_id=1, source_target_pairs={{0,8},{8,0},{1,9},{9,1},{2,10},{10,2},{3,11},{11,3},{4,12},{12,4},... | collective-permute-start | bytes 2359304 | tf_op jit(solution)/shard_map/ppermute | solution.py:44
  87.7 9.5 %collective-permute-start.1 = (bf16[4,192,128]{2,1,0:T(8,128)(2,1)S(1)}, bf16[4,192,128]{2,1,0:T(8,128)(2,1)S(1)}, u32[]{:S(2)}, u32[]{:S(2)}) collective-permute-start(bf16[4,192,128]{2,1,0:T(8,128)(2,1)S(1)} %get-tuple-element.30), channel_id=1, source_target_pairs={{0,256},{4,260},{256,0},{260,4},{1,257},{5,261},{257,1},{261,5},{2... | collective-permute-start | bytes 589832 | tf_op jit(solution)/shard_map/ppermute | solution.py:48
  92.5 8.9 %collective-permute-start.2 = (bf16[4,192,128]{2,1,0:T(8,128)(2,1)S(1)}, bf16[4,192,128]{2,1,0:T(8,128)(2,1)S(1)}, u32[]{:S(2)}, u32[]{:S(2)}) collective-permute-start(bf16[4,192,128]{2,1,0:T(8,128)(2,1)S(1)} %get-tuple-element.31), channel_id=1, source_target_pairs={{0,260},{4,256},{256,4},{260,0},{1,261},{5,257},{257,5},{261,1},{2... | collective-permute-start | bytes 589832 | tf_op jit(solution)/shard_map/ppermute | solution.py:48
  95.3 7.4 %collective-permute-start.3 = (bf16[4,192,128]{2,1,0:T(8,128)(2,1)S(1)}, bf16[4,192,128]{2,1,0:T(8,128)(2,1)S(1)}, u32[]{:S(2)}, u32[]{:S(2)}) collective-permute-start(bf16[4,192,128]{2,1,0:T(8,128)(2,1)S(1)} %get-tuple-element.32), channel_id=1, source_target_pairs={{0,4},{4,0},{256,260},{260,256},{1,5},{5,1},{257,261},{261,257},{2... | collective-permute-start | bytes 589832 | tf_op jit(solution)/shard_map/ppermute | solution.py:48
  102.8 11.2 %collective-permute-start.4 = (bf16[192,128]{1,0:T(8,128)(2,1)S(1)}, bf16[192,128]{1,0:T(8,128)(2,1)S(1)}, u32[]{:S(2)}, u32[]{:S(2)}) collective-permute-start(bf16[192,128]{1,0:T(8,128)(2,1)S(1)} %get-tuple-element.34), channel_id=1, source_target_pairs={{0,2},{1,3},{2,0},{3,1},{4,6},{5,7},{6,4},{7,5},{8,10},{9,11},{10,... | collective-permute-start | bytes 147464 | tf_op jit(solution)/shard_map/ppermute | solution.py:52
  107.4 6.5 %collective-permute-start.5 = (bf16[192,128]{1,0:T(8,128)(2,1)S(1)}, bf16[192,128]{1,0:T(8,128)(2,1)S(1)}, u32[]{:S(2)}, u32[]{:S(2)}) collective-permute-start(bf16[192,128]{1,0:T(8,128)(2,1)S(1)} %get-tuple-element.35), channel_id=1, source_target_pairs={{0,1},{1,2},{2,3},{3,0},{4,5},{5,6},{6,7},{7,4},{8,9},{9,10},{10,1... | collective-permute-start | bytes 147464 | tf_op jit(solution)/shard_map/ppermute | solution.py:52
  109.6 5.5 %collective-permute-start.6 = (bf16[192,128]{1,0:T(8,128)(2,1)S(1)}, bf16[192,128]{1,0:T(8,128)(2,1)S(1)}, u32[]{:S(2)}, u32[]{:S(2)}) collective-permute-start(bf16[192,128]{1,0:T(8,128)(2,1)S(1)} %get-tuple-element.36), channel_id=1, source_target_pairs={{0,3},{1,0},{2,1},{3,2},{4,7},{5,4},{6,5},{7,6},{8,11},{9,8},{10,9... | collective-permute-start | bytes 147464 | tf_op jit(solution)/shard_map/ppermute | solution.py:52
  116.0 17.4 %all-to-all-start.3 = ((f32[32,8,128]{2,1,0:T(8,128)}), f32[32,8,128]{2,1,0:T(8,128)S(1)}, u32[]{:S(2)}, u32[]{:S(2)}) async-start(f32[32,8,128]{2,1,0:T(8,128)} %get-tuple-element.37), calls=%async_computation.3 | async-start | bytes 262144 | tf_op jit(solution)/shard_map/all_to_all | solution.py:40

commit v6 on v5

--- a/solution.py
+++ b/solution.py
@@ -264,17 +264,17 @@
     )
     mine, one, two, three = call(
         add_x_body, [((PIECE, LANES), F32)] + [((PIECE, LANES), BF)] * 3,
-        (own, along_x(two, 2), along_x(three, 3), along_x(one, 1)),
+        (own, along_x(two, 2), along_x(one, 1), along_x(three, 3)),
         [VMEM] * 4, "add_x", moved=1_200_000,
     )
     (image_grad,) = call(
         add_y_body, [((BLOCK, COLUMNS), F32)],
-        (mine, along_y(two, 2), along_y(one, 1), along_y(three, 3)),
+        (mine, along_y(two, 2), along_y(three, 3), along_y(one, 1)),
         [VMEM] * 4, "add_y", moved=350_000,
     )
 
     text_grad, loss = call(
-        text_body, [((SHARD, WIDTH), F32), ((N_PLANE, 8, LANES), F32)], (sums, u_txt, inv_txt, image_grad),
+        text_body, [((SHARD, WIDTH), F32), ((N_PLANE, 1, LANES), F32)], (sums, u_txt, inv_txt, image_grad),
         [VMEM] * 3 + [pl.BlockSpec(memory_space=pl.ANY)], "text", moved=1_000_000,
     )
     loss = exchange(loss, PLANE)

time: 137 us -> 135 us (0.985)
  starting transfers between devices: 55.2 us -> 51.2 us
  waiting for transfers between devices: 15.4 us -> 17.9 us
    all_to_all x3, starting transfers between devices: 26.8 us -> 24.1 us  [exchange(): return lax.all_to_all(value, axes, 0, 0, tiled=True)]
    ppermute x3, waiting for transfers between devices: 1.14 us -> 3.85 us  [along_y(): return lax.ppermute(value, 'y', [(i, (i + step) % 4) for i in range(4)])]
where the time goes in v6:
time: 135 us; the launch traced here: 134 us
  starting transfers between devices  51.2 us (38%)
  blocking collectives  48.4 us (36%)
  waiting for transfers between devices  17.9 us (13%)
  Pallas kernels  7 us (5%)
  between operations  3.9 us (3%)
  local copies, waits for them, and re-layouts  2.92 us (2%)
  matrix products  2.42 us (2%)
    all_gather x1, blocking collectives, on_device(): texts = lax.all_gather(unit_txt, ('z',), axis=0, tiled=True)  33.6 us
    all_to_all x3, starting transfers between devices, exchange(): return lax.all_to_all(value, axes, 0, 0, tiled=True)  24.1 us
    all_to_all x1, blocking collectives, exchange(): return lax.all_to_all(value, axes, 0, 0, tiled=True)  14.8 us
    ppermute x3, starting transfers between devices, along_y(): return lax.ppermute(value, 'y', [(i, (i + step) % 4) for i in range(4)])  9.82 us
    ppermute x3, starting transfers between devices, along_x(): return lax.ppermute(value, X, [(i, i ^ flip) for i in range(4)])  9.52 us
    ppermute x1, starting transfers between devices, other_core(): return lax.ppermute(value, 'core', [(0, 1), (1, 0)])  7.69 us
    all_to_all x3, waiting for transfers between devices, exchange(): return lax.all_to_all(value, axes, 0, 0, tiled=True)  6.14 us
    ppermute x3, waiting for transfers between devices, along_x(): return lax.ppermute(value, X, [(i, i ^ flip) for i in range(4)])  6.07 us
  transfers between devices with their start and end apart: 10, of which 5 were waited for; matrix products, arithmetic and copies ran while one was open for 1% of the time, Pallas kernels for 1%

profile of v6, /device:TPU:1, one launch (start us, length us, event | category | flops | bytes accessed | tf_op | source)
XLA Modules:
  0.0 134.4 jit_solution(1062283740092841392)
XLA Ops:
  0.6 0.0 copy-start
  0.6 1.0 copy-done
  1.7 1.1 convolution_convert_fusion
  2.8 1.4 %convolution_convert_fusion.1 = bf16[128,1536]{1,0:T(8,128)(2,1)S(1)} fusion(bf16[128,176]{0,1:T(8,128)(2,1)} %param.6, bf16[176,1536]{1,0:T(8,128)(2,1)} %param.8), kind=kOutput, calls=%fused_computation.1 | convolution fusion | flops 69402624 | bytes 978944 | tf_op jit(solution)/shard_map/dot_general | solution.py:209
  4.1 0.1 pad_maximum_fusion
  4.2 14.8 %all_to_all.20.parts_ref = bf16[8,32,1536]{2,1,0:T(8,128)(2,1)S(1)} all-to-all(bf16[8,32,1536]{2,1,0:T(8,128)(2,1)S(1)} %pad_maximum_fusion), channel_id=1, replica_groups=mesh['xh'=2,'z'=16,'core'=2,'xl'=2,'y'=4] {'xl','y'}, dimensions={0} | all-to-all | bytes 1572864 | tf_op jit(solution)/shard_map/all_to_all | solution.py:40
  18.9 1.4 %normalize.1 = (bf16[32,16,1664]{2,1,0:T(8,128)(2,1)}, bf16[16,1536]{1,0:T(8,128)(2,1)S(1)}, f32[16,1536]{1,0:T(8,128)S(1)}, f32[16,128]{1,0:T(8,128)S(1)}) custom-call(bf16[8,32,1536]{2,1,0:T(8,128)(2,1)S(1)} %all_to_all.20.parts_ref), custom_call_target="tpu_custom_call" | custom-call | bytes 2700000 | tf_op jit(solution)/shard_map/normalize/pallas_call | solution.py:215
  20.4 9.4 %all-to-all-start.1 = ((bf16[32,16,1664]{2,1,0:T(8,128)(2,1)}), bf16[32,16,1664]{2,1,0:T(8,128)(2,1)S(1)}, u32[]{:S(2)}, u32[]{:S(2)}) async-start(bf16[32,16,1664]{2,1,0:T(8,128)(2,1)} %get-tuple-element.21), calls=%async_computation.1 | async-start | bytes 3407872 | tf_op jit(solution)/shard_map/all_to_all | solution.py:40
  31.1 33.6 %all_gather.3.texts_ref = bf16[256,1536]{1,0:T(8,128)(2,1)S(1)} all-gather(bf16[16,1536]{1,0:T(8,128)(2,1)S(1)} %get-tuple-element.22), channel_id=1, replica_groups=mesh['xh'=2,'z'=16,'core'=2,'xl'=2,'y'=4] {'z'}, dimensions={0}, use_global_device_ids=true | all-gather | bytes 835584 | tf_op jit(solution)/shard_map/all_gather | solution.py:236
  64.7 0.0 copy-start.1
  64.7 0.0 all-to-all-done.1
  64.7 2.8 %pairs.1 = (bf16[512,256]{1,0:T(8,128)(2,1)}, bf16[16,16,1664]{2,1,0:T(8,128)(2,1)}) custom-call(f32[1,1]{1,0:T(1,128)} %bitcast.10.scale_ref, f32[1,1]{1,0:T(1,128)} %bitcast.12.offset_ref, bf16[512,1664]{1,0:T(8,128)(2,1)S(1)} %bitcast.13, bf16[256,1536]{1,0:T(8,128)(2,1)S(1)} %all_gather.3.texts_ref), custom_call_target="tpu_custom_call" | custom-call | flops 806000000 | bytes 3500000 | tf_op jit(solution)/shard_map/pairs/pallas_call | solution.py:239
  67.5 0.0 copy-start.3
  67.5 0.0 copy-done.1
  67.6 7.6 %all-to-all-start.2 = ((bf16[16,16,1664]{2,1,0:T(8,128)(2,1)}), bf16[16,16,1664]{2,1,0:T(8,128)(2,1)S(1)}, u32[]{:S(2)}, u32[]{:S(2)}) async-start(bf16[16,16,1664]{2,1,0:T(8,128)(2,1)} %get-tuple-element.23), calls=%async_computation.2 | async-start | bytes 1703936 | tf_op jit(solution)/shard_map/all_to_all | solution.py:40
  75.2 0.0 copy-done.3
  75.2 0.0 copy-start.2
  75.2 1.1 copy-done.2
  76.3 1.6 %image_terms.1 = (f32[16,192,128]{2,1,0:T(8,128)S(1)}, bf16[16,192,128]{2,1,0:T(8,128)(2,1)S(1)}) custom-call(f32[1,1]{1,0:T(1,128)} %bitcast.11.scale_ref, bf16[512,1664]{1,0:T(8,128)(2,1)S(1)} %bitcast.14, bf16[256,1536]{1,0:T(8,128)(2,1)S(1)} %copy-done.2, bf16[512,256]{1,0:T(8,128)(2,1)S(1)} %copy-done.3), custom_call_target="tpu_custom_call" | custom-call | flops 403000000 | bytes 4700000 | tf_op jit(solution)/shard_map/image_terms/pallas_call | solution.py:56
  78.0 7.7 %collective-permute-start = (bf16[16,192,128]{2,1,0:T(8,128)(2,1)S(1)}, bf16[16,192,128]{2,1,0:T(8,128)(2,1)S(1)}, u32[]{:S(2)}, u32[]{:S(2)}) collective-permute-start(bf16[16,192,128]{2,1,0:T(8,128)(2,1)S(1)} %get-tuple-element.28), channel_id=1, source_target_pairs={{0,8},{8,0},{1,9},{9,1},{2,10},{10,2},{3,11},{11,3},{4,12},{12,4},... | collective-permute-start | bytes 2359304 | tf_op jit(solution)/shard_map/ppermute | solution.py:44
  85.7 1.9 %collective-permute-done.other_ref = bf16[16,192,128]{2,1,0:T(8,128)(2,1)S(1)} collective-permute-done((bf16[16,192,128]{2,1,0:T(8,128)(2,1)S(1)}, bf16[16,192,128]{2,1,0:T(8,128)(2,1)S(1)}, u32[]{:S(2)}, u32[]{:S(2)}) %collective-permute-start) | collective-permute-done | bytes 786464 | tf_op jit(solution)/shard_map/ppermute | solution.py:44
  87.6 0.1 add_core.1
  87.7 4.8 %collective-permute-start.1 = (bf16[4,192,128]{2,1,0:T(8,128)(2,1)S(1)}, bf16[4,192,128]{2,1,0:T(8,128)(2,1)S(1)}, u32[]{:S(2)}, u32[]{:S(2)}) collective-permute-start(bf16[4,192,128]{2,1,0:T(8,128)(2,1)S(1)} %get-tuple-element.30), channel_id=1, source_target_pairs={{0,256},{4,260},{256,0},{260,4},{1,257},{5,261},{257,1},{261,5},{2... | collective-permute-start | bytes 589832 | tf_op jit(solution)/shard_map/ppermute | solution.py:48
  92.5 2.2 %collective-permute-start.2 = (bf16[4,192,128]{2,1,0:T(8,128)(2,1)S(1)}, bf16[4,192,128]{2,1,0:T(8,128)(2,1)S(1)}, u32[]{:S(2)}, u32[]{:S(2)}) collective-permute-start(bf16[4,192,128]{2,1,0:T(8,128)(2,1)S(1)} %get-tuple-element.31), channel_id=1, source_target_pairs={{0,4},{4,0},{256,260},{260,256},{1,5},{5,1},{257,261},{261,257},{2... | collective-permute-start | bytes 589832 | tf_op jit(solution)/shard_map/ppermute | solution.py:48
  94.7 2.5 %collective-permute-start.3 = (bf16[4,192,128]{2,1,0:T(8,128)(2,1)S(1)}, bf16[4,192,128]{2,1,0:T(8,128)(2,1)S(1)}, u32[]{:S(2)}, u32[]{:S(2)}) collective-permute-start(bf16[4,192,128]{2,1,0:T(8,128)(2,1)S(1)} %get-tuple-element.32), channel_id=1, source_target_pairs={{0,260},{4,256},{256,4},{260,0},{1,261},{5,257},{257,5},{261,1},{2... | collective-permute-start | bytes 589832 | tf_op jit(solution)/shard_map/ppermute | solution.py:48
  97.2 0.0 collective-permute-done.1.a_ref
  97.2 4.4 %collective-permute-done.2.b_ref = bf16[4,192,128]{2,1,0:T(8,128)(2,1)S(1)} collective-permute-done((bf16[4,192,128]{2,1,0:T(8,128)(2,1)S(1)}, bf16[4,192,128]{2,1,0:T(8,128)(2,1)S(1)}, u32[]{:S(2)}, u32[]{:S(2)}) %collective-permute-start.2) | collective-permute-done | bytes 196640 | tf_op jit(solution)/shard_map/ppermute | solution.py:48
  101.7 1.6 %collective-permute-done.3.c_ref = bf16[4,192,128]{2,1,0:T(8,128)(2,1)S(1)} collective-permute-done((bf16[4,192,128]{2,1,0:T(8,128)(2,1)S(1)}, bf16[4,192,128]{2,1,0:T(8,128)(2,1)S(1)}, u32[]{:S(2)}, u32[]{:S(2)}) %collective-permute-start.3) | collective-permute-done | bytes 196640 | tf_op jit(solution)/shard_map/ppermute | solution.py:48
  103.3 0.1 add_x.1
  103.4 4.5 %collective-permute-start.4 = (bf16[192,128]{1,0:T(8,128)(2,1)S(1)}, bf16[192,128]{1,0:T(8,128)(2,1)S(1)}, u32[]{:S(2)}, u32[]{:S(2)}) collective-permute-start(bf16[192,128]{1,0:T(8,128)(2,1)S(1)} %get-tuple-element.34), channel_id=1, source_target_pairs={{0,2},{1,3},{2,0},{3,1},{4,6},{5,7},{6,4},{7,5},{8,10},{9,11},{10,... | collective-permute-start | bytes 147464 | tf_op jit(solution)/shard_map/ppermute | solution.py:52
  107.9 2.8 %collective-permute-start.5 = (bf16[192,128]{1,0:T(8,128)(2,1)S(1)}, bf16[192,128]{1,0:T(8,128)(2,1)S(1)}, u32[]{:S(2)}, u32[]{:S(2)}) collective-permute-start(bf16[192,128]{1,0:T(8,128)(2,1)S(1)} %get-tuple-element.35), channel_id=1, source_target_pairs={{0,3},{1,0},{2,1},{3,2},{4,7},{5,4},{6,5},{7,6},{8,11},{9,8},{10,9... | collective-permute-start | bytes 147464 | tf_op jit(solution)/shard_map/ppermute | solution.py:52
  110.8 2.5 %collective-permute-start.6 = (bf16[192,128]{1,0:T(8,128)(2,1)S(1)}, bf16[192,128]{1,0:T(8,128)(2,1)S(1)}, u32[]{:S(2)}, u32[]{:S(2)}) collective-permute-start(bf16[192,128]{1,0:T(8,128)(2,1)S(1)} %get-tuple-element.36), channel_id=1, source_target_pairs={{0,1},{1,2},{2,3},{3,0},{4,5},{5,6},{6,7},{7,4},{8,9},{9,10},{10,1... | collective-permute-start | bytes 147464 | tf_op jit(solution)/shard_map/ppermute | solution.py:52
  113.2 0.0 collective-permute-done.4.a_ref
  113.3 0.0 collective-permute-done.5.b_ref
  113.3 3.8 %collective-permute-done.6.c_ref = bf16[192,128]{1,0:T(8,128)(2,1)S(1)} collective-permute-done((bf16[192,128]{1,0:T(8,128)(2,1)S(1)}, bf16[192,128]{1,0:T(8,128)(2,1)S(1)}, u32[]{:S(2)}, u32[]{:S(2)}) %collective-permute-start.6) | collective-permute-done | bytes 49184 | tf_op jit(solution)/shard_map/ppermute | solution.py:52
  117.1 0.1 add_y.1.image_ref
  117.2 0.0 all-to-all-done.2.sums_ref
  117.2 0.8 text.1
  118.0 7.1 %all-to-all-start.3 = ((f32[32,1,128]{2,1,0:T(1,128)}), f32[32,1,128]{2,1,0:T(1,128)S(1)}, u32[]{:S(2)}, u32[]{:S(2)}) async-start(f32[32,1,128]{2,1,0:T(1,128)} %get-tuple-element.37), calls=%async_computation.3 | async-start | bytes 32768 | tf_op jit(solution)/shard_map/all_to_all | solution.py:40
  125.1 0.7 copy.9
  125.9 6.1 %all-to-all-done.3 = f32[32,1,128]{2,1,0:T(1,128)S(1)} async-done(((f32[32,1,128]{2,1,0:T(1,128)}), f32[32,1,128]{2,1,0:T(1,128)S(1)}, u32[]{:S(2)}, u32[]{:S(2)}) %all-to-all-start.3) | async-done | bytes 16416 | tf_op jit(solution)/shard_map/all_to_all | solution.py:40
  132.0 0.6 slice_reduce_fusion
Async XLA Ops:
  0.6 1.1 copy-start
  20.4 44.3 %all-to-all-start.1 = ((bf16[32,16,1664]{2,1,0:T(8,128)(2,1)}), bf16[32,16,1664]{2,1,0:T(8,128)(2,1)S(1)}, u32[]{:S(2)}, u32[]{:S(2)}) async-start(bf16[32,16,1664]{2,1,0:T(8,128)(2,1)} %get-tuple-element.21), calls=%async_computation.1 | async-start | bytes 3407872 | tf_op jit(solution)/shard_map/all_to_all | solution.py:40
  64.7 2.8 %copy-start.1 = (bf16[256,1536]{1,0:T(8,128)(2,1)}, bf16[256,1536]{1,0:T(8,128)(2,1)S(1)}, u32[]{:S(2)}) copy-start(bf16[256,1536]{1,0:T(8,128)(2,1)S(1)} %all_gather.3.texts_ref) | copy-start | bytes 2359300
  67.5 7.7 %copy-start.3 = (bf16[512,256]{1,0:T(8,128)(2,1)S(1)}, bf16[512,256]{1,0:T(8,128)(2,1)}, u32[]{:S(2)}) copy-start(bf16[512,256]{1,0:T(8,128)(2,1)} %get-tuple-element.26.weight_ref) | copy-start | bytes 786436
  67.6 49.6 %all-to-all-start.2 = ((bf16[16,16,1664]{2,1,0:T(8,128)(2,1)}), bf16[16,16,1664]{2,1,0:T(8,128)(2,1)S(1)}, u32[]{:S(2)}, u32[]{:S(2)}) async-start(bf16[16,16,1664]{2,1,0:T(8,128)(2,1)} %get-tuple-element.23), calls=%async_computation.2 | async-start | bytes 1703936 | tf_op jit(solution)/shard_map/all_to_all | solution.py:40
  75.2 1.1 copy-start.2
  78.0 9.6 %collective-permute-start = (bf16[16,192,128]{2,1,0:T(8,128)(2,1)S(1)}, bf16[16,192,128]{2,1,0:T(8,128)(2,1)S(1)}, u32[]{:S(2)}, u32[]{:S(2)}) collective-permute-start(bf16[16,192,128]{2,1,0:T(8,128)(2,1)S(1)} %get-tuple-element.28), channel_id=1, source_target_pairs={{0,8},{8,0},{1,9},{9,1},{2,10},{10,2},{3,11},{11,3},{4,12},{12,4},... | collective-permute-start | bytes 2359304 | tf_op jit(solution)/shard_map/ppermute | solution.py:44
  87.7 9.5 %collective-permute-start.1 = (bf16[4,192,128]{2,1,0:T(8,128)(2,1)S(1)}, bf16[4,192,128]{2,1,0:T(8,128)(2,1)S(1)}, u32[]{:S(2)}, u32[]{:S(2)}) collective-permute-start(bf16[4,192,128]{2,1,0:T(8,128)(2,1)S(1)} %get-tuple-element.30), channel_id=1, source_target_pairs={{0,256},{4,260},{256,0},{260,4},{1,257},{5,261},{257,1},{261,5},{2... | collective-permute-start | bytes 589832 | tf_op jit(solution)/shard_map/ppermute | solution.py:48
  92.5 9.1 %collective-permute-start.2 = (bf16[4,192,128]{2,1,0:T(8,128)(2,1)S(1)}, bf16[4,192,128]{2,1,0:T(8,128)(2,1)S(1)}, u32[]{:S(2)}, u32[]{:S(2)}) collective-permute-start(bf16[4,192,128]{2,1,0:T(8,128)(2,1)S(1)} %get-tuple-element.31), channel_id=1, source_target_pairs={{0,4},{4,0},{256,260},{260,256},{1,5},{5,1},{257,261},{261,257},{2... | collective-permute-start | bytes 589832 | tf_op jit(solution)/shard_map/ppermute | solution.py:48
  94.7 8.6 %collective-permute-start.3 = (bf16[4,192,128]{2,1,0:T(8,128)(2,1)S(1)}, bf16[4,192,128]{2,1,0:T(8,128)(2,1)S(1)}, u32[]{:S(2)}, u32[]{:S(2)}) collective-permute-start(bf16[4,192,128]{2,1,0:T(8,128)(2,1)S(1)} %get-tuple-element.32), channel_id=1, source_target_pairs={{0,260},{4,256},{256,4},{260,0},{1,261},{5,257},{257,5},{261,1},{2... | collective-permute-start | bytes 589832 | tf_op jit(solution)/shard_map/ppermute | solution.py:48
  103.4 9.8 %collective-permute-start.4 = (bf16[192,128]{1,0:T(8,128)(2,1)S(1)}, bf16[192,128]{1,0:T(8,128)(2,1)S(1)}, u32[]{:S(2)}, u32[]{:S(2)}) collective-permute-start(bf16[192,128]{1,0:T(8,128)(2,1)S(1)} %get-tuple-element.34), channel_id=1, source_target_pairs={{0,2},{1,3},{2,0},{3,1},{4,6},{5,7},{6,4},{7,5},{8,10},{9,11},{10,... | collective-permute-start | bytes 147464 | tf_op jit(solution)/shard_map/ppermute | solution.py:52
  107.9 5.3 %collective-permute-start.5 = (bf16[192,128]{1,0:T(8,128)(2,1)S(1)}, bf16[192,128]{1,0:T(8,128)(2,1)S(1)}, u32[]{:S(2)}, u32[]{:S(2)}) collective-permute-start(bf16[192,128]{1,0:T(8,128)(2,1)S(1)} %get-tuple-element.35), channel_id=1, source_target_pairs={{0,3},{1,0},{2,1},{3,2},{4,7},{5,4},{6,5},{7,6},{8,11},{9,8},{10,9... | collective-permute-start | bytes 147464 | tf_op jit(solution)/shard_map/ppermute | solution.py:52
  110.8 6.3 %collective-permute-start.6 = (bf16[192,128]{1,0:T(8,128)(2,1)S(1)}, bf16[192,128]{1,0:T(8,128)(2,1)S(1)}, u32[]{:S(2)}, u32[]{:S(2)}) collective-permute-start(bf16[192,128]{1,0:T(8,128)(2,1)S(1)} %get-tuple-element.36), channel_id=1, source_target_pairs={{0,1},{1,2},{2,3},{3,0},{4,5},{5,6},{6,7},{7,4},{8,9},{9,10},{10,1... | collective-permute-start | bytes 147464 | tf_op jit(solution)/shard_map/ppermute | solution.py:52
  118.0 14.0 %all-to-all-start.3 = ((f32[32,1,128]{2,1,0:T(1,128)}), f32[32,1,128]{2,1,0:T(1,128)S(1)}, u32[]{:S(2)}, u32[]{:S(2)}) async-start(f32[32,1,128]{2,1,0:T(1,128)} %get-tuple-element.37), calls=%async_computation.3 | async-start | bytes 32768 | tf_op jit(solution)/shard_map/all_to_all | solution.py:40

commit v7 on v6

--- a/solution.py
+++ b/solution.py
@@ -27,6 +27,7 @@
 TEXTS = N_Z * SHARD
 LANES = 128
 WIDE = WIDTH + LANES
+TEXT_ROWS = WIDTH // LANES * SHARD
 HALF = BLOCK // 2
 PIECE = BLOCK + HALF
 
@@ -134,14 +135,19 @@
     send(weight_ref, weight_hbm)
     tag = loss_tag(jnp.sum(total, axis=1, keepdims=True), SHARD)
     for plane in range(N_Z):
-        sums_ref[plane, :, WIDTH:] = tag
+        sums_ref[plane, TEXT_ROWS:] = tag
     for start in range(0, WIDTH, CHUNK):
         cols = pl.ds(start, CHUNK)
         grad = scale * dot(weight_ref[...], images_ref[:, cols], ((0,), (0,)))
         for plane in range(N_Z):
-            sums_ref[plane, :, cols] = grad[plane * SHARD : (plane + 1) * SHARD].astype(BF)
-        cols = pl.ds(start, CHUNK + (LANES if start + CHUNK == WIDTH else 0))
-        send(sums_ref.at[:, :, cols], out_hbm.at[:, :, cols])
+            for part in range(CHUNK // LANES):
+                piece = grad[plane * SHARD : (plane + 1) * SHARD, part * LANES : (part + 1) * LANES]
+                row = (start // LANES + part) * SHARD
+                sums_ref[plane, row : row + SHARD] = piece.astype(BF)
+        first = start // LANES * SHARD
+        size = CHUNK // LANES * SHARD + (8 if start + CHUNK == WIDTH else 0)
+        some = pl.ds(first, size)
+        send(sums_ref.at[:, some], out_hbm.at[:, some])
     for copy in copies:
         copy.wait()
 
@@ -184,9 +190,12 @@
         out_ref[...] = total.astype(out_ref.dtype)
 
 
-def add_y_body(mine_ref, a_ref, b_ref, c_ref, grad_ref):
-    total = mine_ref[...] + a_ref[...].astype(F32)
-    total = total + (b_ref[...].astype(F32) + c_ref[...].astype(F32))
+def add_two_body(mine_ref, a_ref, b_ref, sum_ref):
+    sum_ref[...] = mine_ref[...] + (a_ref[...].astype(F32) + b_ref[...].astype(F32))
+
+
+def add_last_body(sum_ref, a_ref, grad_ref):
+    total = sum_ref[...] + a_ref[...].astype(F32)
     grad_ref[:, :LANES] = total[:BLOCK]
     grad_ref[:HALF, LANES:] = total[BLOCK:, :HALF]
     grad_ref[HALF:, LANES:] = total[BLOCK:, HALF:]
@@ -196,9 +205,9 @@
     total = sums_ref[0].astype(F32)
     for block in range(1, N_Z):
         total = total + sums_ref[block].astype(F32)
-    tags = total[0:1, WIDTH:]
+    tags = total[TEXT_ROWS : TEXT_ROWS + 1]
     loss_ref[...] = jnp.broadcast_to((tags[:, 0:1] + tags[:, 1:2])[None], loss_ref.shape)
-    grad = total[:, :WIDTH]
+    grad = jnp.concatenate([total[row : row + SHARD] for row in range(0, TEXT_ROWS, SHARD)], axis=1)
     u = u_ref[...]
     inverse = inverse_ref[:, 0:1]
     row_dot = jnp.sum(u * grad, axis=1, keepdims=True)
@@ -238,12 +247,12 @@
     scale, offset = sharpness_factor.reshape(1, 1), offset_vector.reshape(1, 1)
     weight, term = pl.pallas_call(
         pairs_body,
-        out_shape=[pltpu.HBM((IMAGES, TEXTS), BF), pltpu.HBM((N_Z, SHARD, WIDE), BF)],
+        out_shape=[pltpu.HBM((IMAGES, TEXTS), BF), pltpu.HBM((N_Z, TEXT_ROWS + 8, LANES), BF)],
         in_specs=[VMEM] * 4,
         out_specs=[HBM, HBM],
         scratch_shapes=[
             pltpu.VMEM((IMAGES, TEXTS), BF),
-            pltpu.VMEM((N_Z, SHARD, WIDE), BF),
+            pltpu.VMEM((N_Z, TEXT_ROWS + SHARD, LANES), BF),
             pltpu.SemaphoreType.DMA((1 + WIDTH // CHUNK,)),
         ],
         compiler_params=pltpu.CompilerParams(vmem_limit_bytes=24 * 1024 * 1024),
@@ -267,14 +276,17 @@
         (own, along_x(two, 2), along_x(one, 1), along_x(three, 3)),
         [VMEM] * 4, "add_x", moved=1_200_000,
     )
+    last = along_y(two, 2)
+    (total,) = call(
+        add_two_body, [((PIECE, LANES), F32)], (mine, along_y(one, 1), along_y(three, 3)),
+        [VMEM] * 3, "add_two", moved=250_000,
+    )
     (image_grad,) = call(
-        add_y_body, [((BLOCK, COLUMNS), F32)],
-        (mine, along_y(two, 2), along_y(three, 3), along_y(one, 1)),
-        [VMEM] * 4, "add_y", moved=350_000,
+        add_last_body, [((BLOCK, COLUMNS), F32)], (total, last), [VMEM] * 2, "add_last", moved=250_000,
     )
 
     text_grad, loss = call(
-        text_body, [((SHARD, WIDTH), F32), ((N_PLANE, 1, LANES), F32)], (sums, u_txt, inv_txt, image_grad),
+        text_body, [((SHARD, WIDTH), F32), ((N_PLANE, 1, LANES), F32)], (sums, u_txt, inv_txt, total),
         [VMEM] * 3 + [pl.BlockSpec(memory_space=pl.ANY)], "text", moved=1_000_000,
     )
     loss = exchange(loss, PLANE)

time: 135 us -> 134 us (level)
  waiting for transfers between devices: 17.9 us -> 14 us
  starting transfers between devices: 51.2 us -> 53.5 us
    ppermute x3, waiting for transfers between devices: 3.85 us -> 0.01 us  [along_y(): return lax.ppermute(value, 'y', [(i, (i + step) % 4) for i in range(4)])]
    all_to_all x3, starting transfers between devices: 24.1 us -> 26.5 us  [exchange(): return lax.all_to_all(value, axes, 0, 0, tiled=True)]
    pallas_call x5 -> x6, Pallas kernels: 2.77 us -> 2.77 us  [call(): pl.pallas_call(body, out_shape=[jax.ShapeDtypeStruct(shape, dtype) for sh...]
  transfers between devices with their start and end apart: 10 -> 10, of which waited for: 5 -> 4; matrix products, arithmetic and copies ran while one was open for 1% -> 1% of each run, Pallas kernels for 1% -> 2%
where the time goes in v7:
time: 134 us; the launch traced here: 133 us
  starting transfers between devices  53.5 us (40%)
  blocking collectives  48.4 us (36%)
  waiting for transfers between devices  14 us (10%)
  Pallas kernels  7.03 us (5%)
  between operations  3.93 us (3%)
  local copies, waits for them, and re-layouts  2.92 us (2%)
  matrix products  2.42 us (2%)
    all_gather x1, blocking collectives, on_device(): texts = lax.all_gather(unit_txt, ('z',), axis=0, tiled=True)  33.6 us
    all_to_all x3, starting transfers between devices, exchange(): return lax.all_to_all(value, axes, 0, 0, tiled=True)  26.5 us
    all_to_all x1, blocking collectives, exchange(): return lax.all_to_all(value, axes, 0, 0, tiled=True)  14.8 us
    ppermute x3, starting transfers between devices, along_y(): return lax.ppermute(value, 'y', [(i, (i + step) % 4) for i in range(4)])  9.83 us
    ppermute x3, starting transfers between devices, along_x(): return lax.ppermute(value, X, [(i, i ^ flip) for i in range(4)])  9.52 us
    ppermute x1, starting transfers between devices, other_core(): return lax.ppermute(value, 'core', [(0, 1), (1, 0)])  7.69 us
    ppermute x3, waiting for transfers between devices, along_x(): return lax.ppermute(value, X, [(i, i ^ flip) for i in range(4)])  6.07 us
    all_to_all x3, waiting for transfers between devices, exchange(): return lax.all_to_all(value, axes, 0, 0, tiled=True)  6.05 us
  transfers between devices with their start and end apart: 10, of which 4 were waited for; matrix products, arithmetic and copies ran while one was open for 1% of the time, Pallas kernels for 2%

profile of v7, /device:TPU:1, one launch (start us, length us, event | category | flops | bytes accessed | tf_op | source)
XLA Modules:
  0.0 132.9 jit_solution(10147265414120528876)
XLA Ops:
  0.6 0.0 copy-start
  0.6 1.0 copy-done
  1.7 1.1 convolution_convert_fusion
  2.8 1.4 %convolution_convert_fusion.1 = bf16[128,1536]{1,0:T(8,128)(2,1)S(1)} fusion(bf16[128,176]{0,1:T(8,128)(2,1)} %param.6, bf16[176,1536]{1,0:T(8,128)(2,1)} %param.8), kind=kOutput, calls=%fused_computation.1 | convolution fusion | flops 69402624 | bytes 978944 | tf_op jit(solution)/shard_map/dot_general | solution.py:218
  4.1 0.1 pad_maximum_fusion
  4.2 14.8 %all_to_all.20.parts_ref = bf16[8,32,1536]{2,1,0:T(8,128)(2,1)S(1)} all-to-all(bf16[8,32,1536]{2,1,0:T(8,128)(2,1)S(1)} %pad_maximum_fusion), channel_id=1, replica_groups=mesh['xh'=2,'z'=16,'core'=2,'xl'=2,'y'=4] {'xl','y'}, dimensions={0} | all-to-all | bytes 1572864 | tf_op jit(solution)/shard_map/all_to_all | solution.py:41
  18.9 1.4 %normalize.1 = (bf16[32,16,1664]{2,1,0:T(8,128)(2,1)}, bf16[16,1536]{1,0:T(8,128)(2,1)S(1)}, f32[16,1536]{1,0:T(8,128)S(1)}, f32[16,128]{1,0:T(8,128)S(1)}) custom-call(bf16[8,32,1536]{2,1,0:T(8,128)(2,1)S(1)} %all_to_all.20.parts_ref), custom_call_target="tpu_custom_call" | custom-call | bytes 2700000 | tf_op jit(solution)/shard_map/normalize/pallas_call | solution.py:224
  20.4 9.4 %all-to-all-start.1 = ((bf16[32,16,1664]{2,1,0:T(8,128)(2,1)}), bf16[32,16,1664]{2,1,0:T(8,128)(2,1)S(1)}, u32[]{:S(2)}, u32[]{:S(2)}) async-start(bf16[32,16,1664]{2,1,0:T(8,128)(2,1)} %get-tuple-element.21), calls=%async_computation.1 | async-start | bytes 3407872 | tf_op jit(solution)/shard_map/all_to_all | solution.py:41
  31.1 33.6 %all_gather.3.texts_ref = bf16[256,1536]{1,0:T(8,128)(2,1)S(1)} all-gather(bf16[16,1536]{1,0:T(8,128)(2,1)S(1)} %get-tuple-element.22), channel_id=1, replica_groups=mesh['xh'=2,'z'=16,'core'=2,'xl'=2,'y'=4] {'z'}, dimensions={0}, use_global_device_ids=true | all-gather | bytes 835584 | tf_op jit(solution)/shard_map/all_gather | solution.py:245
  64.7 0.0 copy-start.1
  64.7 0.0 all-to-all-done.1
  64.7 2.8 %pairs.1 = (bf16[512,256]{1,0:T(8,128)(2,1)}, bf16[16,200,128]{2,1,0:T(8,128)(2,1)}) custom-call(f32[1,1]{1,0:T(1,128)} %bitcast.10.scale_ref, f32[1,1]{1,0:T(1,128)} %bitcast.12.offset_ref, bf16[512,1664]{1,0:T(8,128)(2,1)S(1)} %bitcast.13, bf16[256,1536]{1,0:T(8,128)(2,1)S(1)} %all_gather.3.texts_ref), custom_call_target="tpu_custom_call" | custom-call | flops 806000000 | bytes 3500000 | tf_op jit(solution)/shard_map/pairs/pallas_call | solution.py:248
  67.5 0.0 copy-start.3
  67.6 0.0 copy-done.1
  67.6 7.6 %all-to-all-start.2 = ((bf16[16,200,128]{2,1,0:T(8,128)(2,1)}), bf16[16,200,128]{2,1,0:T(8,128)(2,1)S(1)}, u32[]{:S(2)}, u32[]{:S(2)}) async-start(bf16[16,200,128]{2,1,0:T(8,128)(2,1)} %get-tuple-element.23), calls=%async_computation.2 | async-start | bytes 1638400 | tf_op jit(solution)/shard_map/all_to_all | solution.py:41
  75.2 0.0 copy-done.3
  75.2 0.0 copy-start.2
  75.2 1.1 copy-done.2
  76.4 1.6 %image_terms.1 = (f32[16,192,128]{2,1,0:T(8,128)S(1)}, bf16[16,192,128]{2,1,0:T(8,128)(2,1)S(1)}) custom-call(f32[1,1]{1,0:T(1,128)} %bitcast.11.scale_ref, bf16[512,1664]{1,0:T(8,128)(2,1)S(1)} %bitcast.14, bf16[256,1536]{1,0:T(8,128)(2,1)S(1)} %copy-done.2, bf16[512,256]{1,0:T(8,128)(2,1)S(1)} %copy-done.3), custom_call_target="tpu_custom_call" | custom-call | flops 403000000 | bytes 4700000 | tf_op jit(solution)/shard_map/image_terms/pallas_call | solution.py:57
  78.0 7.7 %collective-permute-start = (bf16[16,192,128]{2,1,0:T(8,128)(2,1)S(1)}, bf16[16,192,128]{2,1,0:T(8,128)(2,1)S(1)}, u32[]{:S(2)}, u32[]{:S(2)}) collective-permute-start(bf16[16,192,128]{2,1,0:T(8,128)(2,1)S(1)} %get-tuple-element.28), channel_id=1, source_target_pairs={{0,8},{8,0},{1,9},{9,1},{2,10},{10,2},{3,11},{11,3},{4,12},{12,4},... | collective-permute-start | bytes 2359304 | tf_op jit(solution)/shard_map/ppermute | solution.py:45
  85.7 1.9 %collective-permute-done.other_ref = bf16[16,192,128]{2,1,0:T(8,128)(2,1)S(1)} collective-permute-done((bf16[16,192,128]{2,1,0:T(8,128)(2,1)S(1)}, bf16[16,192,128]{2,1,0:T(8,128)(2,1)S(1)}, u32[]{:S(2)}, u32[]{:S(2)}) %collective-permute-start) | collective-permute-done | bytes 786464 | tf_op jit(solution)/shard_map/ppermute | solution.py:45
  87.6 0.1 add_core.1
  87.7 4.8 %collective-permute-start.1 = (bf16[4,192,128]{2,1,0:T(8,128)(2,1)S(1)}, bf16[4,192,128]{2,1,0:T(8,128)(2,1)S(1)}, u32[]{:S(2)}, u32[]{:S(2)}) collective-permute-start(bf16[4,192,128]{2,1,0:T(8,128)(2,1)S(1)} %get-tuple-element.30), channel_id=1, source_target_pairs={{0,256},{4,260},{256,0},{260,4},{1,257},{5,261},{257,1},{261,5},{2... | collective-permute-start | bytes 589832 | tf_op jit(solution)/shard_map/ppermute | solution.py:49
  92.5 2.2 %collective-permute-start.2 = (bf16[4,192,128]{2,1,0:T(8,128)(2,1)S(1)}, bf16[4,192,128]{2,1,0:T(8,128)(2,1)S(1)}, u32[]{:S(2)}, u32[]{:S(2)}) collective-permute-start(bf16[4,192,128]{2,1,0:T(8,128)(2,1)S(1)} %get-tuple-element.31), channel_id=1, source_target_pairs={{0,4},{4,0},{256,260},{260,256},{1,5},{5,1},{257,261},{261,257},{2... | collective-permute-start | bytes 589832 | tf_op jit(solution)/shard_map/ppermute | solution.py:49
  94.7 2.5 %collective-permute-start.3 = (bf16[4,192,128]{2,1,0:T(8,128)(2,1)S(1)}, bf16[4,192,128]{2,1,0:T(8,128)(2,1)S(1)}, u32[]{:S(2)}, u32[]{:S(2)}) collective-permute-start(bf16[4,192,128]{2,1,0:T(8,128)(2,1)S(1)} %get-tuple-element.32), channel_id=1, source_target_pairs={{0,260},{4,256},{256,4},{260,0},{1,261},{5,257},{257,5},{261,1},{2... | collective-permute-start | bytes 589832 | tf_op jit(solution)/shard_map/ppermute | solution.py:49
  97.2 0.0 collective-permute-done.1.a_ref
  97.3 4.4 %collective-permute-done.2.b_ref = bf16[4,192,128]{2,1,0:T(8,128)(2,1)S(1)} collective-permute-done((bf16[4,192,128]{2,1,0:T(8,128)(2,1)S(1)}, bf16[4,192,128]{2,1,0:T(8,128)(2,1)S(1)}, u32[]{:S(2)}, u32[]{:S(2)}) %collective-permute-start.2) | collective-permute-done | bytes 196640 | tf_op jit(solution)/shard_map/ppermute | solution.py:49
  101.7 1.6 %collective-permute-done.3.c_ref = bf16[4,192,128]{2,1,0:T(8,128)(2,1)S(1)} collective-permute-done((bf16[4,192,128]{2,1,0:T(8,128)(2,1)S(1)}, bf16[4,192,128]{2,1,0:T(8,128)(2,1)S(1)}, u32[]{:S(2)}, u32[]{:S(2)}) %collective-permute-start.3) | collective-permute-done | bytes 196640 | tf_op jit(solution)/shard_map/ppermute | solution.py:49
  103.3 0.1 add_x.1
  103.4 3.1 %collective-permute-start.4 = (bf16[192,128]{1,0:T(8,128)(2,1)S(1)}, bf16[192,128]{1,0:T(8,128)(2,1)S(1)}, u32[]{:S(2)}, u32[]{:S(2)}) collective-permute-start(bf16[192,128]{1,0:T(8,128)(2,1)S(1)} %get-tuple-element.34), channel_id=1, source_target_pairs={{0,1},{1,2},{2,3},{3,0},{4,5},{5,6},{6,7},{7,4},{8,9},{9,10},{10,1... | collective-permute-start | bytes 147464 | tf_op jit(solution)/shard_map/ppermute | solution.py:53
  106.5 3.4 %collective-permute-start.5 = (bf16[192,128]{1,0:T(8,128)(2,1)S(1)}, bf16[192,128]{1,0:T(8,128)(2,1)S(1)}, u32[]{:S(2)}, u32[]{:S(2)}) collective-permute-start(bf16[192,128]{1,0:T(8,128)(2,1)S(1)} %get-tuple-element.35), channel_id=1, source_target_pairs={{0,3},{1,0},{2,1},{3,2},{4,7},{5,4},{6,5},{7,6},{8,11},{9,8},{10,9... | collective-permute-start | bytes 147464 | tf_op jit(solution)/shard_map/ppermute | solution.py:53
  109.9 3.3 %collective-permute-start.6 = (bf16[192,128]{1,0:T(8,128)(2,1)S(1)}, bf16[192,128]{1,0:T(8,128)(2,1)S(1)}, u32[]{:S(2)}, u32[]{:S(2)}) collective-permute-start(bf16[192,128]{1,0:T(8,128)(2,1)S(1)} %get-tuple-element.37), channel_id=1, source_target_pairs={{0,2},{1,3},{2,0},{3,1},{4,6},{5,7},{6,4},{7,5},{8,10},{9,11},{10,... | collective-permute-start | bytes 147464 | tf_op jit(solution)/shard_map/ppermute | solution.py:53
  113.3 0.0 collective-permute-done.4.a_ref
  113.3 0.0 collective-permute-done.5.b_ref
  113.3 0.0 all-to-all-done.2.sums_ref
  113.3 0.8 text.1
  114.2 9.4 %all-to-all-start.3 = ((f32[32,1,128]{2,1,0:T(1,128)}), f32[32,1,128]{2,1,0:T(1,128)S(1)}, u32[]{:S(2)}, u32[]{:S(2)}) async-start(f32[32,1,128]{2,1,0:T(1,128)} %get-tuple-element.36), calls=%async_computation.3 | async-start | bytes 32768 | tf_op jit(solution)/shard_map/all_to_all | solution.py:41
  123.6 0.0 collective-permute-done.6.a_ref
  123.6 0.1 add_last.1
  123.7 0.7 copy.9
  124.4 6.0 %all-to-all-done.3 = f32[32,1,128]{2,1,0:T(1,128)S(1)} async-done(((f32[32,1,128]{2,1,0:T(1,128)}), f32[32,1,128]{2,1,0:T(1,128)S(1)}, u32[]{:S(2)}, u32[]{:S(2)}) %all-to-all-start.3) | async-done | bytes 16416 | tf_op jit(solution)/shard_map/all_to_all | solution.py:41
  130.5 0.6 slice_reduce_fusion
  (1 shorter events, 0.0 us)
Async XLA Ops:
  0.6 1.1 copy-start
  20.4 44.3 %all-to-all-start.1 = ((bf16[32,16,1664]{2,1,0:T(8,128)(2,1)}), bf16[32,16,1664]{2,1,0:T(8,128)(2,1)S(1)}, u32[]{:S(2)}, u32[]{:S(2)}) async-start(bf16[32,16,1664]{2,1,0:T(8,128)(2,1)} %get-tuple-element.21), calls=%async_computation.1 | async-start | bytes 3407872 | tf_op jit(solution)/shard_map/all_to_all | solution.py:41
  64.7 2.8 %copy-start.1 = (bf16[256,1536]{1,0:T(8,128)(2,1)}, bf16[256,1536]{1,0:T(8,128)(2,1)S(1)}, u32[]{:S(2)}) copy-start(bf16[256,1536]{1,0:T(8,128)(2,1)S(1)} %all_gather.3.texts_ref) | copy-start | bytes 2359300
  67.5 7.7 %copy-start.3 = (bf16[512,256]{1,0:T(8,128)(2,1)S(1)}, bf16[512,256]{1,0:T(8,128)(2,1)}, u32[]{:S(2)}) copy-start(bf16[512,256]{1,0:T(8,128)(2,1)} %get-tuple-element.26.weight_ref) | copy-start | bytes 786436
  67.6 45.7 %all-to-all-start.2 = ((bf16[16,200,128]{2,1,0:T(8,128)(2,1)}), bf16[16,200,128]{2,1,0:T(8,128)(2,1)S(1)}, u32[]{:S(2)}, u32[]{:S(2)}) async-start(bf16[16,200,128]{2,1,0:T(8,128)(2,1)} %get-tuple-element.23), calls=%async_computation.2 | async-start | bytes 1638400 | tf_op jit(solution)/shard_map/all_to_all | solution.py:41
  75.2 1.1 copy-start.2
  78.0 9.6 %collective-permute-start = (bf16[16,192,128]{2,1,0:T(8,128)(2,1)S(1)}, bf16[16,192,128]{2,1,0:T(8,128)(2,1)S(1)}, u32[]{:S(2)}, u32[]{:S(2)}) collective-permute-start(bf16[16,192,128]{2,1,0:T(8,128)(2,1)S(1)} %get-tuple-element.28), channel_id=1, source_target_pairs={{0,8},{8,0},{1,9},{9,1},{2,10},{10,2},{3,11},{11,3},{4,12},{12,4},... | collective-permute-start | bytes 2359304 | tf_op jit(solution)/shard_map/ppermute | solution.py:45
  87.7 9.5 %collective-permute-start.1 = (bf16[4,192,128]{2,1,0:T(8,128)(2,1)S(1)}, bf16[4,192,128]{2,1,0:T(8,128)(2,1)S(1)}, u32[]{:S(2)}, u32[]{:S(2)}) collective-permute-start(bf16[4,192,128]{2,1,0:T(8,128)(2,1)S(1)} %get-tuple-element.30), channel_id=1, source_target_pairs={{0,256},{4,260},{256,0},{260,4},{1,257},{5,261},{257,1},{261,5},{2... | collective-permute-start | bytes 589832 | tf_op jit(solution)/shard_map/ppermute | solution.py:49
  92.5 9.1 %collective-permute-start.2 = (bf16[4,192,128]{2,1,0:T(8,128)(2,1)S(1)}, bf16[4,192,128]{2,1,0:T(8,128)(2,1)S(1)}, u32[]{:S(2)}, u32[]{:S(2)}) collective-permute-start(bf16[4,192,128]{2,1,0:T(8,128)(2,1)S(1)} %get-tuple-element.31), channel_id=1, source_target_pairs={{0,4},{4,0},{256,260},{260,256},{1,5},{5,1},{257,261},{261,257},{2... | collective-permute-start | bytes 589832 | tf_op jit(solution)/shard_map/ppermute | solution.py:49
  94.7 8.6 %collective-permute-start.3 = (bf16[4,192,128]{2,1,0:T(8,128)(2,1)S(1)}, bf16[4,192,128]{2,1,0:T(8,128)(2,1)S(1)}, u32[]{:S(2)}, u32[]{:S(2)}) collective-permute-start(bf16[4,192,128]{2,1,0:T(8,128)(2,1)S(1)} %get-tuple-element.32), channel_id=1, source_target_pairs={{0,260},{4,256},{256,4},{260,0},{1,261},{5,257},{257,5},{261,1},{2... | collective-permute-start | bytes 589832 | tf_op jit(solution)/shard_map/ppermute | solution.py:49
  103.4 9.9 %collective-permute-start.4 = (bf16[192,128]{1,0:T(8,128)(2,1)S(1)}, bf16[192,128]{1,0:T(8,128)(2,1)S(1)}, u32[]{:S(2)}, u32[]{:S(2)}) collective-permute-start(bf16[192,128]{1,0:T(8,128)(2,1)S(1)} %get-tuple-element.34), channel_id=1, source_target_pairs={{0,1},{1,2},{2,3},{3,0},{4,5},{5,6},{6,7},{7,4},{8,9},{9,10},{10,1... | collective-permute-start | bytes 147464 | tf_op jit(solution)/shard_map/ppermute | solution.py:53
  106.5 6.8 %collective-permute-start.5 = (bf16[192,128]{1,0:T(8,128)(2,1)S(1)}, bf16[192,128]{1,0:T(8,128)(2,1)S(1)}, u32[]{:S(2)}, u32[]{:S(2)}) collective-permute-start(bf16[192,128]{1,0:T(8,128)(2,1)S(1)} %get-tuple-element.35), channel_id=1, source_target_pairs={{0,3},{1,0},{2,1},{3,2},{4,7},{5,4},{6,5},{7,6},{8,11},{9,8},{10,9... | collective-permute-start | bytes 147464 | tf_op jit(solution)/shard_map/ppermute | solution.py:53
  109.9 13.7 %collective-permute-start.6 = (bf16[192,128]{1,0:T(8,128)(2,1)S(1)}, bf16[192,128]{1,0:T(8,128)(2,1)S(1)}, u32[]{:S(2)}, u32[]{:S(2)}) collective-permute-start(bf16[192,128]{1,0:T(8,128)(2,1)S(1)} %get-tuple-element.37), channel_id=1, source_target_pairs={{0,2},{1,3},{2,0},{3,1},{4,6},{5,7},{6,4},{7,5},{8,10},{9,11},{10,... | collective-permute-start | bytes 147464 | tf_op jit(solution)/shard_map/ppermute | solution.py:53
  114.2 16.3 %all-to-all-start.3 = ((f32[32,1,128]{2,1,0:T(1,128)}), f32[32,1,128]{2,1,0:T(1,128)S(1)}, u32[]{:S(2)}, u32[]{:S(2)}) async-start(f32[32,1,128]{2,1,0:T(1,128)} %get-tuple-element.36), calls=%async_computation.3 | async-start | bytes 32768 | tf_op jit(solution)/shard_map/all_to_all | solution.py:41

commit v8 on v7

--- a/solution.py
+++ b/solution.py
@@ -27,7 +27,6 @@
 TEXTS = N_Z * SHARD
 LANES = 128
 WIDE = WIDTH + LANES
-TEXT_ROWS = WIDTH // LANES * SHARD
 HALF = BLOCK // 2
 PIECE = BLOCK + HALF
 
@@ -69,13 +68,16 @@
     return lax.dot_general(a, b, (contract, ((), ())), preferred_element_type=F32)
 
 
-def terms(similarity, scale, offset, labels):
+def weigh(similarity, scale, offset, labels):
     value = -labels * (scale * similarity + offset)
     small = jnp.exp(-jnp.abs(value))
-    loss = jnp.maximum(value, 0.0) + jnp.log1p(small)
     share = 1.0 / (1.0 + small)
     sigmoid = jnp.where(value >= 0.0, share, small * share)
-    return loss, (-labels * sigmoid).astype(BF)
+    return value, (-labels * sigmoid).astype(BF)
+
+
+def softplus(value):
+    return jnp.maximum(value, 0.0) + jnp.log1p(jnp.exp(-jnp.abs(value)))
 
 
 def loss_tag(total, rows):
@@ -113,7 +115,9 @@
         copy.wait()
 
 
-def pairs_body(scale_ref, offset_ref, images_ref, texts_ref, weight_hbm, out_hbm, weight_ref, sums_ref, sems):
+def pairs_body(
+    scale_ref, offset_ref, images_ref, texts_ref, weight_hbm, out_hbm, weight_ref, value_ref, sums_ref, sems
+):
     scale, offset = scale_ref[...], offset_ref[...]
     at_plane, at_z = lax.axis_index(PLANE), lax.axis_index("z")
     copies = []
@@ -122,32 +126,30 @@
         copies.append(pltpu.make_async_copy(source, target, sems.at[len(copies)]))
         copies[-1].start()
 
-    total = jnp.zeros((1, TEXTS), F32)
     for block in range(IMAGES // BLOCK):
         rows = pl.ds(block * BLOCK, BLOCK)
         similarity = dot(images_ref[rows, :WIDTH], texts_ref[...], ((1,), (1,)))
         image = lax.broadcasted_iota(jnp.int32, similarity.shape, 0) + block * BLOCK
         text = lax.broadcasted_iota(jnp.int32, similarity.shape, 1)
         same = (image // SHARD == at_plane) & (image - SHARD * at_plane == text - SHARD * at_z)
-        loss, weight = terms(similarity, scale, offset, jnp.where(same, 1.0, -1.0))
-        total = total + jnp.sum(loss, axis=0, keepdims=True)
+        value, weight = weigh(similarity, scale, offset, jnp.where(same, 1.0, -1.0))
+        value_ref[rows, :] = value
         weight_ref[rows, :] = weight
-    send(weight_ref, weight_hbm)
-    tag = loss_tag(jnp.sum(total, axis=1, keepdims=True), SHARD)
-    for plane in range(N_Z):
-        sums_ref[plane, TEXT_ROWS:] = tag
     for start in range(0, WIDTH, CHUNK):
         cols = pl.ds(start, CHUNK)
         grad = scale * dot(weight_ref[...], images_ref[:, cols], ((0,), (0,)))
         for plane in range(N_Z):
-            for part in range(CHUNK // LANES):
-                piece = grad[plane * SHARD : (plane + 1) * SHARD, part * LANES : (part + 1) * LANES]
-                row = (start // LANES + part) * SHARD
-                sums_ref[plane, row : row + SHARD] = piece.astype(BF)
-        first = start // LANES * SHARD
-        size = CHUNK // LANES * SHARD + (8 if start + CHUNK == WIDTH else 0)
-        some = pl.ds(first, size)
-        send(sums_ref.at[:, some], out_hbm.at[:, some])
+            sums_ref[plane, :, cols] = grad[plane * SHARD : (plane + 1) * SHARD].astype(BF)
+        send(sums_ref.at[:, :, cols], out_hbm.at[:, :, cols])
+    send(weight_ref, weight_hbm)
+    total = jnp.zeros((1, TEXTS), F32)
+    for block in range(IMAGES // BLOCK):
+        rows = pl.ds(block * BLOCK, BLOCK)
+        total = total + jnp.sum(softplus(value_ref[rows, :]), axis=0, keepdims=True)
+    tag = loss_tag(jnp.sum(total, axis=1, keepdims=True), SHARD)
+    for plane in range(N_Z):
+        sums_ref[plane, :, WIDTH:] = tag
+    send(sums_ref.at[:, :, WIDTH:], out_hbm.at[:, :, WIDTH:])
     for copy in copies:
         copy.wait()
 
@@ -205,9 +207,9 @@
     total = sums_ref[0].astype(F32)
     for block in range(1, N_Z):
         total = total + sums_ref[block].astype(F32)
-    tags = total[TEXT_ROWS : TEXT_ROWS + 1]
+    tags = total[0:1, WIDTH:]
     loss_ref[...] = jnp.broadcast_to((tags[:, 0:1] + tags[:, 1:2])[None], loss_ref.shape)
-    grad = jnp.concatenate([total[row : row + SHARD] for row in range(0, TEXT_ROWS, SHARD)], axis=1)
+    grad = total[:, :WIDTH]
     u = u_ref[...]
     inverse = inverse_ref[:, 0:1]
     row_dot = jnp.sum(u * grad, axis=1, keepdims=True)
@@ -247,13 +249,14 @@
     scale, offset = sharpness_factor.reshape(1, 1), offset_vector.reshape(1, 1)
     weight, term = pl.pallas_call(
         pairs_body,
-        out_shape=[pltpu.HBM((IMAGES, TEXTS), BF), pltpu.HBM((N_Z, TEXT_ROWS + 8, LANES), BF)],
+        out_shape=[pltpu.HBM((IMAGES, TEXTS), BF), pltpu.HBM((N_Z, SHARD, WIDE), BF)],
         in_specs=[VMEM] * 4,
         out_specs=[HBM, HBM],
         scratch_shapes=[
             pltpu.VMEM((IMAGES, TEXTS), BF),
-            pltpu.VMEM((N_Z, TEXT_ROWS + SHARD, LANES), BF),
-            pltpu.SemaphoreType.DMA((1 + WIDTH // CHUNK,)),
+            pltpu.VMEM((IMAGES, TEXTS), F32),
+            pltpu.VMEM((N_Z, SHARD, WIDE), BF),
+            pltpu.SemaphoreType.DMA((2 + WIDTH // CHUNK,)),
         ],
         compiler_params=pltpu.CompilerParams(vmem_limit_bytes=24 * 1024 * 1024),
         cost_estimate=pl.CostEstimate(flops=806_000_000, bytes_accessed=3_500_000, transcendentals=0),

time: 134 us -> 135 us (level)
  starting transfers between devices: 53.5 us -> 55.1 us
    all_to_all x3, starting transfers between devices: 26.5 us -> 28 us  [exchange(): return lax.all_to_all(value, axes, 0, 0, tiled=True)]
where the time goes in v8:
time: 135 us
  starting transfers between devices  55.1 us (41%)
  blocking collectives  48.4 us (36%)
  waiting for transfers between devices  14 us (10%)
  Pallas kernels  7.12 us (5%)
  between operations  3.93 us (3%)
  local copies, waits for them, and re-layouts  2.92 us (2%)
  matrix products  2.42 us (2%)
    all_gather x1, blocking collectives, on_device(): texts = lax.all_gather(unit_txt, ('z',), axis=0, tiled=True)  33.6 us
    all_to_all x3, starting transfers between devices, exchange(): return lax.all_to_all(value, axes, 0, 0, tiled=True)  28 us
    all_to_all x1, blocking collectives, exchange(): return lax.all_to_all(value, axes, 0, 0, tiled=True)  14.8 us
    ppermute x3, starting transfers between devices, along_y(): return lax.ppermute(value, 'y', [(i, (i + step) % 4) for i in range(4)])  9.82 us
    ppermute x3, starting transfers between devices, along_x(): return lax.ppermute(value, X, [(i, i ^ flip) for i in range(4)])  9.52 us
    ppermute x1, starting transfers between devices, other_core(): return lax.ppermute(value, 'core', [(0, 1), (1, 0)])  7.69 us
    ppermute x3, waiting for transfers between devices, along_x(): return lax.ppermute(value, X, [(i, i ^ flip) for i in range(4)])  6.07 us
    all_to_all x3, waiting for transfers between devices, exchange(): return lax.all_to_all(value, axes, 0, 0, tiled=True)  6.05 us
  transfers between devices with their start and end apart: 10, of which 4 were waited for; matrix products, arithmetic and copies ran while one was open for 1% of the time, Pallas kernels for 2%

profile of v8, /device:TPU:1, one launch (start us, length us, event | category | flops | bytes accessed | tf_op | source)
XLA Modules:
  0.0 134.5 jit_solution(8079768151844113693)
XLA Ops:
  0.6 0.0 copy-start
  0.6 1.0 copy-done
  1.7 1.1 convolution_convert_fusion
  2.8 1.4 %convolution_convert_fusion.1 = bf16[128,1536]{1,0:T(8,128)(2,1)S(1)} fusion(bf16[128,176]{0,1:T(8,128)(2,1)} %param.6, bf16[176,1536]{1,0:T(8,128)(2,1)} %param.8), kind=kOutput, calls=%fused_computation.1 | convolution fusion | flops 69402624 | bytes 978944 | tf_op jit(solution)/shard_map/dot_general | solution.py:220
  4.1 0.1 pad_maximum_fusion
  4.2 14.8 %all_to_all.20.parts_ref = bf16[8,32,1536]{2,1,0:T(8,128)(2,1)S(1)} all-to-all(bf16[8,32,1536]{2,1,0:T(8,128)(2,1)S(1)} %pad_maximum_fusion), channel_id=1, replica_groups=mesh['xh'=2,'z'=16,'core'=2,'xl'=2,'y'=4] {'xl','y'}, dimensions={0} | all-to-all | bytes 1572864 | tf_op jit(solution)/shard_map/all_to_all | solution.py:40
  18.9 1.4 %normalize.1 = (bf16[32,16,1664]{2,1,0:T(8,128)(2,1)}, bf16[16,1536]{1,0:T(8,128)(2,1)S(1)}, f32[16,1536]{1,0:T(8,128)S(1)}, f32[16,128]{1,0:T(8,128)S(1)}) custom-call(bf16[8,32,1536]{2,1,0:T(8,128)(2,1)S(1)} %all_to_all.20.parts_ref), custom_call_target="tpu_custom_call" | custom-call | bytes 2700000 | tf_op jit(solution)/shard_map/normalize/pallas_call | solution.py:226
  20.4 9.4 %all-to-all-start.1 = ((bf16[32,16,1664]{2,1,0:T(8,128)(2,1)}), bf16[32,16,1664]{2,1,0:T(8,128)(2,1)S(1)}, u32[]{:S(2)}, u32[]{:S(2)}) async-start(bf16[32,16,1664]{2,1,0:T(8,128)(2,1)} %get-tuple-element.21), calls=%async_computation.1 | async-start | bytes 3407872 | tf_op jit(solution)/shard_map/all_to_all | solution.py:40
  31.1 33.6 %all_gather.3.texts_ref = bf16[256,1536]{1,0:T(8,128)(2,1)S(1)} all-gather(bf16[16,1536]{1,0:T(8,128)(2,1)S(1)} %get-tuple-element.22), channel_id=1, replica_groups=mesh['xh'=2,'z'=16,'core'=2,'xl'=2,'y'=4] {'z'}, dimensions={0}, use_global_device_ids=true | all-gather | bytes 835584 | tf_op jit(solution)/shard_map/all_gather | solution.py:247
  64.7 0.0 copy-start.1
  64.7 0.0 all-to-all-done.1
  64.7 2.9 %pairs.1 = (bf16[512,256]{1,0:T(8,128)(2,1)}, bf16[16,16,1664]{2,1,0:T(8,128)(2,1)}) custom-call(f32[1,1]{1,0:T(1,128)} %bitcast.10.scale_ref, f32[1,1]{1,0:T(1,128)} %bitcast.12.offset_ref, bf16[512,1664]{1,0:T(8,128)(2,1)S(1)} %bitcast.13, bf16[256,1536]{1,0:T(8,128)(2,1)S(1)} %all_gather.3.texts_ref), custom_call_target="tpu_custom_call" | custom-call | flops 806000000 | bytes 3500000 | tf_op jit(solution)/shard_map/pairs/pallas_call | solution.py:250
  67.6 0.0 copy-start.3
  67.7 0.0 copy-done.1
  67.7 7.6 %all-to-all-start.2 = ((bf16[16,16,1664]{2,1,0:T(8,128)(2,1)}), bf16[16,16,1664]{2,1,0:T(8,128)(2,1)S(1)}, u32[]{:S(2)}, u32[]{:S(2)}) async-start(bf16[16,16,1664]{2,1,0:T(8,128)(2,1)} %get-tuple-element.23), calls=%async_computation.2 | async-start | bytes 1703936 | tf_op jit(solution)/shard_map/all_to_all | solution.py:40
  75.3 0.0 copy-done.3
  75.3 0.0 copy-start.2
  75.3 1.1 copy-done.2
  76.5 1.6 %image_terms.1 = (f32[16,192,128]{2,1,0:T(8,128)S(1)}, bf16[16,192,128]{2,1,0:T(8,128)(2,1)S(1)}) custom-call(f32[1,1]{1,0:T(1,128)} %bitcast.11.scale_ref, bf16[512,1664]{1,0:T(8,128)(2,1)S(1)} %bitcast.14, bf16[256,1536]{1,0:T(8,128)(2,1)S(1)} %copy-done.2, bf16[512,256]{1,0:T(8,128)(2,1)S(1)} %copy-done.3), custom_call_target="tpu_custom_call" | custom-call | flops 403000000 | bytes 4700000 | tf_op jit(solution)/shard_map/image_terms/pallas_call | solution.py:56
  78.1 7.7 %collective-permute-start = (bf16[16,192,128]{2,1,0:T(8,128)(2,1)S(1)}, bf16[16,192,128]{2,1,0:T(8,128)(2,1)S(1)}, u32[]{:S(2)}, u32[]{:S(2)}) collective-permute-start(bf16[16,192,128]{2,1,0:T(8,128)(2,1)S(1)} %get-tuple-element.28), channel_id=1, source_target_pairs={{0,8},{8,0},{1,9},{9,1},{2,10},{10,2},{3,11},{11,3},{4,12},{12,4},... | collective-permute-start | bytes 2359304 | tf_op jit(solution)/shard_map/ppermute | solution.py:44
  85.8 1.9 %collective-permute-done.other_ref = bf16[16,192,128]{2,1,0:T(8,128)(2,1)S(1)} collective-permute-done((bf16[16,192,128]{2,1,0:T(8,128)(2,1)S(1)}, bf16[16,192,128]{2,1,0:T(8,128)(2,1)S(1)}, u32[]{:S(2)}, u32[]{:S(2)}) %collective-permute-start) | collective-permute-done | bytes 786464 | tf_op jit(solution)/shard_map/ppermute | solution.py:44
  87.7 0.1 add_core.1
  87.8 4.8 %collective-permute-start.1 = (bf16[4,192,128]{2,1,0:T(8,128)(2,1)S(1)}, bf16[4,192,128]{2,1,0:T(8,128)(2,1)S(1)}, u32[]{:S(2)}, u32[]{:S(2)}) collective-permute-start(bf16[4,192,128]{2,1,0:T(8,128)(2,1)S(1)} %get-tuple-element.30), channel_id=1, source_target_pairs={{0,256},{4,260},{256,0},{260,4},{1,257},{5,261},{257,1},{261,5},{2... | collective-permute-start | bytes 589832 | tf_op jit(solution)/shard_map/ppermute | solution.py:48
  92.6 2.2 %collective-permute-start.2 = (bf16[4,192,128]{2,1,0:T(8,128)(2,1)S(1)}, bf16[4,192,128]{2,1,0:T(8,128)(2,1)S(1)}, u32[]{:S(2)}, u32[]{:S(2)}) collective-permute-start(bf16[4,192,128]{2,1,0:T(8,128)(2,1)S(1)} %get-tuple-element.31), channel_id=1, source_target_pairs={{0,4},{4,0},{256,260},{260,256},{1,5},{5,1},{257,261},{261,257},{2... | collective-permute-start | bytes 589832 | tf_op jit(solution)/shard_map/ppermute | solution.py:48
  94.8 2.5 %collective-permute-start.3 = (bf16[4,192,128]{2,1,0:T(8,128)(2,1)S(1)}, bf16[4,192,128]{2,1,0:T(8,128)(2,1)S(1)}, u32[]{:S(2)}, u32[]{:S(2)}) collective-permute-start(bf16[4,192,128]{2,1,0:T(8,128)(2,1)S(1)} %get-tuple-element.32), channel_id=1, source_target_pairs={{0,260},{4,256},{256,4},{260,0},{1,261},{5,257},{257,5},{261,1},{2... | collective-permute-start | bytes 589832 | tf_op jit(solution)/shard_map/ppermute | solution.py:48
  97.3 0.0 collective-permute-done.1.a_ref
  97.4 4.4 %collective-permute-done.2.b_ref = bf16[4,192,128]{2,1,0:T(8,128)(2,1)S(1)} collective-permute-done((bf16[4,192,128]{2,1,0:T(8,128)(2,1)S(1)}, bf16[4,192,128]{2,1,0:T(8,128)(2,1)S(1)}, u32[]{:S(2)}, u32[]{:S(2)}) %collective-permute-start.2) | collective-permute-done | bytes 196640 | tf_op jit(solution)/shard_map/ppermute | solution.py:48
  101.8 1.6 %collective-permute-done.3.c_ref = bf16[4,192,128]{2,1,0:T(8,128)(2,1)S(1)} collective-permute-done((bf16[4,192,128]{2,1,0:T(8,128)(2,1)S(1)}, bf16[4,192,128]{2,1,0:T(8,128)(2,1)S(1)}, u32[]{:S(2)}, u32[]{:S(2)}) %collective-permute-start.3) | collective-permute-done | bytes 196640 | tf_op jit(solution)/shard_map/ppermute | solution.py:48
  103.4 0.1 add_x.1
  103.5 3.1 %collective-permute-start.4 = (bf16[192,128]{1,0:T(8,128)(2,1)S(1)}, bf16[192,128]{1,0:T(8,128)(2,1)S(1)}, u32[]{:S(2)}, u32[]{:S(2)}) collective-permute-start(bf16[192,128]{1,0:T(8,128)(2,1)S(1)} %get-tuple-element.34), channel_id=1, source_target_pairs={{0,1},{1,2},{2,3},{3,0},{4,5},{5,6},{6,7},{7,4},{8,9},{9,10},{10,1... | collective-permute-start | bytes 147464 | tf_op jit(solution)/shard_map/ppermute | solution.py:52
  106.6 3.4 %collective-permute-start.5 = (bf16[192,128]{1,0:T(8,128)(2,1)S(1)}, bf16[192,128]{1,0:T(8,128)(2,1)S(1)}, u32[]{:S(2)}, u32[]{:S(2)}) collective-permute-start(bf16[192,128]{1,0:T(8,128)(2,1)S(1)} %get-tuple-element.35), channel_id=1, source_target_pairs={{0,3},{1,0},{2,1},{3,2},{4,7},{5,4},{6,5},{7,6},{8,11},{9,8},{10,9... | collective-permute-start | bytes 147464 | tf_op jit(solution)/shard_map/ppermute | solution.py:52
  110.0 3.3 %collective-permute-start.6 = (bf16[192,128]{1,0:T(8,128)(2,1)S(1)}, bf16[192,128]{1,0:T(8,128)(2,1)S(1)}, u32[]{:S(2)}, u32[]{:S(2)}) collective-permute-start(bf16[192,128]{1,0:T(8,128)(2,1)S(1)} %get-tuple-element.37), channel_id=1, source_target_pairs={{0,2},{1,3},{2,0},{3,1},{4,6},{5,7},{6,4},{7,5},{8,10},{9,11},{10,... | collective-permute-start | bytes 147464 | tf_op jit(solution)/shard_map/ppermute | solution.py:52
  113.4 0.0 collective-permute-done.4.a_ref
  113.4 0.0 collective-permute-done.5.b_ref
  113.4 0.0 all-to-all-done.2.sums_ref
  113.4 0.8 text.1
  114.3 11.0 %all-to-all-start.3 = ((f32[32,1,128]{2,1,0:T(1,128)}), f32[32,1,128]{2,1,0:T(1,128)S(1)}, u32[]{:S(2)}, u32[]{:S(2)}) async-start(f32[32,1,128]{2,1,0:T(1,128)} %get-tuple-element.36), calls=%async_computation.3 | async-start | bytes 32768 | tf_op jit(solution)/shard_map/all_to_all | solution.py:40
  125.2 0.0 collective-permute-done.6.a_ref
  125.3 0.1 add_last.1
  125.3 0.7 copy.9
  126.1 6.0 %all-to-all-done.3 = f32[32,1,128]{2,1,0:T(1,128)S(1)} async-done(((f32[32,1,128]{2,1,0:T(1,128)}), f32[32,1,128]{2,1,0:T(1,128)S(1)}, u32[]{:S(2)}, u32[]{:S(2)}) %all-to-all-start.3) | async-done | bytes 16416 | tf_op jit(solution)/shard_map/all_to_all | solution.py:40
  132.1 0.6 slice_reduce_fusion
  (1 shorter events, 0.0 us)
Async XLA Ops:
  0.6 1.1 copy-start
  20.4 44.3 %all-to-all-start.1 = ((bf16[32,16,1664]{2,1,0:T(8,128)(2,1)}), bf16[32,16,1664]{2,1,0:T(8,128)(2,1)S(1)}, u32[]{:S(2)}, u32[]{:S(2)}) async-start(bf16[32,16,1664]{2,1,0:T(8,128)(2,1)} %get-tuple-element.21), calls=%async_computation.1 | async-start | bytes 3407872 | tf_op jit(solution)/shard_map/all_to_all | solution.py:40
  64.7 2.9 %copy-start.1 = (bf16[256,1536]{1,0:T(8,128)(2,1)}, bf16[256,1536]{1,0:T(8,128)(2,1)S(1)}, u32[]{:S(2)}) copy-start(bf16[256,1536]{1,0:T(8,128)(2,1)S(1)} %all_gather.3.texts_ref) | copy-start | bytes 2359300
  67.6 7.7 %copy-start.3 = (bf16[512,256]{1,0:T(8,128)(2,1)S(1)}, bf16[512,256]{1,0:T(8,128)(2,1)}, u32[]{:S(2)}) copy-start(bf16[512,256]{1,0:T(8,128)(2,1)} %get-tuple-element.26.weight_ref) | copy-start | bytes 786436
  67.7 45.7 %all-to-all-start.2 = ((bf16[16,16,1664]{2,1,0:T(8,128)(2,1)}), bf16[16,16,1664]{2,1,0:T(8,128)(2,1)S(1)}, u32[]{:S(2)}, u32[]{:S(2)}) async-start(bf16[16,16,1664]{2,1,0:T(8,128)(2,1)} %get-tuple-element.23), calls=%async_computation.2 | async-start | bytes 1703936 | tf_op jit(solution)/shard_map/all_to_all | solution.py:40
  75.3 1.1 copy-start.2
  78.1 9.6 %collective-permute-start = (bf16[16,192,128]{2,1,0:T(8,128)(2,1)S(1)}, bf16[16,192,128]{2,1,0:T(8,128)(2,1)S(1)}, u32[]{:S(2)}, u32[]{:S(2)}) collective-permute-start(bf16[16,192,128]{2,1,0:T(8,128)(2,1)S(1)} %get-tuple-element.28), channel_id=1, source_target_pairs={{0,8},{8,0},{1,9},{9,1},{2,10},{10,2},{3,11},{11,3},{4,12},{12,4},... | collective-permute-start | bytes 2359304 | tf_op jit(solution)/shard_map/ppermute | solution.py:44
  87.8 9.5 %collective-permute-start.1 = (bf16[4,192,128]{2,1,0:T(8,128)(2,1)S(1)}, bf16[4,192,128]{2,1,0:T(8,128)(2,1)S(1)}, u32[]{:S(2)}, u32[]{:S(2)}) collective-permute-start(bf16[4,192,128]{2,1,0:T(8,128)(2,1)S(1)} %get-tuple-element.30), channel_id=1, source_target_pairs={{0,256},{4,260},{256,0},{260,4},{1,257},{5,261},{257,1},{261,5},{2... | collective-permute-start | bytes 589832 | tf_op jit(solution)/shard_map/ppermute | solution.py:48
  92.6 9.1 %collective-permute-start.2 = (bf16[4,192,128]{2,1,0:T(8,128)(2,1)S(1)}, bf16[4,192,128]{2,1,0:T(8,128)(2,1)S(1)}, u32[]{:S(2)}, u32[]{:S(2)}) collective-permute-start(bf16[4,192,128]{2,1,0:T(8,128)(2,1)S(1)} %get-tuple-element.31), channel_id=1, source_target_pairs={{0,4},{4,0},{256,260},{260,256},{1,5},{5,1},{257,261},{261,257},{2... | collective-permute-start | bytes 589832 | tf_op jit(solution)/shard_map/ppermute | solution.py:48
  94.8 8.6 %collective-permute-start.3 = (bf16[4,192,128]{2,1,0:T(8,128)(2,1)S(1)}, bf16[4,192,128]{2,1,0:T(8,128)(2,1)S(1)}, u32[]{:S(2)}, u32[]{:S(2)}) collective-permute-start(bf16[4,192,128]{2,1,0:T(8,128)(2,1)S(1)} %get-tuple-element.32), channel_id=1, source_target_pairs={{0,260},{4,256},{256,4},{260,0},{1,261},{5,257},{257,5},{261,1},{2... | collective-permute-start | bytes 589832 | tf_op jit(solution)/shard_map/ppermute | solution.py:48
  103.5 9.8 %collective-permute-start.4 = (bf16[192,128]{1,0:T(8,128)(2,1)S(1)}, bf16[192,128]{1,0:T(8,128)(2,1)S(1)}, u32[]{:S(2)}, u32[]{:S(2)}) collective-permute-start(bf16[192,128]{1,0:T(8,128)(2,1)S(1)} %get-tuple-element.34), channel_id=1, source_target_pairs={{0,1},{1,2},{2,3},{3,0},{4,5},{5,6},{6,7},{7,4},{8,9},{9,10},{10,1... | collective-permute-start | bytes 147464 | tf_op jit(solution)/shard_map/ppermute | solution.py:52
  106.6 6.8 %collective-permute-start.5 = (bf16[192,128]{1,0:T(8,128)(2,1)S(1)}, bf16[192,128]{1,0:T(8,128)(2,1)S(1)}, u32[]{:S(2)}, u32[]{:S(2)}) collective-permute-start(bf16[192,128]{1,0:T(8,128)(2,1)S(1)} %get-tuple-element.35), channel_id=1, source_target_pairs={{0,3},{1,0},{2,1},{3,2},{4,7},{5,4},{6,5},{7,6},{8,11},{9,8},{10,9... | collective-permute-start | bytes 147464 | tf_op jit(solution)/shard_map/ppermute | solution.py:52
  110.0 15.2 %collective-permute-start.6 = (bf16[192,128]{1,0:T(8,128)(2,1)S(1)}, bf16[192,128]{1,0:T(8,128)(2,1)S(1)}, u32[]{:S(2)}, u32[]{:S(2)}) collective-permute-start(bf16[192,128]{1,0:T(8,128)(2,1)S(1)} %get-tuple-element.37), channel_id=1, source_target_pairs={{0,2},{1,3},{2,0},{3,1},{4,6},{5,7},{6,4},{7,5},{8,10},{9,11},{10,... | collective-permute-start | bytes 147464 | tf_op jit(solution)/shard_map/ppermute | solution.py:52
  114.3 17.9 %all-to-all-start.3 = ((f32[32,1,128]{2,1,0:T(1,128)}), f32[32,1,128]{2,1,0:T(1,128)S(1)}, u32[]{:S(2)}, u32[]{:S(2)}) async-start(f32[32,1,128]{2,1,0:T(1,128)} %get-tuple-element.36), calls=%async_computation.3 | async-start | bytes 32768 | tf_op jit(solution)/shard_map/all_to_all | solution.py:40
